TPU v7x, 512 devices: a whole 4x8x8 slice. The times are simulated.
512 devices in a mesh: tm: 128 (over z, y, core), plane: 4 (over x).
Axes of the slice: x: 4, y: 8, z: 8, core: 2. Of those that a mesh axis runs over, the one named last changes fastest.
Arguments:
- source: float32 [128, 16, 256, 256], P('tm', 'plane'), may hold values from -6 to 6
- potential: float32 [16, 256, 256], P('plane'), may hold values from 0.1 to 10
- level_shift: float32 [4], replicated, may hold values from 0.5 to 16
Outputs:
- result: float32 [128, 16, 256, 256], P('tm', 'plane')
All inputs are finite; a program needn't handle non-finite values.
Results may differ from a plain program's by a relative error of at most 0.00002.
Values sent between devices are 32-bit elements; how exact they have to be, the bound alone decides.
A program may use at most 192 MiB of HBM per device.

v0:
```python
import math

import jax
import jax.numpy as jnp
from jax import lax
from jax.sharding import PartitionSpec as P

CB = 8


OMEGA = 0.8
INV_ROOT = 1.0 / math.sqrt(2.0)


def from_partner(value, axis, stride):
    return lax.ppermute(value, axis, [(i, i ^ 1 << stride) for i in range(lax.axis_size(axis))])


def extended_2(block, sides, width):
    for axis, dim in sides:
        count = lax.axis_size(axis)
        forward = [(i, i + 1) for i in range(count - 1)]
        backward = [(target, source) for source, target in forward]
        low = lax.ppermute(
            lax.slice_in_dim(block, block.shape[dim] - width, None, axis=dim), axis, forward
        )
        high = lax.ppermute(lax.slice_in_dim(block, 0, width, axis=dim), axis, backward)
        block = jnp.concatenate([low, block, high], axis=dim)
    return block


def neighbours(extended):
    inner = extended[1:-1]
    padded = jnp.pad(inner, ((0, 0), (1, 1), (1, 1)))
    total = extended[2:] + extended[:-2]
    total = total + padded[:, 2:, 1:-1] + padded[:, :-2, 1:-1]
    return total + padded[:, 1:-1, 2:] + padded[:, 1:-1, :-2]


def block_sum(field):
    planes, rows, cols = field.shape
    return field.reshape(planes, rows // CB, CB, cols // CB, CB).sum(axis=(0, 2, 4))


def coarse_fix(coarse_rem, coarse_pot, shift_now, planes_all):
    coarse_diag = (
        coarse_pot + shift_now * (CB * CB * planes_all) + 2.0 * CB * CB + 4.0 * CB * planes_all
    )
    coarse_one = coarse_rem / coarse_diag
    padded = jnp.pad(coarse_one, 1)
    beside_all = padded[2:, 1:-1] + padded[:-2, 1:-1] + padded[1:-1, 2:] + padded[1:-1, :-2]
    applied = coarse_diag * coarse_one - CB * planes_all * beside_all
    return coarse_one + (coarse_rem - applied) / coarse_diag


def prolong(coarse):
    rows, cols = coarse.shape
    return jnp.broadcast_to(coarse[:, None, :, None], (rows, CB, cols, CB)).reshape(
        rows * CB, cols * CB
    )


def level_of(position):
    return (
        (position % 2 == 0).astype(jnp.int32)
        + (position % 4 == 0).astype(jnp.int32)
        + (position % 8 == 0).astype(jnp.int32)
    )


def time_lift(block, levels):
    position = lax.axis_index("tm")
    for level in levels:
        partner = from_partner(block, "tm", level)
        upper_bit = (position >> level) % 2
        active = position % (1 << level) == 0
        mixed = jnp.where(
            upper_bit == 0, (block + partner) * INV_ROOT, (partner - block) * INV_ROOT
        )
        block = jnp.where(active, mixed, block)
    return block


def with_rim(field):
    return extended_2(field, (("plane", 0),), 1)


def shards(source, potential, level_shift):
    position = lax.axis_index("tm")
    level_id = level_of(position)
    shift_now = jnp.sum(jnp.where(jnp.arange(4) == level_id, level_shift, 0.0))
    waves = time_lift(source, (0, 1, 2))
    wave_src = waves[0]
    planes = wave_src.shape[0]
    diagonal = 6.0 + potential + shift_now
    first_pass = OMEGA * wave_src / diagonal
    second_pass = (
        first_pass
        + OMEGA * (wave_src - (diagonal * first_pass - neighbours(with_rim(first_pass)))) / diagonal
    )
    remainder = wave_src - (diagonal * second_pass - neighbours(with_rim(second_pass)))
    coarse_rem, coarse_pot = lax.psum((block_sum(remainder), block_sum(potential)), "plane")
    correction = coarse_fix(coarse_rem, coarse_pot, shift_now, planes * lax.axis_size("plane"))
    fixed = (second_pass + prolong(correction)[None])[None]
    return time_lift(fixed, (2, 1, 0))


def solution(mesh):
    in_specs = (P("tm", "plane", None, None), P("plane", None, None), P())
    out_specs = P("tm", "plane", None, None)
    return jax.shard_map(shards, mesh=mesh, in_specs=in_specs, out_specs=out_specs, check_vma=False)
```

profile of v0, /device:TPU:1, one launch (start us, length us, event | category | flops | bytes accessed | tf_op | source)
XLA Modules:
  0.0 231.6 jit_solution(14724060041243785986)
XLA Ops:
  0.0 0.0 copy-start.3
  0.0 0.0 copy-start
  0.0 8.9 %collective-permute-start = (f32[1,4,256,256]{3,2,1,0:T(8,128)}, f32[1,4,256,256]{3,2,1,0:T(8,128)S(1)}, u32[]{:S(2)}, u32[]{:S(2)}) collective-permute-start(f32[1,4,256,256]{3,2,1,0:T(8,128)} %param.3), channel_id=1, source_target_pairs={{0,4},{4,0},{8,12},{12,8},{16,20},{20,16},{24,28},{28,24},{32,36},... | collective-permute-start | bytes 3145736 | tf_op jit(solution)/shard_map/ppermute | solution.py:16
  8.9 2.5 %collective-permute-done = f32[1,4,256,256]{3,2,1,0:T(8,128)S(1)} collective-permute-done((f32[1,4,256,256]{3,2,1,0:T(8,128)}, f32[1,4,256,256]{3,2,1,0:T(8,128)S(1)}, u32[]{:S(2)}, u32[]{:S(2)}) %collective-permute-start) | collective-permute-done | bytes 1048608 | tf_op jit(solution)/shard_map/ppermute | solution.py:16
  11.4 1.4 multiply_select_fusion.1
  12.8 1.9 collective-permute-start.1
  14.7 24.4 %collective-permute-done.1 = f32[1,4,256,256]{3,2,1,0:T(8,128)} collective-permute-done((f32[1,4,256,256]{3,2,1,0:T(8,128)S(1)}, f32[1,4,256,256]{3,2,1,0:T(8,128)}, u32[]{:S(2)}, u32[]{:S(2)}) %collective-permute-start.1) | collective-permute-done | bytes 1048608 | tf_op jit(solution)/shard_map/ppermute | solution.py:16
  39.2 1.4 select_select_fusion.3
  40.6 0.0 copy-start.1
  40.6 1.9 collective-permute-start.2
  42.6 0.0 copy-done.3
  42.6 0.7 fusion.28
  43.3 0.0 copy-done.1
  43.3 47.6 %collective-permute-done.2 = f32[1,4,256,256]{3,2,1,0:T(8,128)S(1)} collective-permute-done((f32[1,4,256,256]{3,2,1,0:T(8,128)S(1)}, f32[1,4,256,256]{3,2,1,0:T(8,128)S(1)}, u32[]{:S(2)}, u32[]{:S(2)}) %collective-permute-start.2) | collective-permute-done | bytes 1048608 | tf_op jit(solution)/shard_map/ppermute | solution.py:16
  90.9 0.0 copy-done
  90.9 2.2 fusion.18
  93.2 1.3 collective-permute-start.3
  94.5 4.0 %collective-permute-start.4 = (f32[1,256,256]{2,1,0:T(8,128)S(1)}, f32[1,256,256]{2,1,0:T(8,128)S(1)}, u32[]{:S(2)}, u32[]{:S(2)}) collective-permute-start(f32[1,256,256]{2,1,0:T(8,128)S(1)} %get-tuple-element.14), channel_id=1, source_target_pairs={{0,1},{1,2},{2,3},{4,5},{5,6},{6,7},{8,9},{9,10},{10,11},{12,13},{... | collective-permute-start | bytes 786440 | tf_op jit(solution)/shard_map/ppermute | solution.py:24
  98.5 3.9 %collective-permute-done.3 = f32[1,256,256]{2,1,0:T(8,128)S(1)} collective-permute-done((f32[1,256,256]{2,1,0:T(8,128)S(1)}, f32[1,256,256]{2,1,0:T(8,128)S(1)}, u32[]{:S(2)}, u32[]{:S(2)}) %collective-permute-start.3) | collective-permute-done | bytes 262176 | tf_op jit(solution)/shard_map/ppermute | solution.py:27
  102.4 0.9 collective-permute-done.4
  103.3 1.4 fusion.8
  104.7 0.8 fusion.30
  105.5 1.3 collective-permute-start.5
  106.8 5.4 %collective-permute-start.6 = (f32[1,256,256]{2,1,0:T(8,128)}, f32[1,256,256]{2,1,0:T(8,128)}, u32[]{:S(2)}, u32[]{:S(2)}) collective-permute-start(f32[1,256,256]{2,1,0:T(8,128)} %get-tuple-element.12), channel_id=1, source_target_pairs={{0,1},{1,2},{2,3},{4,5},{5,6},{6,7},{8,9},{9,10},{10,11},{12,13},{... | collective-permute-start | bytes 786440 | tf_op jit(solution)/shard_map/ppermute | solution.py:24
  112.9 1.8 collective-permute-done.5
  114.7 0.0 copy-start.2
  114.7 0.7 copy-done.2
  115.4 0.3 collective-permute-done.6
  115.7 3.1 %fusion.29 = (f32[256,256]{1,0:T(8,128)}, f32[256,256]{1,0:T(8,128)S(1)}) fusion(f32[4,256,256]{2,1,0:T(8,128)S(1)} %copy-done, f32[4,256,256]{2,1,0:T(8,128)S(1)} %fusion.8, f32[1,256,256]{2,1,0:T(8,128)} %collective-permute-done.6, f32[1,256,256]{2,1,0:T(8,128)} %copy-done.2, f32[]{:T(128)} %fusion.28, f32[1,4,256,256]{3,2,1,0:T(8,128)S(1)} %get-tuple-element.10), kind=kLoop, calls=%fused_computation.56 | loop fusion | flops 3538944 | bytes 4194308 | tf_op jit(solution)/shard_map/reduce_sum | solution.py:42
  118.8 4.5 %reduce_sum.46 = f32[32,8,32,8]{3,2,1,0:T(8,128)} reshape(f32[256,256]{1,0:T(8,128)} %get-tuple-element.5) | data formatting | bytes 524288 | tf_op jit(solution)/shard_map/reduce_sum | solution.py:42
  123.3 3.6 %reduce_sum.36 = f32[32,8,32,8]{3,2,1,0:T(8,128)} reshape(f32[256,256]{1,0:T(8,128)S(1)} %get-tuple-element.6) | data formatting | bytes 524288 | tf_op jit(solution)/shard_map/reduce_sum | solution.py:42
  126.9 2.6 %reduce_sum.47 = f32[32,32]{1,0:T(8,128)S(1)} reduce(f32[32,8,32,8]{3,2,1,0:T(8,128)} %reduce_sum.46, f32[]{:T(128)} %constant.90.clone.1), dimensions={1,3}, to_apply=%region_5.6 | reduce | flops 64512 | bytes 266244 | tf_op jit(solution)/shard_map/reduce_sum | solution.py:42
  129.5 2.6 %reduce_sum.44 = f32[32,32]{1,0:T(8,128)S(1)} reduce(f32[32,8,32,8]{3,2,1,0:T(8,128)} %reduce_sum.36, f32[]{:T(128)} %constant.90.clone.1), dimensions={1,3}, to_apply=%region_2.3 | reduce | flops 64512 | bytes 266244 | tf_op jit(solution)/shard_map/reduce_sum | solution.py:42
  132.0 14.0 %all-reduce.3 = (f32[32,32]{1,0:T(8,128)S(1)}, f32[32,32]{1,0:T(8,128)S(1)}) all-reduce(f32[32,32]{1,0:T(8,128)S(1)} %reduce_sum.44, f32[32,32]{1,0:T(8,128)S(1)} %reduce_sum.47), channel_id=1, replica_groups=mesh['tm'=128,'plane'=4] {'plane'}, use_global_device_ids=true, to_apply=%region_3.4 | all-reduce | flops 2048 | bytes 16384 | tf_op jit(solution)/shard_map/psum | solution.py:102
  146.1 0.1 fusion.26
  146.2 2.5 %broadcast_in_dim.14 = f32[32,8,32,8]{3,2,1,0:T(8,128)} broadcast(f32[32,32]{1,0:T(8,128)S(1)} %fusion.26), dimensions={0,2} | broadcast | bytes 266240 | tf_op jit(solution)/shard_map/broadcast_in_dim | solution.py:58
  148.7 4.0 %add.178 = f32[256,256]{1,0:T(8,128)S(1)} reshape(f32[32,8,32,8]{3,2,1,0:T(8,128)} %broadcast_in_dim.14) | data formatting | bytes 524288 | tf_op jit(solution)/shard_map/add | solution.py:104
  152.7 0.1 add_bitcast_fusion
  152.8 1.9 collective-permute-start.7
  154.8 43.5 %collective-permute-done.7 = f32[1,4,256,256]{3,2,1,0:T(8,128)S(1)} collective-permute-done((f32[1,4,256,256]{3,2,1,0:T(8,128)S(1)}, f32[1,4,256,256]{3,2,1,0:T(8,128)S(1)}, u32[]{:S(2)}, u32[]{:S(2)}) %collective-permute-start.7) | collective-permute-done | bytes 1048608 | tf_op jit(solution)/shard_map/ppermute | solution.py:16
  198.3 0.2 select_select_fusion.1
  198.6 1.9 collective-permute-start.8
  200.5 24.2 %collective-permute-done.8 = f32[1,4,256,256]{3,2,1,0:T(8,128)S(1)} collective-permute-done((f32[1,4,256,256]{3,2,1,0:T(8,128)S(1)}, f32[1,4,256,256]{3,2,1,0:T(8,128)S(1)}, u32[]{:S(2)}, u32[]{:S(2)}) %collective-permute-start.8) | collective-permute-done | bytes 1048608 | tf_op jit(solution)/shard_map/ppermute | solution.py:16
  224.7 0.2 select_select_fusion
  224.9 3.2 %collective-permute-start.9 = (f32[1,4,256,256]{3,2,1,0:T(8,128)S(1)}, f32[1,4,256,256]{3,2,1,0:T(8,128)S(1)}, u32[]{:S(2)}, u32[]{:S(2)}) collective-permute-start(f32[1,4,256,256]{3,2,1,0:T(8,128)S(1)} %select_select_fusion), channel_id=1, source_target_pairs={{0,4},{4,0},{8,12},{12,8},{16,20},{20,16},{24,28},{28,24},{32,36},... | collective-permute-start | bytes 3145736 | tf_op jit(solution)/shard_map/ppermute | solution.py:16
  228.1 2.3 collective-permute-done.9
  230.4 1.1 multiply_select_fusion
  (2 shorter events, 0.1 us)
Async XLA Ops:
  0.0 42.6 %copy-start.3 = (f32[4]{0:T(128)S(1)}, f32[4]{0:T(128)}, u32[]{:S(2)}) copy-start(f32[4]{0:T(128)} %param.5) | copy-start | bytes 52
  0.0 90.9 %copy-start = (f32[4,256,256]{2,1,0:T(8,128)S(1)}, f32[4,256,256]{2,1,0:T(8,128)}, u32[]{:S(2)}) copy-start(f32[4,256,256]{2,1,0:T(8,128)} %param.4) | copy-start | bytes 3145732
  0.0 11.4 %collective-permute-start = (f32[1,4,256,256]{3,2,1,0:T(8,128)}, f32[1,4,256,256]{3,2,1,0:T(8,128)S(1)}, u32[]{:S(2)}, u32[]{:S(2)}) collective-permute-start(f32[1,4,256,256]{3,2,1,0:T(8,128)} %param.3), channel_id=1, source_target_pairs={{0,4},{4,0},{8,12},{12,8},{16,20},{20,16},{24,28},{28,24},{32,36},... | collective-permute-start | bytes 3145736 | tf_op jit(solution)/shard_map/ppermute | solution.py:16
  12.8 26.4 %collective-permute-start.1 = (f32[1,4,256,256]{3,2,1,0:T(8,128)S(1)}, f32[1,4,256,256]{3,2,1,0:T(8,128)}, u32[]{:S(2)}, u32[]{:S(2)}) collective-permute-start(f32[1,4,256,256]{3,2,1,0:T(8,128)S(1)} %multiply_select_fusion.1), channel_id=1, source_target_pairs={{0,8},{4,12},{8,0},{12,4},{16,24},{20,28},{24,16},{28,20},{32,40},... | collective-permute-start | bytes 3145736 | tf_op jit(solution)/shard_map/ppermute | solution.py:16
  40.6 2.7 %copy-start.1 = (f32[1,4,256,256]{3,2,1,0:T(8,128)}, f32[1,4,256,256]{3,2,1,0:T(8,128)S(1)}, u32[]{:S(2)}) copy-start(f32[1,4,256,256]{3,2,1,0:T(8,128)S(1)} %select_select_fusion.3) | copy-start | bytes 3145732
  40.6 50.3 %collective-permute-start.2 = (f32[1,4,256,256]{3,2,1,0:T(8,128)S(1)}, f32[1,4,256,256]{3,2,1,0:T(8,128)S(1)}, u32[]{:S(2)}, u32[]{:S(2)}) collective-permute-start(f32[1,4,256,256]{3,2,1,0:T(8,128)S(1)} %select_select_fusion.3), channel_id=1, source_target_pairs={{0,16},{4,20},{8,24},{12,28},{16,0},{20,4},{24,8},{28,12},{32,48},... | collective-permute-start | bytes 3145736 | tf_op jit(solution)/shard_map/ppermute | solution.py:16
  93.2 9.2 %collective-permute-start.3 = (f32[1,256,256]{2,1,0:T(8,128)S(1)}, f32[1,256,256]{2,1,0:T(8,128)S(1)}, u32[]{:S(2)}, u32[]{:S(2)}) collective-permute-start(f32[1,256,256]{2,1,0:T(8,128)S(1)} %get-tuple-element.13), channel_id=1, source_target_pairs={{1,0},{2,1},{3,2},{5,4},{6,5},{7,6},{9,8},{10,9},{11,10},{13,12},{... | collective-permute-start | bytes 786440 | tf_op jit(solution)/shard_map/ppermute | solution.py:27
  94.5 8.8 %collective-permute-start.4 = (f32[1,256,256]{2,1,0:T(8,128)S(1)}, f32[1,256,256]{2,1,0:T(8,128)S(1)}, u32[]{:S(2)}, u32[]{:S(2)}) collective-permute-start(f32[1,256,256]{2,1,0:T(8,128)S(1)} %get-tuple-element.14), channel_id=1, source_target_pairs={{0,1},{1,2},{2,3},{4,5},{5,6},{6,7},{8,9},{9,10},{10,11},{12,13},{... | collective-permute-start | bytes 786440 | tf_op jit(solution)/shard_map/ppermute | solution.py:24
  105.5 9.2 %collective-permute-start.5 = (f32[1,256,256]{2,1,0:T(8,128)}, f32[1,256,256]{2,1,0:T(8,128)S(1)}, u32[]{:S(2)}, u32[]{:S(2)}) collective-permute-start(f32[1,256,256]{2,1,0:T(8,128)} %get-tuple-element.11), channel_id=1, source_target_pairs={{1,0},{2,1},{3,2},{5,4},{6,5},{7,6},{9,8},{10,9},{11,10},{13,12},{... | collective-permute-start | bytes 786440 | tf_op jit(solution)/shard_map/ppermute | solution.py:27
  106.8 8.9 %collective-permute-start.6 = (f32[1,256,256]{2,1,0:T(8,128)}, f32[1,256,256]{2,1,0:T(8,128)}, u32[]{:S(2)}, u32[]{:S(2)}) collective-permute-start(f32[1,256,256]{2,1,0:T(8,128)} %get-tuple-element.12), channel_id=1, source_target_pairs={{0,1},{1,2},{2,3},{4,5},{5,6},{6,7},{8,9},{9,10},{10,11},{12,13},{... | collective-permute-start | bytes 786440 | tf_op jit(solution)/shard_map/ppermute | solution.py:24
  114.7 0.7 copy-start.2
  152.8 45.5 %collective-permute-start.7 = (f32[1,4,256,256]{3,2,1,0:T(8,128)S(1)}, f32[1,4,256,256]{3,2,1,0:T(8,128)S(1)}, u32[]{:S(2)}, u32[]{:S(2)}) collective-permute-start(f32[1,4,256,256]{3,2,1,0:T(8,128)S(1)} %add_bitcast_fusion), channel_id=1, source_target_pairs={{0,16},{4,20},{8,24},{12,28},{16,0},{20,4},{24,8},{28,12},{32,48},... | collective-permute-start | bytes 3145736 | tf_op jit(solution)/shard_map/ppermute | solution.py:16
  198.6 26.1 %collective-permute-start.8 = (f32[1,4,256,256]{3,2,1,0:T(8,128)S(1)}, f32[1,4,256,256]{3,2,1,0:T(8,128)S(1)}, u32[]{:S(2)}, u32[]{:S(2)}) collective-permute-start(f32[1,4,256,256]{3,2,1,0:T(8,128)S(1)} %select_select_fusion.1), channel_id=1, source_target_pairs={{0,8},{4,12},{8,0},{12,4},{16,24},{20,28},{24,16},{28,20},{32,40},... | collective-permute-start | bytes 3145736 | tf_op jit(solution)/shard_map/ppermute | solution.py:16
  224.9 5.5 %collective-permute-start.9 = (f32[1,4,256,256]{3,2,1,0:T(8,128)S(1)}, f32[1,4,256,256]{3,2,1,0:T(8,128)S(1)}, u32[]{:S(2)}, u32[]{:S(2)}) collective-permute-start(f32[1,4,256,256]{3,2,1,0:T(8,128)S(1)} %select_select_fusion), channel_id=1, source_target_pairs={{0,4},{4,0},{8,12},{12,8},{16,20},{20,16},{24,28},{28,24},{32,36},... | collective-permute-start | bytes 3145736 | tf_op jit(solution)/shard_map/ppermute | solution.py:16
where the time goes:
time: 232 us
  waiting for transfers between devices  151 us (65%)
  starting transfers between devices  31.8 us (14%)
  other arithmetic  17.1 us (7%)
  local copies, waits for them, and re-layouts  16.3 us (7%)
  blocking collectives  14 us (6%)
    ppermute x6, waiting for transfers between devices, from_partner(): lax.ppermute(value, axis, [(i, i ^ 1 << stride) for i in range(lax.axis_s...  145 us
    ppermute x6, starting transfers between devices, from_partner(): lax.ppermute(value, axis, [(i, i ^ 1 << stride) for i in range(lax.axis_s...  19.8 us
    psum x1, blocking collectives, shards(): lax.psum((block_sum(remainder), block_sum(potential)), 'plane')  14 us
    ppermute x2, starting transfers between devices, extended_2(): lax.ppermute(lax.slice_in_dim(block, block.shape[dim] - width, None, axis...  9.43 us
    reduce_sum x3, other arithmetic, block_sum(): field.reshape(planes, rows // CB, CB, cols // CB, CB).sum(axis=(0, 2, 4))  8.19 us
    reduce_sum x2, local copies, waits for them, and re-layouts, block_sum(): field.reshape(planes, rows // CB, CB, cols // CB, CB).sum(axis=(0, 2, 4))  8.13 us
    ppermute x2, waiting for transfers between devices, extended_2(): lax.ppermute(lax.slice_in_dim(block, 0, width, axis=dim), axis, backward)  5.75 us
  transfers between devices with their start and end apart: 10, of which 10 were waited for; matrix products, arithmetic and copies ran while one was open for 0% of the time, Pallas kernels for 0%

commit v1 on v0

v1 whole, which is shorter than its diff:
```python
import math

import jax
import jax.numpy as jnp
from jax import lax
from jax.experimental import pallas as pl
from jax.experimental.pallas import tpu as pltpu
from jax.sharding import PartitionSpec as P

F32 = jnp.float32
MESH = pl.DeviceIdType.MESH
ROOT = 1.0 / math.sqrt(2.0)
OMEGA = 0.8
PLANES = (0, 3, 1, 2)
SLOT = {plane: slot for slot, plane in enumerate(PLANES)}
LEVELS = (3, 1, 2, 1)


def dot(a, b):
    return jnp.dot(a, b, precision=lax.Precision.HIGHEST, preferred_element_type=F32)


def iota(shape, dim):
    return lax.broadcasted_iota(jnp.int32, shape, dim)


def ones_where(mask):
    return jnp.where(mask, 1.0, 0.0).astype(F32)


def beside_yz(ext):
    rows = ext.shape[0] - 16
    mid = ext[8 : 8 + rows]
    up = pltpu.roll(ext, 1, 0)[8 : 8 + rows]
    down = pltpu.roll(ext, rows + 15, 0)[8 : 8 + rows]
    col = iota(mid.shape, 1)
    left = jnp.where(col == 0, 0.0, pltpu.roll(mid, 1, 1))
    right = jnp.where(col == 255, 0.0, pltpu.roll(mid, 255, 1))
    return mid, (up + down) + (left + right)


def kernel(
    shift_ref, source, potential, out,
    own, other, pot, s_buf, fd, sd, strip, rs, rstrip, fs, r_s, r_strip, hd, hs, sb, bk,
    t_d, x_d, t_s, x_s, pot_all, coarse, coarse_x, total, tr, dr, xs, xd, mine, yours,
    l_sem, p_sem, s0, r0, sy, ry, st, rt, sxd, rxd, sxs, rxs, sp, rp, sc, rc, sg, rg, sdp, rdp, sbk, rbk, so, ro, lo,
):
    t, x = lax.axis_index("tm"), lax.axis_index("plane")
    e = t % 8
    base = t - e
    k, c = e % 2, e // 2
    partner = t + 1 - 2 * k
    chips = [(c + m) % 4 for m in (1, 2, 3)]
    x_peers = [(x + m) % 4 for m in (1, 2, 3)]
    group = [base + (e + m) % 8 for m in range(1, 8)]

    barrier = pltpu.get_barrier_semaphore()
    for peer in group:
        pl.semaphore_signal(barrier, inc=1, device_id=(peer, x), device_id_type=MESH)
    for peer in x_peers:
        pl.semaphore_signal(barrier, inc=1, device_id=(t, peer), device_id_type=MESH)

    rows_from = pl.multiple_of(120 * k, 8)
    rows_to = pl.multiple_of(8 - 8 * k, 8)
    loads = []
    for slot, plane in enumerate(PLANES):
        load = pltpu.make_async_copy(
            source.at[0, plane, pl.ds(rows_from, 136), :],
            own.at[slot, pl.ds(rows_to, 136), :],
            l_sem.at[slot],
        )
        load.start()
        loads.append(load)
    pot_loads = []
    for slot, plane in enumerate(PLANES):
        load = pltpu.make_async_copy(
            potential.at[plane, pl.ds(rows_from, 136), :],
            pot.at[slot, pl.ds(rows_to, 136), :],
            p_sem.at[slot],
        )
        load.start()
        pot_loads.append(load)
    blank = pl.multiple_of(136 * k, 8)
    for slot in range(4):
        own[slot, pl.ds(blank, 8), :] = jnp.zeros((8, 256), F32)
        other[slot, pl.ds(blank, 8), :] = jnp.zeros((8, 256), F32)
        pot[slot, pl.ds(blank, 8), :] = jnp.zeros((8, 256), F32)

    pl.semaphore_wait(barrier, 10)

    def remote(src, dst, send, recv, where):
        return pltpu.make_async_remote_copy(
            src_ref=src, dst_ref=dst, send_sem=send, recv_sem=recv, device_id=where, device_id_type=MESH
        )

    their_from = pl.multiple_of(120 - 120 * k, 8)
    their_to = pl.multiple_of(8 * k, 8)
    swaps = []
    for slot, plane in enumerate(PLANES):
        copy = remote(
            source.at[0, plane, pl.ds(their_from, 136), :],
            other.at[slot, pl.ds(their_to, 136), :],
            s0.at[slot], r0.at[slot], (partner, x),
        )
        copy.start()
        swaps.append(copy)

    lifts, strips = [], []
    for part in range(2):
        for slot in (2 * part, 2 * part + 1):
            loads[slot].wait()
            swaps[slot].wait_recv()
            s_buf[slot] = (own[slot] + other[slot]) * ROOT
        if part == 1:
            for q in range(4):
                for slot in range(4):
                    strip[q, slot : slot + 1, :] = s_buf[slot, 7 + 32 * q : 8 + 32 * q, :]
                    strip[q, 4 + slot : 5 + slot, :] = s_buf[slot, 40 + 32 * q : 41 + 32 * q, :]
            for m, chip in enumerate(chips):
                copy = remote(strip.at[chip], rstrip.at[c], st.at[m], rt.at[m], (base + 2 * chip + k, x))
                copy.start()
                strips.append(copy)
        for m, chip in enumerate(chips):
            copy = remote(
                s_buf.at[2 * part : 2 * part + 2, pl.ds(pl.multiple_of(8 + 32 * chip, 8), 32), :],
                rs.at[c, 2 * part : 2 * part + 2],
                sy.at[3 * part + m], ry.at[3 * part + m], (base + 2 * chip + k, x),
            )
            copy.start()
            lifts.append(copy)

    sign = (1 - 2 * k).astype(F32)
    scale = ROOT * sign
    shift_0 = shift_ref[0]
    for slot in range(4):
        pot_loads[slot].wait()
        fd[slot] = (own[slot] - other[slot]) * scale * (OMEGA / (6.0 + pot[slot] + shift_0))
    halo_d = [
        remote(fd.at[0, 8:136, :], hd.at[1], sxd.at[0], rxd.at[0], (t, (x + 3) % 4)),
        remote(fd.at[1, 8:136, :], hd.at[0], sxd.at[1], rxd.at[1], (t, (x + 1) % 4)),
    ]
    for copy in halo_d:
        copy.start()

    lane_block = ones_where(iota((256, 128), 0) // 8 == iota((256, 128), 1) % 32)
    row_block = ones_where(iota((24, 144), 1) // 8 == iota((24, 144), 0))
    pot_sum = pot[0] + pot[1] + pot[2] + pot[3]
    pot_all[0] = dot(row_block, dot(pot_sum, lane_block))
    pots = []
    for m, peer in enumerate(x_peers):
        copy = remote(pot_all.at[0], pot_all.at[m + 1], sp.at[m], rp.at[m], (t, peer))
        copy.start()
        pots.append(copy)

    quarter = pl.multiple_of(8 + 32 * c, 8)
    for slot in range(4):
        here = 6.0 + pot[slot, pl.ds(quarter, 32), :]
        for level in (1, 2, 3):
            r_s[level - 1, slot] = OMEGA / (here + shift_ref[level])
        rs[c, slot] = s_buf[slot, pl.ds(quarter, 32), :]
        above = pot[slot, pl.ds(pl.multiple_of(32 * c, 8), 8), :]
        below = pot[slot, pl.ds(pl.multiple_of(40 + 32 * c, 8), 8), :]
        for level in (1, 2, 3):
            r_strip[level - 1, slot : slot + 1, :] = OMEGA / (6.0 + above[7:8] + shift_ref[level])
            r_strip[level - 1, 4 + slot : 5 + slot, :] = OMEGA / (6.0 + below[0:1] + shift_ref[level])
    rstrip[c] = strip[c]

    keep_low, keep_high = ones_where(x > 0), ones_where(x < 3)
    edge_low, edge_high = 1.0 - keep_low, 1.0 - keep_high
    for copy in halo_d:
        copy.wait_recv()

    def odd_rows(step, _):
        at = pl.multiple_of(32 * step, 8)
        mids = {}
        summed = jnp.zeros((32, 256), F32)
        waves = jnp.zeros((32, 256), F32)
        edges = jnp.zeros((32, 256), F32)
        center = pl.ds(pl.multiple_of(at + 8, 8), 32)
        for plane in range(4):
            slot = SLOT[plane]
            mid, beside = beside_yz(fd[slot, pl.ds(at, 48), :])
            if plane > 0:
                low = fd[SLOT[plane - 1], center, :]
            else:
                low = hd[0, pl.ds(at, 32), :] * keep_low
            if plane < 3:
                high = fd[SLOT[plane + 1], center, :]
            else:
                high = hd[1, pl.ds(at, 32), :] * keep_high
            diagonal = 6.0 + pot[slot, center, :] + shift_0
            second = 1.2 * mid + (OMEGA / diagonal) * (beside + (low + high))
            sd[slot, pl.ds(at, 32), :] = second
            q = second - OMEGA * mid
            summed = summed + q
            waves = waves + (own[slot, center, :] - other[slot, center, :])
            if plane == 0:
                edges = edges + q * edge_low
            if plane == 3:
                edges = edges + q * edge_high
        t_d[pl.ds(at, 32), :] = summed
        x_d[pl.ds(at, 32), :] = (0.04 * scale) * waves - edges
        return 0

    lax.fori_loop(0, 4, odd_rows, 0)

    in_block = iota((256, 128), 0) // 8 == iota((256, 128), 1)
    z_at, z_block = iota((256, 128), 0), iota((256, 128), 1)
    block = ones_where(in_block)
    around = (
        2.0 * block
        + ones_where((z_at + 7) // 8 == z_block + 1)
        + ones_where((z_at + 1) // 8 == z_block)
    )
    around = jnp.where(z_block < 32, around, 0.0)
    y_at, y_row = iota((24, 128), 1), iota((24, 128), 0)
    odd_in = ones_where((y_at // 8 + 1 == y_row))
    odd_beside = ones_where((y_at + 7) // 8 == y_row) + ones_where((y_at + 1) // 8 + 1 == y_row)
    t_now = t_d[...]
    coarse[8:32, :] = dot(odd_in, dot(x_d[...], block) + dot(t_now, around)) + dot(odd_beside, dot(t_now, block))

    def even_first(slot):
        s_0, s_1, s_2, s_3 = (rs[i, slot] for i in range(4))
        u_a, u_b = (s_0 + s_1) * ROOT, (s_2 + s_3) * ROOT
        waves = ((u_a + u_b) * ROOT, (s_0 - s_1) * ROOT, (u_a - u_b) * ROOT, (s_2 - s_3) * ROOT)
        for j in range(4):
            fs[j, slot, 8:40, :] = waves[j] * r_s[LEVELS[j] - 1, slot]
            if slot == 0:
                x_s[j] = waves[j]
            else:
                x_s[j] += waves[j]

    for m in range(3):
        lifts[m].wait_recv()
    even_first(0)
    even_first(1)
    halo_s = [
        remote(fs.at[:, 0, 8:40, :], hs.at[1], sxs.at[0], rxs.at[0], (t, (x + 3) % 4)),
        remote(fs.at[:, 1, 8:40, :], hs.at[0], sxs.at[1], rxs.at[1], (t, (x + 1) % 4)),
    ]
    for copy in halo_s:
        copy.start()
    for copy in strips:
        copy.wait_recv()
    s_0, s_1, s_2, s_3 = (rstrip[i] for i in range(4))
    u_a, u_b = (s_0 + s_1) * ROOT, (s_2 + s_3) * ROOT
    rims = ((u_a + u_b) * ROOT, (s_0 - s_1) * ROOT, (u_a - u_b) * ROOT, (s_2 - s_3) * ROOT)
    for j in range(4):
        rim = rims[j] * r_strip[LEVELS[j] - 1]
        for slot in range(4):
            fs[j, slot, 7:8, :] = rim[slot : slot + 1]
            fs[j, slot, 40:41, :] = rim[4 + slot : 5 + slot]
    for m in range(3):
        lifts[3 + m].wait_recv()
    even_first(2)
    even_first(3)

    def even_second(slot):
        plane = PLANES[slot]
        seconds = []
        for j in range(4):
            mid, beside = beside_yz(fs[j, slot])
            if plane > 0:
                low = fs[j, SLOT[plane - 1], 8:40, :]
            else:
                low = hs[0, j] * keep_low
            if plane < 3:
                high = fs[j, SLOT[plane + 1], 8:40, :]
            else:
                high = hs[1, j] * keep_high
            second = 1.2 * mid + r_s[LEVELS[j] - 1, slot] * (beside + (low + high))
            q = second - OMEGA * mid
            if slot == 2:
                t_s[j] = q
                x_s[j] = 0.04 * x_s[j]
            else:
                t_s[j] += q
            if plane == 0:
                x_s[j] -= q * edge_low
            if plane == 3:
                x_s[j] -= q * edge_high
            seconds.append(second)
        u_a, u_b = (seconds[0] + seconds[2]) * ROOT, (seconds[0] - seconds[2]) * ROOT
        sb[0, slot] = (u_a + seconds[1]) * ROOT
        sb[1, slot] = (u_a - seconds[1]) * ROOT
        sb[2, slot] = (u_b + seconds[3]) * ROOT
        sb[3, slot] = (u_b - seconds[3]) * ROOT

    backs = {}
    own_rows = pl.ds(pl.multiple_of(32 * c, 8), 32)
    for part in (1, 0):
        if part == 0:
            for copy in halo_s:
                copy.wait_recv()
        even_second(2 * part)
        even_second(2 * part + 1)
        for m, chip in enumerate(chips):
            copy = remote(
                sb.at[chip, 2 * part : 2 * part + 2],
                bk.at[2 * part : 2 * part + 2, own_rows, :],
                sbk.at[3 * part + m], rbk.at[3 * part + m], (base + 2 * chip + k, x),
            )
            copy.start()
            backs[part, m] = copy
    for slot in range(4):
        bk[slot, own_rows, :] = sb[c, slot]

    y_at, y_row = iota((32, 128), 1), iota((32, 128), 0)
    same = y_at // 32 == y_row // 8
    y_at, y_row = y_at % 32, y_row % 8
    even_in = ones_where(same & (y_at // 8 + 1 == y_row))
    even_beside = ones_where(same & ((y_at + 7) // 8 == y_row)) + ones_where(same & ((y_at + 1) // 8 + 1 == y_row))
    t_now = t_s[...].reshape(128, 256)
    sums = dot(even_in, dot(x_s[...].reshape(128, 256), block) + dot(t_now, around)) + dot(even_beside, dot(t_now, block))
    packed = sums[0:8]
    for j in (1, 2, 3):
        packed = packed + pltpu.roll(sums[8 * j : 8 * j + 8], 32 * j, 1)
    coarse[0:8, :] = packed
    reduces = []
    for m, peer in enumerate(x_peers):
        copy = remote(coarse, coarse_x.at[m], sc.at[m], rc.at[m], (t, peer))
        copy.start()
        reduces.append(copy)
    for copy in pots:
        copy.wait_recv()
    for copy in reduces:
        copy.wait_recv()
    total[...] = (coarse[...] + coarse_x[0]) + (coarse_x[1] + coarse_x[2])
    gathers = []
    for m, peer in enumerate(group):
        copy = remote(total.at[0:8, :], tr.at[e], sg.at[m], rg.at[m], (peer, x))
        copy.start()
        gathers.append(copy)
    pair = remote(total.at[8:32, :], dr, sdp, rdp, (partner, x))
    pair.start()
    tr[e] = total[0:8, :]
    coarse_pot = (pot_all[0] + pot_all[1]) + (pot_all[2] + pot_all[3])
    for copy in gathers:
        copy.wait_recv()
    pair.wait_recv()

    row, col = iota((24, 64), 0), iota((24, 64), 1)
    sender, r = col // 8, col % 8
    where = 16 * (sender % 2) + 4 * (sender // 2) - 1 + r
    pick = ones_where((r < 6) & (where >= 0) & (where < 32) & (where == 16 * k - 1 + row))
    even_rem = dot(pick, tr[...].reshape(64, 128))
    row, col = iota((24, 24), 0), iota((24, 24), 1)
    where = 16 * (1 - k) - 1 + col
    pick = ones_where((col < 18) & (where >= 0) & (where < 32) & (where == 16 * k - 1 + row))
    row = iota((24, 128), 0)
    lane = iota((24, 128), 1)
    inside = (row < 18) & (16 * k - 1 + row >= 0) & (16 * k - 1 + row < 32)
    odd_rem = jnp.where(inside, total[8:32, :], 0.0) + dot(pick, dr[...])
    coef = lane // 32
    shifts = jnp.where(
        coef == 0, shift_ref[3], jnp.where(coef == 2, shift_ref[2], shift_ref[1])
    )

    def coarse_fix(rem, shift):
        diag = coarse_pot + shift * 1024.0 + 640.0
        one = rem / diag
        up, down = pltpu.roll(one, 1, 0), pltpu.roll(one, 23, 0)
        left = jnp.where(lane % 32 == 0, 0.0, pltpu.roll(one, 1, 1))
        right = jnp.where(lane % 32 == 31, 0.0, pltpu.roll(one, 127, 1))
        applied = diag * one - 128.0 * ((up + down) + (left + right))
        return one + (rem - applied) / diag

    half = jnp.where(coef == 2, jnp.where(c < 2, 0.5, -0.5), 0.5)
    detail = jnp.where(coef == 1, jnp.where(c == 0, ROOT, jnp.where(c == 1, -ROOT, 0.0)), 0.0)
    detail = detail + jnp.where(coef == 3, jnp.where(c == 2, ROOT, jnp.where(c == 3, -ROOT, 0.0)), 0.0)
    weight = jnp.where(coef % 2 == 0, half, detail)
    even_fix = coarse_fix(even_rem, shifts) * weight
    odd_fix = jnp.where(lane < 32, coarse_fix(odd_rem, shift_0), 0.0)
    widen = ones_where(iota((128, 256), 0) % 32 == iota((128, 256), 1) // 8)
    heighten = ones_where(iota((128, 24), 0) // 8 + 1 == iota((128, 24), 1))
    xs[...] = dot(heighten, dot(even_fix, widen))
    xd[...] = dot(heighten, dot(odd_fix, widen)) * sign

    half_rows = pl.ds(pl.multiple_of(128 * k, 8), 128)
    sends, stores = [], []
    for part in (1, 0):
        for m in range(3):
            backs[part, m].wait_recv()
        for slot in (2 * part, 2 * part + 1):
            even = bk[slot] + xs[...]
            odd = sd[slot] * sign + xd[...]
            yours[slot] = (even - odd) * ROOT
            there = out.at[0, PLANES[slot], half_rows, :]
            copy = remote(yours.at[slot], there, so.at[slot], ro.at[slot], (partner, x))
            copy.start()
            sends.append(copy)
            mine[slot] = (even + odd) * ROOT
            copy = pltpu.make_async_copy(mine.at[slot], there, lo.at[slot])
            copy.start()
            stores.append(copy)

    for copy in swaps + lifts + strips + halo_d + halo_s + pots + reduces + gathers + [pair] + list(backs.values()):
        copy.wait_send()
    for copy in sends + stores:
        copy.wait()


def shards(source, potential, level_shift):
    dma = pltpu.SemaphoreType.DMA
    vmem = lambda *shape: pltpu.VMEM(shape, F32)
    scratch = dict(
        own=vmem(4, 144, 256), other=vmem(4, 144, 256), pot=vmem(4, 144, 256), s_buf=vmem(4, 144, 256),
        fd=vmem(4, 144, 256), sd=vmem(4, 128, 256), strip=vmem(4, 8, 256), rs=vmem(4, 4, 32, 256),
        rstrip=vmem(4, 8, 256), fs=vmem(4, 4, 48, 256), r_s=vmem(3, 4, 32, 256), r_strip=vmem(3, 8, 256),
        hd=vmem(2, 128, 256), hs=vmem(2, 4, 32, 256), sb=vmem(4, 4, 32, 256), bk=vmem(4, 128, 256),
        t_d=vmem(128, 256), x_d=vmem(128, 256), t_s=vmem(4, 32, 256), x_s=vmem(4, 32, 256),
        pot_all=vmem(4, 24, 128), coarse=vmem(32, 128), coarse_x=vmem(3, 32, 128), total=vmem(32, 128),
        tr=vmem(8, 8, 128), dr=vmem(24, 128), xs=vmem(128, 256), xd=vmem(128, 256),
        mine=vmem(4, 128, 256), yours=vmem(4, 128, 256),
        l_sem=dma((4,)), p_sem=dma((4,)), s0=dma((4,)), r0=dma((4,)), sy=dma((6,)), ry=dma((6,)),
        st=dma((3,)), rt=dma((3,)), sxd=dma((2,)), rxd=dma((2,)), sxs=dma((2,)), rxs=dma((2,)),
        sp=dma((3,)), rp=dma((3,)), sc=dma((3,)), rc=dma((3,)), sg=dma((7,)), rg=dma((7,)),
        sdp=dma(()), rdp=dma(()), sbk=dma((6,)), rbk=dma((6,)), so=dma((4,)), ro=dma((4,)), lo=dma((4,)),
    )
    return pl.pallas_call(
        kernel,
        out_shape=jax.ShapeDtypeStruct(source.shape, F32),
        in_specs=[
            pl.BlockSpec(memory_space=pltpu.SMEM),
            pl.BlockSpec(memory_space=pl.ANY),
            pl.BlockSpec(memory_space=pl.ANY),
        ],
        out_specs=pl.BlockSpec(memory_space=pl.ANY),
        scratch_shapes=list(scratch.values()),
        compiler_params=pltpu.CompilerParams(
            collective_id=0, has_side_effects=True, vmem_limit_bytes=40 * 2**20
        ),
        name="space_time_apply",
    )(level_shift, source, potential)


def solution(mesh):
    in_specs = (P("tm", "plane", None, None), P("plane", None, None), P())
    out_specs = P("tm", "plane", None, None)
    return jax.shard_map(shards, mesh=mesh, in_specs=in_specs, out_specs=out_specs, check_vma=False)
```

time: 232 us -> 44.9 us (0.19)
  waiting for transfers between devices: 151 us -> 0 us
  Pallas kernels: 0 us -> 40.6 us
  starting transfers between devices: 31.8 us -> 0 us
  other arithmetic: 17.1 us -> 0 us
  blocking collectives: 14 us -> 0 us
  local copies, waits for them, and re-layouts: 16.3 us -> 4.08 us
    ppermute x10 -> x0, waiting for transfers between devices: 151 us -> none  [the longest x6 145 us: from_partner(): lax.ppermute(value, axis, [(i, i ^ 1 << stride) for i in range(lax.axis_s...]
    pallas_call x0 -> x1, Pallas kernels: none -> 40.6 us  [shards(): pl.pallas_call(kernel, out_shape=jax.ShapeDtypeStruct(source.shape, F32),...]
    ppermute x10 -> x0, starting transfers between devices: 31.8 us -> none  [the longest x6 19.8 us: from_partner(): lax.ppermute(value, axis, [(i, i ^ 1 << stride) for i in range(lax.axis_s...]
    psum x1 -> x0, blocking collectives: 14 us -> none  [shards(): lax.psum((block_sum(remainder), block_sum(potential)), 'plane')]
    reduce_sum x4 -> x0, other arithmetic: 8.86 us -> none  [the longest x3 8.19 us: block_sum(): field.reshape(planes, rows // CB, CB, cols // CB, CB).sum(axis=(0, 2, 4))]
    reduce_sum x2 -> x0, local copies, waits for them, and re-layouts: 8.13 us -> none  [block_sum(): field.reshape(planes, rows // CB, CB, cols // CB, CB).sum(axis=(0, 2, 4))]
    select_n x5 -> x0, other arithmetic: 4.42 us -> none  [the longest x2 2.54 us: time_lift(): jnp.where(upper_bit == 0, (block + partner) * INV_ROOT, (partner - block)...]
    add x1 -> x0, local copies, waits for them, and re-layouts: 4.02 us -> none  [shards(): fixed = (second_pass + prolong(correction)[None])[None]]
  transfers between devices with their start and end apart: 10 -> 0, of which waited for: 10 -> 0; matrix products, arithmetic and copies ran while one was open for 0% -> 0% of each run, Pallas kernels for 0% -> 0%
where the time goes in v1:
time: 44.9 us; the launch traced here: 44.7 us
  Pallas kernels  40.6 us (90%)
  local copies, waits for them, and re-layouts  4.08 us (9%)
    pallas_call x1, Pallas kernels, shards(): pl.pallas_call(kernel, out_shape=jax.ShapeDtypeStruct(source.shape, F32),...  40.6 us
    unnamed x7, local copies, waits for them, and re-layouts  4.08 us

profile of v1, /device:TPU:1, one launch (start us, length us, event | category | flops | bytes accessed | tf_op | source)
XLA Modules:
  0.0 44.7 jit_solution(13392476582691250635)
XLA Ops:
  0.0 0.0 copy-start
  0.0 1.2 %copy-done = f32[1,4,256,256]{3,2,1,0:T(8,128)S(1)} copy-done((f32[1,4,256,256]{3,2,1,0:T(8,128)S(1)}, f32[1,4,256,256]{3,2,1,0:T(8,128)}, u32[]{:S(2)}) %copy-start) | copy-done | bytes 1048600
  1.2 0.0 copy-start.1
  1.2 1.2 %copy-done.1 = f32[4,256,256]{2,1,0:T(8,128)S(1)} copy-done((f32[4,256,256]{2,1,0:T(8,128)S(1)}, f32[4,256,256]{2,1,0:T(8,128)}, u32[]{:S(2)}) %copy-start.1) | copy-done | bytes 1048600
  2.5 0.0 copy-start.2
  2.5 0.7 %copy-done.2 = f32[4]{0:T(128)S(1)} copy-done((f32[4]{0:T(128)S(1)}, f32[4]{0:T(128)}, u32[]{:S(2)}) %copy-start.2) | copy-done | bytes 40
  3.1 40.6 %space_time_apply.1 = f32[1,4,256,256]{3,2,1,0:T(8,128)S(1)} custom-call(f32[4]{0:T(128)S(1)} %copy-done.2, f32[1,4,256,256]{3,2,1,0:T(8,128)S(1)} %copy-done, f32[4,256,256]{2,1,0:T(8,128)S(1)} %copy-done.1), custom_call_target="tpu_custom_call" | custom-call | tf_op jit(solution)/shard_map/space_time_apply/pallas_call | solution.py:420
  43.8 1.0 %copy.5 = f32[1,4,256,256]{3,2,1,0:T(8,128)} copy(f32[1,4,256,256]{3,2,1,0:T(8,128)S(1)} %space_time_apply.1) | data formatting | bytes 2097152
Async XLA Ops:
  0.0 1.2 %copy-start = (f32[1,4,256,256]{3,2,1,0:T(8,128)S(1)}, f32[1,4,256,256]{3,2,1,0:T(8,128)}, u32[]{:S(2)}) copy-start(f32[1,4,256,256]{3,2,1,0:T(8,128)} %source.1) | copy-start | bytes 3145732
  1.2 1.2 %copy-start.1 = (f32[4,256,256]{2,1,0:T(8,128)S(1)}, f32[4,256,256]{2,1,0:T(8,128)}, u32[]{:S(2)}) copy-start(f32[4,256,256]{2,1,0:T(8,128)} %potential.1) | copy-start | bytes 3145732
  2.5 0.7 %copy-start.2 = (f32[4]{0:T(128)S(1)}, f32[4]{0:T(128)}, u32[]{:S(2)}) copy-start(f32[4]{0:T(128)} %shift_ref.1) | copy-start | bytes 52

commit v2 on v0

v2 whole, which is shorter than its diff:
```python
import math

import jax
import jax.numpy as jnp
from jax import lax
from jax.experimental import pallas as pl
from jax.experimental.pallas import tpu as pltpu
from jax.sharding import PartitionSpec as P

F32 = jnp.float32
MESH = pl.DeviceIdType.MESH
ROOT = 1.0 / math.sqrt(2.0)
OMEGA = 0.8
PLANES = (0, 3, 1, 2)
SLOT = {plane: slot for slot, plane in enumerate(PLANES)}


def dot(a, b):
    return jnp.dot(a, b, precision=lax.Precision.HIGHEST, preferred_element_type=F32)


def iota(shape, dim):
    return lax.broadcasted_iota(jnp.int32, shape, dim)


def ones_where(mask):
    return jnp.where(mask, 1.0, 0.0).astype(F32)


def beside_yz(ext):
    rows = ext.shape[0] - 16
    mid = ext[8 : 8 + rows]
    up = pltpu.roll(ext, 1, 0)[8 : 8 + rows]
    down = pltpu.roll(ext, rows + 15, 0)[8 : 8 + rows]
    col = iota(mid.shape, 1)
    left = jnp.where(col == 0, 0.0, pltpu.roll(mid, 1, 1))
    right = jnp.where(col == 255, 0.0, pltpu.roll(mid, 255, 1))
    return mid, (up + down) + (left + right)


def kernel(
    shift_hbm, source, potential, out,
    shift_ref, own, other, pot, s_buf, rd, fd, sd, strip, nb, nstrip, u_buf, fv, rv, sv, ustrip, nu, nustrip, fu, ru,
    hd, hv, hu, ub, give, bk, gives, t_d, x_d, t_v, x_v, t_u, x_u, pot_all, coarse, coarse_x, total, tr, pick,
    xs, xd, mine, yours,
    h_sem, l_sem, p_sem, s0, r0, s1, r1, s2, r2, st, rt, su, ru_sem, sx, rx, sp, rp, sc, rc, sg, rg,
    sb2, rb2, sb1, rb1, so, ro, lo,
):
    t, x = lax.axis_index("tm"), lax.axis_index("plane")
    e = t % 8
    k, c = e % 2, e // 2
    b, p = c % 2, c // 2
    partner = t + 1 - 2 * k
    near = t + 2 - 4 * b
    far = t + 4 - 8 * p
    x_peers = [(x + m) % 4 for m in (1, 2, 3)]
    group = [t - e + (e + m) % 8 for m in range(1, 8)]

    barrier = pltpu.get_barrier_semaphore()
    for peer in group:
        pl.semaphore_signal(barrier, inc=1, device_id=(peer, x), device_id_type=MESH)
    for peer in x_peers:
        pl.semaphore_signal(barrier, inc=1, device_id=(t, peer), device_id_type=MESH)

    def rows(start, count):
        return pl.ds(pl.multiple_of(start, 8), count)

    def remote(src, dst, send, recv, where):
        copy = pltpu.make_async_remote_copy(
            src_ref=src, dst_ref=dst, send_sem=send, recv_sem=recv, device_id=where, device_id_type=MESH
        )
        copy.start()
        return copy

    def local(src, dst, sem):
        copy = pltpu.make_async_copy(src, dst, sem)
        copy.start()
        return copy

    loads = [
        local(source.at[0, plane, rows(120 * k, 136), :], own.at[slot, rows(8 - 8 * k, 136), :], l_sem.at[slot])
        for slot, plane in enumerate(PLANES)
    ]
    shift_load = local(shift_hbm, shift_ref, h_sem)
    pot_loads = [
        local(potential.at[plane, rows(120 * k, 136), :], pot.at[slot, rows(8 - 8 * k, 136), :], p_sem.at[slot])
        for slot, plane in enumerate(PLANES)
    ]
    for slot in range(4):
        for ref in (own, other, pot):
            ref[slot, rows(136 * k, 8), :] = jnp.zeros((8, 256), F32)

    pl.semaphore_wait(barrier, 10)

    swaps = [
        remote(
            source.at[0, plane, rows(120 - 120 * k, 136), :], other.at[slot, rows(8 * k, 136), :],
            s0.at[slot], r0.at[slot], (partner, x),
        )
        for slot, plane in enumerate(PLANES)
    ]

    firsts = []
    for slot in range(4):
        loads[slot].wait()
        swaps[slot].wait_recv()
        s_buf[slot] = (own[slot] + other[slot]) * ROOT
        if slot == 3:
            for q in range(2):
                for i in range(4):
                    strip[q, i : i + 1, :] = s_buf[i, 7 + 64 * q : 8 + 64 * q, :]
                    strip[q, 4 + i : 5 + i, :] = s_buf[i, 72 + 64 * q : 73 + 64 * q, :]
            strip_1 = remote(strip.at[1 - b], nstrip, st, rt, (near, x))
        firsts.append(
            remote(s_buf.at[slot, rows(72 - 64 * b, 64), :], nb.at[slot], s1.at[slot], r1.at[slot], (near, x))
        )

    sign = (1 - 2 * k).astype(F32)
    near_sign = (1 - 2 * b).astype(F32)
    far_sign = (1 - 2 * p).astype(F32)
    scale = ROOT * sign
    keep_low, keep_high = ones_where(x > 0), ones_where(x < 3)
    edge_low, edge_high = 1.0 - keep_low, 1.0 - keep_high
    shift_load.wait()
    shift_0 = shift_ref[0]
    for slot in range(4):
        pot_loads[slot].wait()
        rd[slot] = OMEGA / (6.0 + pot[slot] + shift_0)
        fd[slot] = (own[slot] - other[slot]) * scale * rd[slot]
    below, above = (t, (x + 3) % 4), (t, (x + 1) % 4)
    halo_d = [
        remote(fd.at[0, 8:136, :], hd.at[1], sx.at[0], rx.at[0], below),
        remote(fd.at[1, 8:136, :], hd.at[0], sx.at[1], rx.at[1], above),
    ]

    for slot in range(4):
        rv[slot] = OMEGA / (6.0 + pot[slot, rows(64 * b, 80), :] + shift_ref[1])
        here = 6.0 + pot[slot, rows(64 * b + 32 * p, 48), :]
        ru[0, slot] = OMEGA / (here + shift_ref[3])
        ru[1, slot] = OMEGA / (here + shift_ref[2])

    lane_block = ones_where(iota((256, 128), 0) // 8 == iota((256, 128), 1) % 32)
    row_block = ones_where(iota((24, 144), 1) // 8 == iota((24, 144), 0))
    pot_sum = (pot[0] + pot[1]) + (pot[2] + pot[3])
    pot_all[0] = dot(row_block, dot(pot_sum, lane_block))
    pots = [
        remote(pot_all.at[0], pot_all.at[m + 1], sp.at[m], rp.at[m], (t, peer)) for m, peer in enumerate(x_peers)
    ]

    seconds = []
    for slot in range(4):
        firsts[slot].wait_recv()
        here = s_buf[slot, rows(8 + 64 * b, 64), :]
        u_buf[slot, 8:72, :] = (here + nb[slot]) * ROOT
        seconds.append(
            remote(u_buf.at[slot, rows(40 - 32 * p, 32), :], nu.at[slot], s2.at[slot], r2.at[slot], (far, x))
        )
        detail = (here - nb[slot]) * (ROOT * near_sign)
        fv[slot, 8:72, :] = detail * rv[slot, 8:72, :]
        x_v[...] = detail if slot == 0 else x_v[...] + detail
        if slot == 1:
            halo_v = [
                remote(fv.at[0, 8:72, :], hv.at[1], sx.at[2], rx.at[2], below),
                remote(fv.at[1, 8:72, :], hv.at[0], sx.at[3], rx.at[3], above),
            ]
    strip_1.wait_recv()
    here = strip[b]
    sums = (here + nstrip[...]) * ROOT
    details = (here - nstrip[...]) * (ROOT * near_sign)
    for slot in range(4):
        u_buf[slot, 7:8, :] = sums[slot : slot + 1]
        u_buf[slot, 72:73, :] = sums[4 + slot : 5 + slot]
        fv[slot, 7:8, :] = details[slot : slot + 1] * rv[slot, 7:8, :]
        fv[slot, 72:73, :] = details[4 + slot : 5 + slot] * rv[slot, 72:73, :]
    for q in range(2):
        for i in range(4):
            ustrip[q, i : i + 1, :] = u_buf[i, 7 + 32 * q : 8 + 32 * q, :]
            ustrip[q, 4 + i : 5 + i, :] = u_buf[i, 40 + 32 * q : 41 + 32 * q, :]
    strip_2 = remote(ustrip.at[1 - p], nustrip, su, ru_sem, (far, x))

    row, col = iota((24, 192), 0), iota((24, 192), 1)
    sender, r = col // 24, col % 24
    sk, sc_, sb, sp_ = sender % 2, sender // 2, sender // 2 % 2, sender // 4
    wanted = 16 * k - 1 + row
    real = (wanted >= 0) & (wanted < 32) & (row < 18)
    pick[0] = ones_where(real & (r < 6) & (16 * sk + 8 * sb + 4 * sp_ - 1 + r == wanted))
    pick[1] = ones_where(real & (r < 10) & (sp_ == p) & (16 * sk + 8 * sb - 1 + r == wanted))
    pick[2] = ones_where(real & (r < 18) & (sc_ == c) & (16 * sk - 1 + r == wanted))

    z_at, z_block = iota((256, 128), 0), iota((256, 128), 1)
    block = ones_where(z_at // 8 == z_block)
    around = (
        2.0 * block
        + ones_where((z_at + 7) // 8 == z_block + 1)
        + ones_where((z_at + 1) // 8 == z_block)
    )
    around = jnp.where(z_block < 32, around, 0.0)

    def block_sums(fields, outer, out_rows, span, stride):
        shape = (out_rows, fields.shape[0])
        y_at, y_row = iota(shape, 1), iota(shape, 0)
        same = y_at // span == y_row // stride
        y_at, y_row = y_at % span, y_row % stride
        inner = ones_where(same & (y_at // 8 + 1 == y_row))
        beside = ones_where(same & ((y_at + 7) // 8 == y_row)) + ones_where(same & ((y_at + 1) // 8 + 1 == y_row))
        return dot(inner, dot(outer, block) + dot(fields, around)) + dot(beside, dot(fields, block))

    def second_pass(f, weight, low_rim, high_rim, at, order, done):
        center = rows(at + 8, 32)
        total, outer = None, None
        for plane in order:
            slot = SLOT[plane]
            mid, beside = beside_yz(f[slot, rows(at, 48), :])
            low = f[SLOT[plane - 1], center, :] if plane > 0 else low_rim() * keep_low
            high = f[SLOT[plane + 1], center, :] if plane < 3 else high_rim() * keep_high
            second = 1.2 * mid + weight[slot, center, :] * (beside + (low + high))
            done(slot, second)
            q = second - OMEGA * mid
            total = q if total is None else total + q
            if plane in (0, 3):
                rim = q * (edge_low if plane == 0 else edge_high)
                outer = rim if outer is None else outer + rim
        return total, outer

    for copy in halo_d:
        copy.wait_recv()

    def odd_rows(step, _):
        at = 32 * step
        here = rows(at, 32)

        def done(slot, second):
            sd[slot, here, :] = second

        summed, outer = second_pass(
            fd, rd, lambda: hd[0, here, :], lambda: hd[1, here, :], at, range(4), done
        )
        center = rows(at + 8, 32)
        waves = (own[0, center, :] - other[0, center, :]) + (own[1, center, :] - other[1, center, :])
        waves = waves + (own[2, center, :] - other[2, center, :]) + (own[3, center, :] - other[3, center, :])
        t_d[here, :] = summed
        x_d[here, :] = (0.04 * scale) * waves - outer
        return 0

    lax.fori_loop(0, 4, odd_rows, 0)

    for copy in halo_v:
        copy.wait_recv()

    def near_rows(step, _):
        at = 32 * step
        here = rows(at, 32)

        def done(slot, second):
            sv[slot, here, :] = second

        summed, outer = second_pass(
            fv, rv, lambda: hv[0, here, :], lambda: hv[1, here, :], at, range(4), done
        )
        t_v[here, :] = summed
        x_v[here, :] = 0.04 * x_v[here, :] - outer
        return 0

    lax.fori_loop(0, 2, near_rows, 0)
    coarse[...] = pltpu.roll(block_sums(t_d[...], x_d[...], 24, 128, 24), 96, 1) + pltpu.roll(
        block_sums(t_v[...], x_v[...], 24, 64, 24), 64, 1
    )

    for slot in range(4):
        seconds[slot].wait_recv()
        here = u_buf[slot, rows(8 + 32 * p, 32), :]
        low, high = (here + nu[slot]) * ROOT, (here - nu[slot]) * (ROOT * far_sign)
        fu[0, slot, 8:40, :] = low * ru[0, slot, 8:40, :]
        fu[1, slot, 8:40, :] = high * ru[1, slot, 8:40, :]
        x_u[0] = low if slot == 0 else x_u[0] + low
        x_u[1] = high if slot == 0 else x_u[1] + high
        if slot == 1:
            halo_u = [
                remote(fu.at[:, 0, 8:40, :], hu.at[1], sx.at[4], rx.at[4], below),
                remote(fu.at[:, 1, 8:40, :], hu.at[0], sx.at[5], rx.at[5], above),
            ]
    strip_2.wait_recv()
    here = ustrip[p]
    low, high = (here + nustrip[...]) * ROOT, (here - nustrip[...]) * (ROOT * far_sign)
    for slot in range(4):
        for j, rim in enumerate((low, high)):
            fu[j, slot, 7:8, :] = rim[slot : slot + 1] * ru[j, slot, 7:8, :]
            fu[j, slot, 40:41, :] = rim[4 + slot : 5 + slot] * ru[j, slot, 40:41, :]

    backs_2 = {}
    for planes in ((1,), (2,), (0,), (3,)):
        if planes == (0,):
            for copy in halo_u:
                copy.wait_recv()
        made = []
        for j in range(2):
            summed, outer = second_pass(
                fu.at[j], ru.at[j], lambda j=j: hu[0, j], lambda j=j: hu[1, j], 0, planes,
                lambda slot, second: made.append(second),
            )
            t_u[j] = summed if planes == (1,) else t_u[j] + summed
            x_u[j] = 0.04 * x_u[j] if planes == (1,) else x_u[j]
            if outer is not None:
                x_u[j] = x_u[j] - outer
        slot = SLOT[planes[0]]
        low, high = made[0] * ROOT, made[1] * (ROOT * far_sign)
        give[slot] = low - high
        backs_2[slot] = remote(
            give.at[slot], ub.at[slot, rows(32 * p, 32), :], sb2.at[slot], rb2.at[slot], (far, x)
        )
        ub[slot, rows(32 * p, 32), :] = low + high

    sums = block_sums(t_u[...].reshape(64, 256), x_u[...].reshape(64, 256), 16, 32, 8)
    coarse[0:8, :] = coarse[0:8, :] + (sums[0:8] + pltpu.roll(sums[8:16], 32, 1))
    reduces = [
        remote(coarse, coarse_x.at[m], sc.at[m], rc.at[m], (t, peer)) for m, peer in enumerate(x_peers)
    ]

    backs_1 = {}

    def level_1(slot):
        backs_2[slot].wait_recv()
        low, high = ub[slot] * ROOT, sv[slot] * (ROOT * near_sign)
        gives[slot] = low - high
        backs_1[slot] = remote(
            gives.at[slot], bk.at[slot, rows(64 * b, 64), :], sb1.at[slot], rb1.at[slot], (near, x)
        )
        bk[slot, rows(64 * b, 64), :] = low + high

    level_1(2)
    level_1(3)
    for copy in pots + reduces:
        copy.wait_recv()
    total[...] = (coarse[...] + coarse_x[0]) + (coarse_x[1] + coarse_x[2])
    gathers = [
        remote(total, tr.at[e], sg.at[m], rg.at[m], (peer, x)) for m, peer in enumerate(group)
    ]
    tr[e] = total[...]
    level_1(0)
    level_1(1)
    for copy in gathers:
        copy.wait_recv()

    lane = iota((24, 128), 1)
    coef = lane // 32
    sent = tr[...].reshape(192, 128)
    rem = jnp.where(coef < 2, dot(pick[0], sent), jnp.where(coef == 2, dot(pick[1], sent), dot(pick[2], sent)))
    shift = jnp.where(
        coef == 0, shift_ref[3], jnp.where(coef == 1, shift_ref[2], jnp.where(coef == 2, shift_ref[1], shift_0))
    )
    coarse_pot = (pot_all[0] + pot_all[1]) + (pot_all[2] + pot_all[3])
    diag = coarse_pot + shift * 1024.0 + 640.0
    one = rem / diag
    up, down = pltpu.roll(one, 1, 0), pltpu.roll(one, 23, 0)
    left = jnp.where(lane % 32 == 0, 0.0, pltpu.roll(one, 1, 1))
    right = jnp.where(lane % 32 == 31, 0.0, pltpu.roll(one, 127, 1))
    applied = diag * one - 128.0 * ((up + down) + (left + right))
    fix = one + (rem - applied) / diag
    weight = jnp.where(coef == 0, 0.5, jnp.where(coef == 1, 0.5 * far_sign, ROOT * near_sign))
    widen = ones_where(iota((128, 256), 0) % 32 == iota((128, 256), 1) // 8)
    heighten = ones_where(iota((128, 24), 0) // 8 + 1 == iota((128, 24), 1))
    xs[...] = dot(heighten, dot(jnp.where(coef < 3, fix * weight, 0.0), widen))
    xd[...] = dot(heighten, dot(jnp.where(coef == 3, fix, 0.0), widen)) * sign

    sends, stores = [], []
    for slot in (2, 3, 0, 1):
        backs_1[slot].wait_recv()
        even = bk[slot] + xs[...]
        odd = sd[slot] * sign + xd[...]
        yours[slot] = (even - odd) * ROOT
        there = out.at[0, PLANES[slot], rows(128 * k, 128), :]
        sends.append(remote(yours.at[slot], there, so.at[slot], ro.at[slot], (partner, x)))
        mine[slot] = (even + odd) * ROOT
        stores.append(local(mine.at[slot], there, lo.at[slot]))

    sent_all = swaps + firsts + seconds + [strip_1, strip_2] + halo_d + halo_v + halo_u + pots + reduces + gathers
    for copy in sent_all + list(backs_2.values()) + list(backs_1.values()):
        copy.wait_send()
    for copy in sends + stores:
        copy.wait()


def shards(source, potential, level_shift):
    dma = pltpu.SemaphoreType.DMA
    vmem = lambda *shape: pltpu.VMEM(shape, F32)
    scratch = dict(
        shift_ref=pltpu.SMEM((4,), F32),
        own=vmem(4, 144, 256), other=vmem(4, 144, 256), pot=vmem(4, 144, 256), s_buf=vmem(4, 144, 256),
        rd=vmem(4, 144, 256), fd=vmem(4, 144, 256), sd=vmem(4, 128, 256), strip=vmem(2, 8, 256),
        nb=vmem(4, 64, 256), nstrip=vmem(8, 256), u_buf=vmem(4, 80, 256), fv=vmem(4, 80, 256), rv=vmem(4, 80, 256),
        sv=vmem(4, 64, 256), ustrip=vmem(2, 8, 256), nu=vmem(4, 32, 256), nustrip=vmem(8, 256),
        fu=vmem(2, 4, 48, 256), ru=vmem(2, 4, 48, 256),
        hd=vmem(2, 128, 256), hv=vmem(2, 64, 256), hu=vmem(2, 2, 32, 256),
        ub=vmem(4, 64, 256), give=vmem(4, 32, 256), bk=vmem(4, 128, 256), gives=vmem(4, 64, 256),
        t_d=vmem(128, 256), x_d=vmem(128, 256), t_v=vmem(64, 256), x_v=vmem(64, 256),
        t_u=vmem(2, 32, 256), x_u=vmem(2, 32, 256),
        pot_all=vmem(4, 24, 128), coarse=vmem(24, 128), coarse_x=vmem(3, 24, 128), total=vmem(24, 128),
        tr=vmem(8, 24, 128), pick=vmem(3, 24, 192), xs=vmem(128, 256), xd=vmem(128, 256),
        mine=vmem(4, 128, 256), yours=vmem(4, 128, 256),
        h_sem=dma(()), l_sem=dma((4,)), p_sem=dma((4,)), s0=dma((4,)), r0=dma((4,)), s1=dma((4,)), r1=dma((4,)),
        s2=dma((4,)), r2=dma((4,)), st=dma(()), rt=dma(()), su=dma(()), ru_sem=dma(()), sx=dma((6,)), rx=dma((6,)),
        sp=dma((3,)), rp=dma((3,)), sc=dma((3,)), rc=dma((3,)), sg=dma((7,)), rg=dma((7,)),
        sb2=dma((4,)), rb2=dma((4,)), sb1=dma((4,)), rb1=dma((4,)), so=dma((4,)), ro=dma((4,)), lo=dma((4,)),
    )
    return pl.pallas_call(
        kernel,
        out_shape=jax.ShapeDtypeStruct(source.shape, F32),
        in_specs=[
            pl.BlockSpec(memory_space=pltpu.HBM),
            pl.BlockSpec(memory_space=pltpu.HBM),
            pl.BlockSpec(memory_space=pltpu.HBM),
        ],
        out_specs=pl.BlockSpec(memory_space=pl.ANY),
        scratch_shapes=list(scratch.values()),
        compiler_params=pltpu.CompilerParams(
            collective_id=0, has_side_effects=True, vmem_limit_bytes=105 * 2**19
        ),
        name="space_time_apply",
    )(level_shift, source, potential)


def solution(mesh):
    in_specs = (P("tm", "plane", None, None), P("plane", None, None), P())
    out_specs = P("tm", "plane", None, None)
    return jax.shard_map(shards, mesh=mesh, in_specs=in_specs, out_specs=out_specs, check_vma=False)
```

time: 232 us -> 41.1 us (0.18)
  waiting for transfers between devices: 151 us -> 0 us
  Pallas kernels: 0 us -> 39.3 us
  starting transfers between devices: 31.8 us -> 0 us
  other arithmetic: 17.1 us -> 0 us
  local copies, waits for them, and re-layouts: 16.3 us -> 1.63 us
  blocking collectives: 14 us -> 0 us
    ppermute x10 -> x0, waiting for transfers between devices: 151 us -> none  [the longest x6 145 us: from_partner(): lax.ppermute(value, axis, [(i, i ^ 1 << stride) for i in range(lax.axis_s...]
    pallas_call x0 -> x1, Pallas kernels: none -> 39.3 us  [shards(): pl.pallas_call(kernel, out_shape=jax.ShapeDtypeStruct(source.shape, F32),...]
    ppermute x10 -> x0, starting transfers between devices: 31.8 us -> none  [the longest x6 19.8 us: from_partner(): lax.ppermute(value, axis, [(i, i ^ 1 << stride) for i in range(lax.axis_s...]
    psum x1 -> x0, blocking collectives: 14 us -> none  [shards(): lax.psum((block_sum(remainder), block_sum(potential)), 'plane')]
    reduce_sum x4 -> x0, other arithmetic: 8.86 us -> none  [the longest x3 8.19 us: block_sum(): field.reshape(planes, rows // CB, CB, cols // CB, CB).sum(axis=(0, 2, 4))]
    reduce_sum x2 -> x0, local copies, waits for them, and re-layouts: 8.13 us -> none  [block_sum(): field.reshape(planes, rows // CB, CB, cols // CB, CB).sum(axis=(0, 2, 4))]
    select_n x5 -> x0, other arithmetic: 4.42 us -> none  [the longest x2 2.54 us: time_lift(): jnp.where(upper_bit == 0, (block + partner) * INV_ROOT, (partner - block)...]
    add x1 -> x0, local copies, waits for them, and re-layouts: 4.02 us -> none  [shards(): fixed = (second_pass + prolong(correction)[None])[None]]
  transfers between devices with their start and end apart: 10 -> 0, of which waited for: 10 -> 0; matrix products, arithmetic and copies ran while one was open for 0% -> 0% of each run, Pallas kernels for 0% -> 0%
where the time goes in v2:
time: 41.1 us; the launch traced here: 41 us
  Pallas kernels  39.3 us (96%)
  local copies, waits for them, and re-layouts  1.63 us (4%)
    pallas_call x1, Pallas kernels, shards(): pl.pallas_call(kernel, out_shape=jax.ShapeDtypeStruct(source.shape, F32),...  39.3 us
    unnamed x3, local copies, waits for them, and re-layouts  1.63 us

profile of v2, /device:TPU:1, one launch (start us, length us, event | category | flops | bytes accessed | tf_op | source)
XLA Modules:
  0.0 41.0 jit_solution(10478407437410918356)
XLA Ops:
  0.0 0.0 copy-start
  0.0 0.7 %copy-done = f32[4]{0:T(128)S(1)} copy-done((f32[4]{0:T(128)S(1)}, f32[4]{0:T(128)}, u32[]{:S(2)}) %copy-start) | copy-done | bytes 40
  0.7 39.3 %space_time_apply.1 = f32[1,4,256,256]{3,2,1,0:T(8,128)S(1)} custom-call(f32[4]{0:T(128)S(1)} %copy-done, f32[1,4,256,256]{3,2,1,0:T(8,128)} %source.1, f32[4,256,256]{2,1,0:T(8,128)} %potential.1), custom_call_target="tpu_custom_call" | custom-call | tf_op jit(solution)/shard_map/space_time_apply/pallas_call | solution.py:405
  40.0 1.0 %copy.5 = f32[1,4,256,256]{3,2,1,0:T(8,128)} copy(f32[1,4,256,256]{3,2,1,0:T(8,128)S(1)} %space_time_apply.1) | data formatting | bytes 2097152
Async XLA Ops:
  0.0 0.7 %copy-start = (f32[4]{0:T(128)S(1)}, f32[4]{0:T(128)}, u32[]{:S(2)}) copy-start(f32[4]{0:T(128)} %shift_hbm.1) | copy-start | bytes 52

commit v3 on v2

v3 whole, which is shorter than its diff:
```python
import math

import jax
import jax.numpy as jnp
from jax import lax
from jax.experimental import pallas as pl
from jax.experimental.pallas import tpu as pltpu
from jax.sharding import PartitionSpec as P

F32 = jnp.float32
MESH = pl.DeviceIdType.MESH
ROOT = 1.0 / math.sqrt(2.0)
OMEGA = 0.8
PLANES = (0, 3, 1, 2)
SLOT = {plane: slot for slot, plane in enumerate(PLANES)}


def dot(a, b):
    return jnp.dot(a, b, precision=lax.Precision.HIGHEST, preferred_element_type=F32)


def iota(shape, dim):
    return lax.broadcasted_iota(jnp.int32, shape, dim)


def ones_where(mask):
    return jnp.where(mask, 1.0, 0.0).astype(F32)


def beside_yz(ext):
    rows = ext.shape[0] - 16
    mid = ext[8 : 8 + rows]
    up = pltpu.roll(ext, 1, 0)[8 : 8 + rows]
    down = pltpu.roll(ext, rows + 15, 0)[8 : 8 + rows]
    col = iota(mid.shape, 1)
    left = jnp.where(col == 0, 0.0, pltpu.roll(mid, 1, 1))
    right = jnp.where(col == 255, 0.0, pltpu.roll(mid, 255, 1))
    return mid, (up + down) + (left + right)


def kernel(
    shift_hbm, source, potential, out, fix_out,
    shift_ref, own, other, pot, pot_other, s_buf, rd, fd, sd, strip, nb, nstrip, u_buf, fv, rv, sv, ustrip, nu, nustrip, fu, ru,
    hd, hv, hu, ub, ub_own, give, bk, gives, t_d, x_d, t_uv, x_uv, pot_all, d_sums, d_x, d_total, d_other, uv_sums, uv_x, uv_total,
    tr, blocks, pick, pick_d, fix_all, mine, yours,
    h_sem, l_sem, p_sem, q_sem, f_sem, s0, r0, s1, r1, s2, r2, st, rt, su, ru_sem, sx, rx, sp, rp, sdx, rdx, sdp, rdp, sc, rc, sg, rg,
    sb2, rb2, sb1, rb1, so, ro, lo,
):
    t, x = lax.axis_index("tm"), lax.axis_index("plane")
    e = t % 8
    k, c = e % 2, e // 2
    b, p = c % 2, c // 2
    partner = t + 1 - 2 * k
    near = t + 2 - 4 * b
    far = t + 4 - 8 * p
    x_peers = [(x + m) % 4 for m in (1, 2, 3)]
    group = [t - e + (e + m) % 8 for m in range(1, 8)]

    barrier = pltpu.get_barrier_semaphore()
    for peer in group:
        pl.semaphore_signal(barrier, inc=1, device_id=(peer, x), device_id_type=MESH)
    for peer in x_peers:
        pl.semaphore_signal(barrier, inc=1, device_id=(t, peer), device_id_type=MESH)

    def rows(start, count):
        return pl.ds(pl.multiple_of(start, 8), count)

    def remote(src, dst, send, recv, where):
        copy = pltpu.make_async_remote_copy(
            src_ref=src, dst_ref=dst, send_sem=send, recv_sem=recv, device_id=where, device_id_type=MESH
        )
        copy.start()
        return copy

    def local(src, dst, sem):
        copy = pltpu.make_async_copy(src, dst, sem)
        copy.start()
        return copy

    loads = [
        local(source.at[0, plane, rows(120 * k, 136), :], own.at[slot, rows(8 - 8 * k, 136), :], l_sem.at[slot])
        for slot, plane in enumerate(PLANES)
    ]
    shift_load = local(shift_hbm, shift_ref, h_sem)
    pot_loads = [
        local(potential.at[plane, rows(120 * k, 136), :], pot.at[slot, rows(8 - 8 * k, 136), :], p_sem.at[slot])
        for slot, plane in enumerate(PLANES)
    ]
    rest_load = local(potential.at[:, rows(128 - 128 * k, 128), :], pot_other, q_sem)
    for slot in range(4):
        for ref in (own, other, pot):
            ref[slot, rows(136 * k, 8), :] = jnp.zeros((8, 256), F32)

    pl.semaphore_wait(barrier, 10)

    swaps = [
        remote(
            source.at[0, plane, rows(120 - 120 * k, 136), :], other.at[slot, rows(8 * k, 136), :],
            s0.at[slot], r0.at[slot], (partner, x),
        )
        for slot, plane in enumerate(PLANES)
    ]

    def to_near(index, q, slots, start=0, count=32):
        at = 32 * q + start
        return remote(
            s_buf.at[slots, rows(72 - 64 * b + at, count), :], nb.at[slots, rows(at, count), :],
            s1.at[index], r1.at[index], (near, x),
        )

    firsts = {}
    for slot in range(4):
        loads[slot].wait()
        swaps[slot].wait_recv()
        s_buf[slot] = (own[slot] + other[slot]) * ROOT
        if slot < 2:
            firsts[slot] = to_near(slot, 1 - p, slot)
        if slot == 1:
            firsts[4] = to_near(4, p, 0)
            firsts[5] = to_near(5, p, 1)
    for h in range(2):
        for i in range(4):
            for at, row in ((0, 7), (4, 40), (8, 39), (12, 72)):
                strip[h, at + i : at + i + 1, :] = s_buf[i, row + 64 * h : row + 64 * h + 1, :]
    strip_1 = remote(strip.at[1 - b], nstrip, st, rt, (near, x))

    sign = (1 - 2 * k).astype(F32)
    near_sign = (1 - 2 * b).astype(F32)
    far_sign = (1 - 2 * p).astype(F32)
    scale = ROOT * sign
    keep_low, keep_high = ones_where(x > 0), ones_where(x < 3)
    edge_low, edge_high = 1.0 - keep_low, 1.0 - keep_high
    shift_load.wait()
    shift_0 = shift_ref[0]
    for slot in range(4):
        pot_loads[slot].wait()
        rd[slot] = OMEGA / (6.0 + pot[slot] + shift_0)
        fd[slot] = (own[slot] - other[slot]) * scale * rd[slot]
    below, above = (t, (x + 3) % 4), (t, (x + 1) % 4)
    halo_d = [
        remote(fd.at[0, 8:136, :], hd.at[1], sx.at[0], rx.at[0], below),
        remote(fd.at[1, 8:136, :], hd.at[0], sx.at[1], rx.at[1], above),
    ]

    for slot in range(4):
        rv[slot] = OMEGA / (6.0 + pot[slot, rows(64 * b, 80), :] + shift_ref[1])
        here = 6.0 + pot[slot, rows(64 * b + 32 * p, 48), :]
        ru[0, slot] = OMEGA / (here + shift_ref[3])
        ru[1, slot] = OMEGA / (here + shift_ref[2])

    z_at, z_block = iota((256, 128), 0), iota((256, 128), 1)
    lane_block = ones_where(z_at // 8 == z_block % 32)
    row, col = iota((32, 128), 0), iota((32, 128), 1)
    rest_load.wait()
    pot_sum = (pot[0, 8:136, :] + pot[1, 8:136, :]) + (pot[2, 8:136, :] + pot[3, 8:136, :])
    pot_rest = (pot_other[0] + pot_other[1]) + (pot_other[2] + pot_other[3])
    pot_all[0] = dot(ones_where(col // 8 + 16 * k == row), dot(pot_sum, lane_block)) + dot(
        ones_where(col // 8 + 16 - 16 * k == row), dot(pot_rest, lane_block)
    )
    pots = [
        remote(pot_all.at[0], pot_all.at[m + 1], sp.at[m], rp.at[m], (t, peer)) for m, peer in enumerate(x_peers)
    ]
    block = ones_where(z_at // 8 == z_block)
    around = ones_where((z_at + 7) // 8 == z_block + 1) + ones_where((z_at + 1) // 8 == z_block)
    blocks[0] = block
    blocks[1] = jnp.where(z_block < 32, 2.0 * block + around, 0.0)

    row, col = iota((32, 64), 0), iota((32, 64), 1)
    sender, r = col // 8, col % 8
    sender_c = sender // 2
    sender_b, sender_p = sender_c % 2, sender_c // 2
    sender_at = 16 * (sender % 2) + 8 * sender_b - 1 + r
    pick[0] = ones_where((r < 6) & (sender_at + 4 * sender_p == row))
    pick[1] = ones_where((sender_p == p) & (sender_at == row))
    pick[2] = ones_where((sender_p == p) & (r < 2) & (sender_at + 8 == row))
    row, col = iota((32, 24), 0), iota((32, 24), 1)
    pick_d[0] = ones_where((col < 18) & (16 * k - 1 + col == row))
    pick_d[1] = ones_where((col < 18) & (16 * (1 - k) - 1 + col == row))

    def level_1(slot, q, start=0, count=32):
        inside = 32 * q + start
        here = s_buf[slot, rows(8 + 64 * b + inside, count), :]
        there = nb[slot, rows(inside, count), :]
        at = rows(8 + inside, count)
        u_buf[slot, at, :] = (here + there) * ROOT
        detail = (here - there) * (ROOT * near_sign)
        fv[slot, at, :] = detail * rv[slot, at, :]
        at = rows(inside, count)
        x_uv[at, :] = detail if slot == 0 else x_uv[at, :] + detail

    seconds = {}

    def to_far(index, slots, start=0, count=32):
        seconds[index] = remote(
            u_buf.at[slots, rows(40 - 32 * p + start, count), :], nu.at[slots, start : start + count, :],
            s2.at[index], r2.at[index], (far, x),
        )

    def level_2(slot, start=0, count=32):
        here = u_buf[slot, rows(8 + 32 * p + start, count), :]
        there = nu[slot, start : start + count, :]
        at = slice(8 + start, 8 + start + count)
        low, high = (here + there) * ROOT, (here - there) * (ROOT * far_sign)
        fu[0, slot, at, :] = low * ru[0, slot, at, :]
        fu[1, slot, at, :] = high * ru[1, slot, at, :]
        for base, field in ((64, low), (96, high)):
            at = slice(base + start, base + start + count)
            x_uv[at, :] = field if slot == 0 else x_uv[at, :] + field

    firsts[0].wait_recv()
    level_1(0, 1 - p)
    to_far(0, 0)
    firsts[2] = to_near(2, 1 - p, 2, 0, 24)
    firsts[1].wait_recv()
    level_1(1, 1 - p)
    to_far(1, 1)
    firsts[3] = to_near(3, 1 - p, 3, 0, 24)
    firsts[6] = to_near(6, p, 2, 0, 24)
    firsts[7] = to_near(7, p, 3, 0, 24)
    strip_1.wait_recv()
    ustrip[...] = (strip[b] + nstrip[...]) * ROOT
    strip_2 = remote(ustrip.at[rows(8 - 8 * p, 8), :], nustrip, su, ru_sem, (far, x))
    details = (strip[b] - nstrip[...]) * (ROOT * near_sign)
    for slot in range(4):
        fv[slot, 7:8, :] = details[slot : slot + 1] * rv[slot, 7:8, :]
        fv[slot, 72:73, :] = details[12 + slot : 13 + slot] * rv[slot, 72:73, :]
        if slot > 1:
            fv[slot, 39:40, :] = details[8 + slot : 9 + slot] * rv[slot, 39:40, :]
    for slot in (0, 1):
        firsts[4 + slot].wait_recv()
        level_1(slot, p)
    halo_v = [
        remote(fv.at[0, 8:72, :], hv.at[1], sx.at[2], rx.at[2], below),
        remote(fv.at[1, 8:72, :], hv.at[0], sx.at[3], rx.at[3], above),
    ]
    inner_planes = slice(2, 4)
    for slot in (2, 3):
        firsts[slot].wait_recv()
        level_1(slot, 1 - p, 0, 24)
        to_far(slot, slot, 0, 24)
        firsts[6 + slot] = to_near(6 + slot, 1 - p if slot == 2 else p, inner_planes, 24, 8)
    for slot in (0, 1):
        seconds[slot].wait_recv()
        level_2(slot)
    halo_u = [
        remote(fu.at[:, 0, 8:40, :], hu.at[1], sx.at[4], rx.at[4], below),
        remote(fu.at[:, 1, 8:40, :], hu.at[0], sx.at[5], rx.at[5], above),
    ]

    def second_pass(f, weight, low_rim, high_rim, at, count, order, done):
        center = rows(at + 8, count)
        total, outer = None, None
        for plane in order:
            slot = SLOT[plane]
            mid, beside = beside_yz(f[slot, rows(at, count + 16), :])
            low = f[SLOT[plane - 1], center, :] if plane > 0 else low_rim() * keep_low
            high = f[SLOT[plane + 1], center, :] if plane < 3 else high_rim() * keep_high
            second = 1.2 * mid + weight[slot, center, :] * (beside + (low + high))
            done(slot, second)
            q = second - OMEGA * mid
            total = q if total is None else total + q
            if plane in (0, 3):
                rim = q * (edge_low if plane == 0 else edge_high)
                outer = rim if outer is None else outer + rim
        return total, outer

    for copy in halo_d:
        copy.wait_recv()

    def odd_rows(step, _):
        at = 32 * step
        here = rows(at, 32)

        def done(slot, second):
            sd[slot, here, :] = second

        summed, outer = second_pass(
            fd, rd, lambda: hd[0, here, :], lambda: hd[1, here, :], at, 32, range(4), done
        )
        center = rows(at + 8, 32)
        waves = (own[0, center, :] - other[0, center, :]) + (own[1, center, :] - other[1, center, :])
        waves = waves + (own[2, center, :] - other[2, center, :]) + (own[3, center, :] - other[3, center, :])
        t_d[here, :] = summed
        x_d[here, :] = (0.04 * scale) * waves - outer
        return 0

    lax.fori_loop(0, 4, odd_rows, 0)
    for slot in (2, 3):
        firsts[4 + slot].wait_recv()
        level_1(slot, p, 0, 24)
    firsts[8].wait_recv()
    for slot in (2, 3):
        level_1(slot, 1 - p, 24, 8)
    to_far(4, inner_planes, 24, 8)

    def near_rows(half):
        def body(step, _):
            at = 32 * step + 16 * half
            here = rows(at, 16)

            def done(slot, second):
                sv[slot, here, :] = second

            summed, outer = second_pass(
                fv, rv, lambda: hv[0, here, :], lambda: hv[1, here, :], at, 16, range(4), done
            )
            t_uv[here, :] = summed
            x_uv[here, :] = 0.04 * x_uv[here, :] - outer
            return 0

        lax.fori_loop(0, 2, body, 0)

    for copy in halo_v:
        copy.wait_recv()
    near_rows(0)

    strip_2.wait_recv()
    here = ustrip[rows(8 * p, 8), :]
    low, high = (here + nustrip[...]) * ROOT, (here - nustrip[...]) * (ROOT * far_sign)
    for slot in range(4):
        for j, rim in enumerate((low, high)):
            fu[j, slot, 7:8, :] = rim[slot : slot + 1] * ru[j, slot, 7:8, :]
            fu[j, slot, 40:41, :] = rim[4 + slot : 5 + slot] * ru[j, slot, 40:41, :]
    for slot in (2, 3):
        seconds[slot].wait_recv()
        level_2(slot, 0, 24)

    backs_1, backs_2 = {}, {}

    def far_rows(half, planes):
        here = slice(16 * half, 16 * half + 16)
        for plane in planes:
            made = []
            for j in range(2):
                at = slice(64 + 32 * j + 16 * half, 80 + 32 * j + 16 * half)
                summed, outer = second_pass(
                    fu.at[j], ru.at[j], lambda: hu[0, j, here, :], lambda: hu[1, j, here, :], 16 * half, 16, (plane,),
                    lambda slot, second: made.append(second),
                )
                t_uv[at, :] = summed if plane == 1 else t_uv[at, :] + summed
                if plane == 1:
                    x_uv[at, :] = 0.04 * x_uv[at, :]
                if outer is not None:
                    x_uv[at, :] = x_uv[at, :] - outer
            low, high = made[0] * ROOT, made[1] * (ROOT * far_sign)
            give[SLOT[plane], here, :] = low - high
            ub_own[SLOT[plane], here, :] = low + high
        pair = SLOT[planes[0]] // 2
        slots, index = slice(2 * pair, 2 * pair + 2), 2 * half + pair
        backs_2[index] = remote(
            give.at[slots, here, :], ub.at[slots, here, :], sb2.at[index], rb2.at[index], (far, x)
        )

    def join(half, pair, q, ref, index):
        at = 32 * q + 16 * half
        slots = slice(2 * pair, 2 * pair + 2)
        for slot in (2 * pair, 2 * pair + 1):
            low = ref[slot, 16 * half : 16 * half + 16, :] * ROOT
            high = sv[slot, rows(at, 16), :] * (ROOT * near_sign)
            gives[slot, rows(at, 16), :] = low - high
            bk[slot, rows(64 * b + at, 16), :] = low + high
        backs_1[index] = remote(
            gives.at[slots, rows(at, 16), :], bk.at[slots, rows(64 * b + at, 16), :],
            sb1.at[index], rb1.at[index], (near, x),
        )

    def own_part(half):
        for pair in (1, 0):
            join(half, pair, p, ub_own, 2 * half + pair)

    def rest(half, pair):
        index = 2 * half + pair
        backs_2[index].wait_recv()
        join(half, pair, 1 - p, ub, 4 + index)

    far_rows(0, (1, 2))
    for copy in halo_u:
        copy.wait_recv()
    far_rows(0, (0, 3))
    own_part(0)
    firsts[9].wait_recv()
    for slot in (2, 3):
        level_1(slot, p, 24, 8)
    near_rows(1)
    seconds[4].wait_recv()
    for slot in (2, 3):
        level_2(slot, 24, 8)
    far_rows(1, (1, 2))
    far_rows(1, (0, 3))

    y_at, y_row = iota((32, 128), 1), iota((32, 128), 0)
    start = jnp.where(y_at < 64, 0, 16 + 8 * ((y_at - 64) // 32))
    y_in = jnp.where(y_at < 64, y_at, y_at % 32)
    inner = ones_where(start + y_in // 8 + 1 == y_row)
    beside = ones_where(start + (y_in + 7) // 8 == y_row) + ones_where(start + (y_in + 1) // 8 + 1 == y_row)
    sums = dot(inner, dot(x_uv[...], blocks[0]) + dot(t_uv[...], blocks[1])) + dot(beside, dot(t_uv[...], blocks[0]))
    uv_sums[...] = (sums[16:24] + pltpu.roll(sums[24:32], 32, 1)) + (
        pltpu.roll(sums[0:8], 64, 1) + pltpu.roll(sums[8:16], 96, 1)
    )
    uv_reduces = [
        remote(uv_sums, uv_x.at[m], sc.at[m], rc.at[m], (t, peer)) for m, peer in enumerate(x_peers)
    ]
    own_part(1)
    y_at, y_row = iota((24, 128), 1), iota((24, 128), 0)
    inner = ones_where(y_at // 8 + 1 == y_row)
    beside = ones_where((y_at + 7) // 8 == y_row) + ones_where((y_at + 1) // 8 + 1 == y_row)
    sums = dot(inner, dot(x_d[...], blocks[0]) + dot(t_d[...], blocks[1])) + dot(beside, dot(t_d[...], blocks[0]))
    d_sums[...] = pltpu.roll(sums, 96, 1)
    d_reduces = [
        remote(d_sums, d_x.at[m], sdx.at[m], rdx.at[m], (t, peer)) for m, peer in enumerate(x_peers)
    ]

    for copy in uv_reduces:
        copy.wait_recv()
    uv_total[...] = (uv_sums[...] + uv_x[0]) + (uv_x[1] + uv_x[2])
    gathers = [
        remote(uv_total, tr.at[e], sg.at[m], rg.at[m], (peer, x)) for m, peer in enumerate(group)
    ]
    tr[e] = uv_total[...]
    rest(0, 1)
    rest(0, 0)
    for copy in d_reduces + pots:
        copy.wait_recv()
    d_total[...] = (d_sums[...] + d_x[0]) + (d_x[1] + d_x[2])
    d_swap = remote(d_total, d_other, sdp, rdp, (partner, x))

    sends, stores = [], []

    def finish(slot, start, index):
        here = rows(start, 64)
        even, odd = bk[slot, here, :], sd[slot, here, :] * sign
        yours[slot, here, :] = (even - odd) * ROOT
        there = out.at[0, PLANES[slot], rows(128 * k + start, 64), :]
        sends.append(remote(yours.at[slot, here, :], there, so.at[index], ro.at[index], (partner, x)))
        mine[slot, here, :] = (even + odd) * ROOT
        stores.append(local(mine.at[slot, here, :], there, lo.at[index]))

    for pair in (1, 0):
        rest(1, pair)
        for slot in (2 * pair, 2 * pair + 1):
            finish(slot, 64 * b, slot)

    def finish_pair(pair):
        for index in (pair, 2 + pair, 4 + pair, 6 + pair):
            backs_1[index].wait_recv()
        for slot in (2 * pair, 2 * pair + 1):
            finish(slot, 64 - 64 * b, 4 + slot)

    finish_pair(1)
    for copy in gathers:
        copy.wait_recv()
    d_swap.wait_recv()

    lane = iota((32, 128), 1)
    coef = lane // 32
    sent = tr[...].reshape(64, 128)
    rem_v = dot(pick[1], sent) + pltpu.roll(dot(pick[2], sent), 96, 1)
    rem_d = dot(pick_d[0], d_total[...]) + dot(pick_d[1], d_other[...])
    rem = jnp.where(coef < 2, dot(pick[0], sent), jnp.where(coef == 2, rem_v, rem_d))
    shift = jnp.where(
        coef == 0, shift_ref[3], jnp.where(coef == 1, shift_ref[2], jnp.where(coef == 2, shift_ref[1], shift_0))
    )
    coarse_pot = (pot_all[0] + pot_all[1]) + (pot_all[2] + pot_all[3])
    diag = coarse_pot + shift * 1024.0 + 640.0
    one = rem / diag
    row = iota((32, 128), 0)
    up = jnp.where(row == 0, 0.0, pltpu.roll(one, 1, 0))
    down = jnp.where(row == 31, 0.0, pltpu.roll(one, 31, 0))
    left = jnp.where(lane % 32 == 0, 0.0, pltpu.roll(one, 1, 1))
    right = jnp.where(lane % 32 == 31, 0.0, pltpu.roll(one, 127, 1))
    applied = diag * one - 128.0 * ((up + down) + (left + right))
    fix = one + (rem - applied) / diag
    weight = jnp.where(
        coef == 0, 0.5 * ROOT, jnp.where(coef == 1, 0.5 * ROOT * far_sign, jnp.where(coef == 2, 0.5 * near_sign, scale))
    )
    widen = ones_where(iota((128, 256), 0) % 32 == iota((128, 256), 1) // 8)
    wide = dot(fix * weight, widen)
    for i in range(32):
        fix_all[8 * i : 8 * i + 8, :] = jnp.broadcast_to(wide[i : i + 1], (8, 256))
    stores.append(local(fix_all, fix_out, f_sem))
    finish_pair(0)

    sent_all = swaps + list(firsts.values()) + list(seconds.values()) + [strip_1, strip_2, d_swap] + halo_d + halo_v + halo_u + pots
    for copy in sent_all + d_reduces + uv_reduces + gathers + list(backs_2.values()) + list(backs_1.values()):
        copy.wait_send()
    for copy in sends + stores:
        copy.wait()


def shards(source, potential, level_shift):
    dma = pltpu.SemaphoreType.DMA
    vmem = lambda *shape: pltpu.VMEM(shape, F32)
    scratch = dict(
        shift_ref=pltpu.SMEM((4,), F32),
        own=vmem(4, 144, 256), other=vmem(4, 144, 256), pot=vmem(4, 144, 256), pot_other=vmem(4, 128, 256), s_buf=vmem(4, 144, 256),
        rd=vmem(4, 144, 256), fd=vmem(4, 144, 256), sd=vmem(4, 128, 256), strip=vmem(2, 16, 256),
        nb=vmem(4, 64, 256), nstrip=vmem(16, 256), u_buf=vmem(4, 80, 256), fv=vmem(4, 80, 256), rv=vmem(4, 80, 256),
        sv=vmem(4, 64, 256), ustrip=vmem(16, 256), nu=vmem(4, 32, 256), nustrip=vmem(8, 256),
        fu=vmem(2, 4, 48, 256), ru=vmem(2, 4, 48, 256),
        hd=vmem(2, 128, 256), hv=vmem(2, 64, 256), hu=vmem(2, 2, 32, 256),
        ub=vmem(4, 32, 256), ub_own=vmem(4, 32, 256), give=vmem(4, 32, 256), bk=vmem(4, 128, 256), gives=vmem(4, 64, 256),
        t_d=vmem(128, 256), x_d=vmem(128, 256), t_uv=vmem(128, 256), x_uv=vmem(128, 256),
        pot_all=vmem(4, 32, 128), d_sums=vmem(24, 128), d_x=vmem(3, 24, 128), d_total=vmem(24, 128),
        d_other=vmem(24, 128), uv_sums=vmem(8, 128), uv_x=vmem(3, 8, 128), uv_total=vmem(8, 128),
        tr=vmem(8, 8, 128), blocks=vmem(2, 256, 128), pick=vmem(3, 32, 64), pick_d=vmem(2, 32, 24),
        fix_all=vmem(256, 256), mine=vmem(4, 128, 256), yours=vmem(4, 128, 256),
        h_sem=dma(()), l_sem=dma((4,)), p_sem=dma((4,)), q_sem=dma(()), f_sem=dma(()), s0=dma((4,)), r0=dma((4,)), s1=dma((10,)), r1=dma((10,)),
        s2=dma((5,)), r2=dma((5,)), st=dma(()), rt=dma(()), su=dma(()), ru_sem=dma(()), sx=dma((6,)), rx=dma((6,)),
        sp=dma((3,)), rp=dma((3,)), sdx=dma((3,)), rdx=dma((3,)), sdp=dma(()), rdp=dma(()), sc=dma((3,)), rc=dma((3,)),
        sg=dma((7,)), rg=dma((7,)), sb2=dma((4,)), rb2=dma((4,)), sb1=dma((8,)), rb1=dma((8,)),
        so=dma((8,)), ro=dma((8,)), lo=dma((8,)),
    )
    raw, fix = pl.pallas_call(
        kernel,
        out_shape=(jax.ShapeDtypeStruct(source.shape, F32), jax.ShapeDtypeStruct(source.shape[2:], F32)),
        in_specs=[
            pl.BlockSpec(memory_space=pltpu.HBM),
            pl.BlockSpec(memory_space=pltpu.HBM),
            pl.BlockSpec(memory_space=pltpu.HBM),
        ],
        out_specs=(pl.BlockSpec(memory_space=pl.ANY), pl.BlockSpec(memory_space=pl.ANY)),
        scratch_shapes=list(scratch.values()),
        compiler_params=pltpu.CompilerParams(
            collective_id=0, has_side_effects=True, vmem_limit_bytes=105 * 2**19
        ),
        name="space_time_apply",
    )(level_shift, source, potential)
    return raw + fix[None, None]


def solution(mesh):
    in_specs = (P("tm", "plane", None, None), P("plane", None, None), P())
    out_specs = P("tm", "plane", None, None)
    return jax.shard_map(shards, mesh=mesh, in_specs=in_specs, out_specs=out_specs, check_vma=False)
```

time: 41.1 us -> 37.5 us (0.912)
  Pallas kernels: 39.3 us -> 35.7 us
  other arithmetic: 0 us -> 1.06 us
  local copies, waits for them, and re-layouts: 1.63 us -> 0.65 us
    pallas_call x1, Pallas kernels: 39.3 us -> 35.7 us  [shards(): pl.pallas_call(kernel, out_shape=(jax.ShapeDtypeStruct(source.shape, F32)...]
    add x0 -> x1, other arithmetic: none -> 1.06 us  [shards(): return raw + fix[None, None]]
    unnamed x3 -> x2, local copies, waits for them, and re-layouts: 1.63 us -> 0.65 us
where the time goes in v3:
time: 37.5 us; the launch traced here: 37.4 us
  Pallas kernels  35.7 us (95%)
  other arithmetic  1.06 us (3%)
  local copies, waits for them, and re-layouts  0.65 us (2%)
    pallas_call x1, Pallas kernels, shards(): pl.pallas_call(kernel, out_shape=(jax.ShapeDtypeStruct(source.shape, F32)...  35.7 us
    add x1, other arithmetic, shards(): return raw + fix[None, None]  1.06 us

profile of v3, /device:TPU:1, one launch (start us, length us, event | category | flops | bytes accessed | tf_op | source)
XLA Modules:
  0.0 37.4 jit_solution(3112237527697609509)
XLA Ops:
  0.0 0.0 copy-start
  0.0 0.7 %copy-done = f32[4]{0:T(128)S(1)} copy-done((f32[4]{0:T(128)S(1)}, f32[4]{0:T(128)}, u32[]{:S(2)}) %copy-start) | copy-done | bytes 40
  0.7 35.7 %space_time_apply.1 = (f32[1,4,256,256]{3,2,1,0:T(8,128)S(1)}, f32[256,256]{1,0:T(8,128)S(1)}) custom-call(f32[4]{0:T(128)S(1)} %copy-done, f32[1,4,256,256]{3,2,1,0:T(8,128)} %source.1, f32[4,256,256]{2,1,0:T(8,128)} %potential.1), custom_call_target="tpu_custom_call" | custom-call | tf_op jit(solution)/shard_map/space_time_apply/pallas_call | solution.py:513
  36.3 1.1 %broadcast_add_fusion = f32[1,4,256,256]{3,2,1,0:T(8,128)} fusion(f32[1,4,256,256]{3,2,1,0:T(8,128)S(1)} %get-tuple-element.7, f32[256,256]{1,0:T(8,128)S(1)} %get-tuple-element.8), kind=kLoop, calls=%fused_computation | loop fusion | flops 262144 | bytes 2359296 | tf_op jit(solution)/shard_map/add | solution.py:528
Async XLA Ops:
  0.0 0.7 %copy-start = (f32[4]{0:T(128)S(1)}, f32[4]{0:T(128)}, u32[]{:S(2)}) copy-start(f32[4]{0:T(128)} %shift_hbm.1) | copy-start | bytes 52

commit v4 on v3

v4 whole, which is shorter than its diff:
```python
import math

import jax
import jax.numpy as jnp
from jax import lax
from jax.experimental import pallas as pl
from jax.experimental.pallas import tpu as pltpu
from jax.sharding import PartitionSpec as P

F32 = jnp.float32
MESH = pl.DeviceIdType.MESH
ROOT = 1.0 / math.sqrt(2.0)
OMEGA = 0.8
PLANES = (0, 3, 1, 2)
SLOT = {plane: slot for slot, plane in enumerate(PLANES)}


def dot(a, b):
    return jnp.dot(a, b, precision=lax.Precision.HIGHEST, preferred_element_type=F32)


def iota(shape, dim):
    return lax.broadcasted_iota(jnp.int32, shape, dim)


def ones_where(mask):
    return jnp.where(mask, 1.0, 0.0).astype(F32)


def beside_yz(ext):
    rows = ext.shape[0] - 16
    mid = ext[8 : 8 + rows]
    up = pltpu.roll(ext, 1, 0)[8 : 8 + rows]
    down = pltpu.roll(ext, rows + 15, 0)[8 : 8 + rows]
    col = iota(mid.shape, 1)
    left = jnp.where(col == 0, 0.0, pltpu.roll(mid, 1, 1))
    right = jnp.where(col == 255, 0.0, pltpu.roll(mid, 255, 1))
    return mid, (up + down) + (left + right)


def kernel(
    shift_hbm, source, potential, out, fix_out,
    shift_ref, own, other, pot, pot_other, s_buf, rd, fd, sd, strip, nb, nstrip, u_buf, fv, rv, sv, ustrip, nu, nustrip, fu, ru,
    hd, hv, hu, ub, ub_own, give, bk, gives, t_d, x_d, t_uv, x_uv, pot_all, d_sums, d_x, d_total, d_other, uv_sums, uv_x, uv_total,
    tr, blocks, pick, pick_d, fix_all, mine, yours,
    all_sent, h_sem, l_sem, p_sem, q_sem, f_sem, sent, r0, r1, r2, rt, ru_sem, rx, rp, rdx, rdp, rc, rg, rb2, rb1, ro, lo,
):
    t, x = lax.axis_index("tm"), lax.axis_index("plane")
    e = t % 8
    k, c = e % 2, e // 2
    b, p = c % 2, c // 2
    partner = t + 1 - 2 * k
    near = t + 2 - 4 * b
    far = t + 4 - 8 * p
    x_peers = [(x + m) % 4 for m in (1, 2, 3)]
    group = [t - e + (e + m) % 8 for m in range(1, 8)]

    barrier = pltpu.get_barrier_semaphore()
    for peer in group:
        pl.semaphore_signal(barrier, inc=1, device_id=(peer, x), device_id_type=MESH)
    for peer in x_peers:
        pl.semaphore_signal(barrier, inc=1, device_id=(t, peer), device_id_type=MESH)

    def rows(start, count):
        return pl.ds(pl.multiple_of(start, 8), count)

    def remote(src, dst, recv, where):
        copy = pltpu.make_async_remote_copy(
            src_ref=src, dst_ref=dst, send_sem=sent, recv_sem=recv, device_id=where, device_id_type=MESH
        )
        copy.start()
        return copy

    def absorb(ref, sem):
        pltpu.make_async_copy(ref, ref, sem).wait()

    def local(src, dst, sem):
        copy = pltpu.make_async_copy(src, dst, sem)
        copy.start()
        return copy

    for slot, plane in enumerate(PLANES):
        local(source.at[0, plane, rows(120 * k, 136), :], own.at[slot, rows(8 - 8 * k, 136), :], l_sem)
    shift_load = local(shift_hbm, shift_ref, h_sem)
    for slot, plane in enumerate(PLANES):
        local(potential.at[plane, rows(120 * k, 136), :], pot.at[slot, rows(8 - 8 * k, 136), :], p_sem)
    rest_load = local(potential.at[:, rows(128 - 128 * k, 128), :], pot_other, q_sem)
    for slot in range(4):
        for ref in (own, other, pot):
            ref[slot, rows(136 * k, 8), :] = jnp.zeros((8, 256), F32)

    pl.semaphore_wait(barrier, 10)

    swaps = [
        remote(
            source.at[0, plane, rows(120 - 120 * k, 136), :], other.at[slot, rows(8 * k, 136), :],
            r0.at[slot], (partner, x),
        )
        for slot, plane in enumerate(PLANES)
    ]

    def to_near(index, slot, q):
        firsts[index] = remote(
            s_buf.at[slot, rows(72 - 64 * b + 32 * q, 32), :], nb.at[slot, rows(32 * q, 32), :],
            r1.at[index], (near, x),
        )

    firsts = {}
    absorb(own.at[:, 0:136, :], l_sem)
    for slot in range(4):
        swaps[slot].wait_recv()
        s_buf[slot] = (own[slot] + other[slot]) * ROOT
        if slot < 2:
            to_near(slot, slot, 1 - p)
        if slot == 1:
            to_near(4, 0, p)
            to_near(5, 1, p)
    for h in range(2):
        for i in range(4):
            for at, row in ((0, 7), (4, 40), (8, 39), (12, 72)):
                strip[h, at + i : at + i + 1, :] = s_buf[i, row + 64 * h : row + 64 * h + 1, :]

    sign = (1 - 2 * k).astype(F32)
    near_sign = (1 - 2 * b).astype(F32)
    far_sign = (1 - 2 * p).astype(F32)
    scale = ROOT * sign
    keep_low, keep_high = ones_where(x > 0), ones_where(x < 3)
    edge_low, edge_high = 1.0 - keep_low, 1.0 - keep_high
    shift_load.wait()
    shift_0 = shift_ref[0]
    absorb(pot.at[:, 0:136, :], p_sem)
    for slot in range(4):
        rd[slot] = OMEGA / (6.0 + pot[slot] + shift_0)
        fd[slot] = (own[slot] - other[slot]) * scale * rd[slot]
    below, above = (t, (x + 3) % 4), (t, (x + 1) % 4)
    remote(fd.at[0, 8:136, :], hd.at[1], rx.at[0], below)
    remote(fd.at[1, 8:136, :], hd.at[0], rx.at[0], above)

    for slot in range(4):
        rv[slot] = OMEGA / (6.0 + pot[slot, rows(64 * b, 80), :] + shift_ref[1])
        here = 6.0 + pot[slot, rows(64 * b + 32 * p, 48), :]
        ru[0, slot] = OMEGA / (here + shift_ref[3])
        ru[1, slot] = OMEGA / (here + shift_ref[2])

    z_at, z_block = iota((256, 128), 0), iota((256, 128), 1)
    lane_block = ones_where(z_at // 8 == z_block % 32)
    row, col = iota((32, 128), 0), iota((32, 128), 1)
    rest_load.wait()
    pot_sum = (pot[0, 8:136, :] + pot[1, 8:136, :]) + (pot[2, 8:136, :] + pot[3, 8:136, :])
    pot_rest = (pot_other[0] + pot_other[1]) + (pot_other[2] + pot_other[3])
    pot_all[0] = dot(ones_where(col // 8 + 16 * k == row), dot(pot_sum, lane_block)) + dot(
        ones_where(col // 8 + 16 - 16 * k == row), dot(pot_rest, lane_block)
    )
    for m, peer in enumerate(x_peers):
        remote(pot_all.at[0], pot_all.at[m + 1], rp, (t, peer))
    block = ones_where(z_at // 8 == z_block)
    around = ones_where((z_at + 7) // 8 == z_block + 1) + ones_where((z_at + 1) // 8 == z_block)
    blocks[0] = block
    blocks[1] = jnp.where(z_block < 32, 2.0 * block + around, 0.0)

    row, col = iota((32, 64), 0), iota((32, 64), 1)
    sender, r = col // 8, col % 8
    sender_c = sender // 2
    sender_b, sender_p = sender_c % 2, sender_c // 2
    sender_at = 16 * (sender % 2) + 8 * sender_b - 1 + r
    pick[0] = ones_where((r < 6) & (sender_at + 4 * sender_p == row))
    pick[1] = ones_where((sender_p == p) & (sender_at == row))
    pick[2] = ones_where((sender_p == p) & (r < 2) & (sender_at + 8 == row))
    row, col = iota((32, 24), 0), iota((32, 24), 1)
    pick_d[0] = ones_where((col < 18) & (16 * k - 1 + col == row))
    pick_d[1] = ones_where((col < 18) & (16 * (1 - k) - 1 + col == row))

    def level_1(slot, q):
        here = s_buf[slot, rows(8 + 64 * b + 32 * q, 32), :]
        there = nb[slot, rows(32 * q, 32), :]
        at = rows(8 + 32 * q, 32)
        u_buf[slot, at, :] = (here + there) * ROOT
        detail = (here - there) * (ROOT * near_sign)
        fv[slot, at, :] = detail * rv[slot, at, :]
        at = rows(32 * q, 32)
        x_uv[at, :] = detail if slot == 0 else x_uv[at, :] + detail

    seconds = {}

    def passed_on(slot):
        firsts[slot].wait_recv()
        level_1(slot, 1 - p)
        seconds[slot] = remote(
            u_buf.at[slot, rows(40 - 32 * p, 32), :], nu.at[slot], r2.at[slot], (far, x)
        )

    def level_2(slot):
        seconds[slot].wait_recv()
        here = u_buf[slot, rows(8 + 32 * p, 32), :]
        low, high = (here + nu[slot]) * ROOT, (here - nu[slot]) * (ROOT * far_sign)
        fu[0, slot, 8:40, :] = low * ru[0, slot, 8:40, :]
        fu[1, slot, 8:40, :] = high * ru[1, slot, 8:40, :]
        for at, field in ((64, low), (96, high)):
            x_uv[at : at + 32, :] = field if slot == 0 else x_uv[at : at + 32, :] + field

    passed_on(0)
    passed_on(1)
    to_near(2, 2, 1 - p)
    to_near(3, 3, 1 - p)
    strip_1 = remote(strip.at[1 - b], nstrip, rt, (near, x))
    to_near(6, 2, p)
    for slot in (0, 1):
        firsts[4 + slot].wait_recv()
        level_1(slot, p)
    remote(fv.at[0, 8:72, :], hv.at[1], rx.at[1], below)
    remote(fv.at[1, 8:72, :], hv.at[0], rx.at[1], above)
    passed_on(2)
    passed_on(3)
    to_near(7, 3, p)
    strip_1.wait_recv()
    ustrip[...] = (strip[b] + nstrip[...]) * ROOT
    strip_2 = remote(ustrip.at[rows(8 - 8 * p, 8), :], nustrip, ru_sem, (far, x))
    details = (strip[b] - nstrip[...]) * (ROOT * near_sign)
    for slot in range(4):
        fv[slot, 7:8, :] = details[slot : slot + 1] * rv[slot, 7:8, :]
        fv[slot, 72:73, :] = details[12 + slot : 13 + slot] * rv[slot, 72:73, :]
    level_2(0)
    level_2(1)
    remote(fu.at[:, 0, 8:40, :], hu.at[1], rx.at[2], below)
    remote(fu.at[:, 1, 8:40, :], hu.at[0], rx.at[2], above)

    def second_pass(f, weight, low_rim, high_rim, at, count, order, done):
        center = rows(at + 8, count)
        total, outer = None, None
        for plane in order:
            slot = SLOT[plane]
            mid, beside = beside_yz(f[slot, rows(at, count + 16), :])
            low = f[SLOT[plane - 1], center, :] if plane > 0 else low_rim() * keep_low
            high = f[SLOT[plane + 1], center, :] if plane < 3 else high_rim() * keep_high
            second = 1.2 * mid + weight[slot, center, :] * (beside + (low + high))
            done(slot, second)
            q = second - OMEGA * mid
            total = q if total is None else total + q
            if plane in (0, 3):
                rim = q * (edge_low if plane == 0 else edge_high)
                outer = rim if outer is None else outer + rim
        return total, outer

    absorb(hd, rx.at[0])

    def odd_rows(step, _):
        at = 32 * step
        here = rows(at, 32)

        def done(slot, second):
            sd[slot, here, :] = second

        summed, outer = second_pass(
            fd, rd, lambda: hd[0, here, :], lambda: hd[1, here, :], at, 32, range(4), done
        )
        center = rows(at + 8, 32)
        waves = (own[0, center, :] - other[0, center, :]) + (own[1, center, :] - other[1, center, :])
        waves = waves + (own[2, center, :] - other[2, center, :]) + (own[3, center, :] - other[3, center, :])
        t_d[here, :] = summed
        x_d[here, :] = (0.04 * scale) * waves - outer
        return 0

    lax.fori_loop(0, 4, odd_rows, 0)
    for slot in (2, 3):
        firsts[4 + slot].wait_recv()
        level_1(slot, p)

    def near_rows(step, _):
        at = 32 * step
        here = rows(at, 32)

        def done(slot, second):
            sv[slot, here, :] = second

        summed, outer = second_pass(
            fv, rv, lambda: hv[0, here, :], lambda: hv[1, here, :], at, 32, range(4), done
        )
        t_uv[here, :] = summed
        x_uv[here, :] = 0.04 * x_uv[here, :] - outer
        return 0

    absorb(hv, rx.at[1])
    lax.fori_loop(0, 2, near_rows, 0)

    strip_2.wait_recv()
    here = ustrip[rows(8 * p, 8), :]
    low, high = (here + nustrip[...]) * ROOT, (here - nustrip[...]) * (ROOT * far_sign)
    for slot in range(4):
        for j, rim in enumerate((low, high)):
            fu[j, slot, 7:8, :] = rim[slot : slot + 1] * ru[j, slot, 7:8, :]
            fu[j, slot, 40:41, :] = rim[4 + slot : 5 + slot] * ru[j, slot, 40:41, :]
    level_2(2)
    level_2(3)

    backs_2 = {}

    def far_rows(plane):
        made = []
        for j, at in ((0, slice(64, 96)), (1, slice(96, 128))):
            summed, outer = second_pass(
                fu.at[j], ru.at[j], lambda: hu[0, j], lambda: hu[1, j], 0, 32, (plane,),
                lambda slot, second: made.append(second),
            )
            t_uv[at, :] = summed if plane == 1 else t_uv[at, :] + summed
            if plane == 1:
                x_uv[at, :] = 0.04 * x_uv[at, :]
            if outer is not None:
                x_uv[at, :] = x_uv[at, :] - outer
        slot = SLOT[plane]
        low, high = made[0] * ROOT, made[1] * (ROOT * far_sign)
        give[slot] = low - high
        ub_own[slot] = low + high
        backs_2[slot] = remote(give.at[slot], ub.at[slot], rb2.at[slot], (far, x))

    def join(slot, q, ref):
        low, high = ref[slot] * ROOT, sv[slot, rows(32 * q, 32), :] * (ROOT * near_sign)
        gives[slot, rows(32 * q, 32), :] = low - high
        bk[slot, rows(64 * b + 32 * q, 32), :] = low + high
        remote(
            gives.at[slot, rows(32 * q, 32), :], bk.at[slot, rows(64 * b + 32 * q, 32), :],
            rb1.at[slot], (near, x),
        )

    def rest(slot):
        backs_2[slot].wait_recv()
        join(slot, 1 - p, ub)

    far_rows(1)
    far_rows(2)
    absorb(hu, rx.at[2])
    far_rows(0)
    far_rows(3)

    y_at, y_row = iota((32, 128), 1), iota((32, 128), 0)
    start = jnp.where(y_at < 64, 0, 16 + 8 * ((y_at - 64) // 32))
    y_in = jnp.where(y_at < 64, y_at, y_at % 32)
    inner = ones_where(start + y_in // 8 + 1 == y_row)
    beside = ones_where(start + (y_in + 7) // 8 == y_row) + ones_where(start + (y_in + 1) // 8 + 1 == y_row)
    sums = dot(inner, dot(x_uv[...], blocks[0]) + dot(t_uv[...], blocks[1])) + dot(beside, dot(t_uv[...], blocks[0]))
    uv_sums[...] = (sums[16:24] + pltpu.roll(sums[24:32], 32, 1)) + (
        pltpu.roll(sums[0:8], 64, 1) + pltpu.roll(sums[8:16], 96, 1)
    )
    for m, peer in enumerate(x_peers):
        remote(uv_sums, uv_x.at[m], rc, (t, peer))
    for slot in (2, 3, 0, 1):
        join(slot, p, ub_own)
    y_at, y_row = iota((24, 128), 1), iota((24, 128), 0)
    inner = ones_where(y_at // 8 + 1 == y_row)
    beside = ones_where((y_at + 7) // 8 == y_row) + ones_where((y_at + 1) // 8 + 1 == y_row)
    sums = dot(inner, dot(x_d[...], blocks[0]) + dot(t_d[...], blocks[1])) + dot(beside, dot(t_d[...], blocks[0]))
    d_sums[...] = pltpu.roll(sums, 96, 1)
    for m, peer in enumerate(x_peers):
        remote(d_sums, d_x.at[m], rdx, (t, peer))

    absorb(uv_x, rc)
    uv_total[...] = (uv_sums[...] + uv_x[0]) + (uv_x[1] + uv_x[2])
    for peer in group:
        remote(uv_total, tr.at[e], rg, (peer, x))
    tr[e] = uv_total[...]
    rest(2)
    rest(3)
    absorb(d_x, rdx)
    absorb(pot_all.at[1:4], rp)
    d_total[...] = (d_sums[...] + d_x[0]) + (d_x[1] + d_x[2])
    d_swap = remote(d_total, d_other, rdp, (partner, x))

    def finish(slot, start):
        here = rows(start, 64)
        even, odd = bk[slot, here, :], sd[slot, here, :] * sign
        yours[slot, here, :] = (even - odd) * ROOT
        there = out.at[0, PLANES[slot], rows(128 * k + start, 64), :]
        remote(yours.at[slot, here, :], there, ro, (partner, x))
        mine[slot, here, :] = (even + odd) * ROOT
        local(mine.at[slot, here, :], there, lo)

    rest(0)
    rest(1)
    for slot in (2, 3, 0, 1):
        finish(slot, 64 * b)

    def finish_far(slot):
        absorb(gives.at[slot], rb1.at[slot])
        finish(slot, 64 - 64 * b)

    for slot in (2, 3, 0, 1):
        finish_far(slot)
    absorb(tr.at[0:7], rg)
    d_swap.wait_recv()

    lane = iota((32, 128), 1)
    coef = lane // 32
    gathered = tr[...].reshape(64, 128)
    rem_v = dot(pick[1], gathered) + pltpu.roll(dot(pick[2], gathered), 96, 1)
    rem_d = dot(pick_d[0], d_total[...]) + dot(pick_d[1], d_other[...])
    rem = jnp.where(coef < 2, dot(pick[0], gathered), jnp.where(coef == 2, rem_v, rem_d))
    shift = jnp.where(
        coef == 0, shift_ref[3], jnp.where(coef == 1, shift_ref[2], jnp.where(coef == 2, shift_ref[1], shift_0))
    )
    coarse_pot = (pot_all[0] + pot_all[1]) + (pot_all[2] + pot_all[3])
    diag = coarse_pot + shift * 1024.0 + 640.0
    one = rem / diag
    row = iota((32, 128), 0)
    up = jnp.where(row == 0, 0.0, pltpu.roll(one, 1, 0))
    down = jnp.where(row == 31, 0.0, pltpu.roll(one, 31, 0))
    left = jnp.where(lane % 32 == 0, 0.0, pltpu.roll(one, 1, 1))
    right = jnp.where(lane % 32 == 31, 0.0, pltpu.roll(one, 127, 1))
    applied = diag * one - 128.0 * ((up + down) + (left + right))
    fix = one + (rem - applied) / diag
    weight = jnp.where(
        coef == 0, 0.5 * ROOT, jnp.where(coef == 1, 0.5 * ROOT * far_sign, jnp.where(coef == 2, 0.5 * near_sign, scale))
    )
    widen = ones_where(iota((128, 256), 0) % 32 == iota((128, 256), 1) // 8)
    fix_all[...] = dot(fix * weight, widen)
    fix_store = local(fix_all, fix_out, f_sem)

    absorb(all_sent, sent)
    absorb(yours, ro)
    absorb(mine, lo)
    fix_store.wait()


def shards(source, potential, level_shift):
    dma = pltpu.SemaphoreType.DMA
    vmem = lambda *shape: pltpu.VMEM(shape, F32)
    scratch = dict(
        shift_ref=pltpu.SMEM((4,), F32),
        own=vmem(4, 144, 256), other=vmem(4, 144, 256), pot=vmem(4, 144, 256), pot_other=vmem(4, 128, 256), s_buf=vmem(4, 144, 256),
        rd=vmem(4, 144, 256), fd=vmem(4, 144, 256), sd=vmem(4, 128, 256), strip=vmem(2, 16, 256),
        nb=vmem(4, 64, 256), nstrip=vmem(16, 256), u_buf=vmem(4, 80, 256), fv=vmem(4, 80, 256), rv=vmem(4, 80, 256),
        sv=vmem(4, 64, 256), ustrip=vmem(16, 256), nu=vmem(4, 32, 256), nustrip=vmem(8, 256),
        fu=vmem(2, 4, 48, 256), ru=vmem(2, 4, 48, 256),
        hd=vmem(2, 128, 256), hv=vmem(2, 64, 256), hu=vmem(2, 2, 32, 256),
        ub=vmem(4, 32, 256), ub_own=vmem(4, 32, 256), give=vmem(4, 32, 256), bk=vmem(4, 128, 256), gives=vmem(4, 64, 256),
        t_d=vmem(128, 256), x_d=vmem(128, 256), t_uv=vmem(128, 256), x_uv=vmem(128, 256),
        pot_all=vmem(4, 32, 128), d_sums=vmem(24, 128), d_x=vmem(3, 24, 128), d_total=vmem(24, 128),
        d_other=vmem(24, 128), uv_sums=vmem(8, 128), uv_x=vmem(3, 8, 128), uv_total=vmem(8, 128),
        tr=vmem(8, 8, 128), blocks=vmem(2, 256, 128), pick=vmem(3, 32, 64), pick_d=vmem(2, 32, 24),
        fix_all=vmem(32, 256), mine=vmem(4, 128, 256), yours=vmem(4, 128, 256),
        all_sent=vmem(2496, 256),
        h_sem=dma(()), l_sem=dma(()), p_sem=dma(()), q_sem=dma(()), f_sem=dma(()), sent=dma(()), r0=dma((4,)), r1=dma((8,)),
        r2=dma((4,)), rt=dma(()), ru_sem=dma(()), rx=dma((3,)), rp=dma(()), rdx=dma(()), rdp=dma(()), rc=dma(()),
        rg=dma(()), rb2=dma((4,)), rb1=dma((4,)), ro=dma(()), lo=dma(()),
    )
    raw, fix = pl.pallas_call(
        kernel,
        out_shape=(jax.ShapeDtypeStruct(source.shape, F32), jax.ShapeDtypeStruct((32, 256), F32)),
        in_specs=[
            pl.BlockSpec(memory_space=pltpu.HBM),
            pl.BlockSpec(memory_space=pltpu.HBM),
            pl.BlockSpec(memory_space=pltpu.HBM),
        ],
        out_specs=(pl.BlockSpec(memory_space=pl.ANY), pl.BlockSpec(memory_space=pl.ANY)),
        scratch_shapes=list(scratch.values()),
        compiler_params=pltpu.CompilerParams(
            collective_id=0, has_side_effects=True, vmem_limit_bytes=40 * 2**20
        ),
        name="space_time_apply",
    )(*(pltpu.with_memory_space_constraint(a, pltpu.HBM) for a in (level_shift, source, potential)))
    return (raw.reshape(4, 32, 8, 256) + fix[None, :, None, :]).reshape(source.shape)


def solution(mesh):
    in_specs = (P("tm", "plane", None, None), P("plane", None, None), P())
    out_specs = P("tm", "plane", None, None)
    return jax.shard_map(shards, mesh=mesh, in_specs=in_specs, out_specs=out_specs, check_vma=False)
```

time: 37.5 us -> 35.9 us (0.957)
  Pallas kernels: 35.7 us -> 34.7 us
  local copies, waits for them, and re-layouts: 0.65 us -> 0.02 us
    pallas_call x1, Pallas kernels: 35.7 us -> 34.7 us  [shards(): pl.pallas_call(kernel, out_shape=(jax.ShapeDtypeStruct(source.shape, F32)...]
    unnamed x2 -> x0, local copies, waits for them, and re-layouts: 0.65 us -> none
where the time goes in v4:
time: 35.9 us; the launch traced here: 35.7 us
  Pallas kernels  34.7 us (97%)
  other arithmetic  1.06 us (3%)
    pallas_call x1, Pallas kernels, shards(): pl.pallas_call(kernel, out_shape=(jax.ShapeDtypeStruct(source.shape, F32)...  34.7 us
    add x1, other arithmetic, shards(): raw.reshape(4, 32, 8, 256) + fix[None, :, None, :]  1.06 us

profile of v4, /device:TPU:1, one launch (start us, length us, event | category | flops | bytes accessed | tf_op | source)
XLA Modules:
  0.0 35.7 jit_solution(14262284081412647687)
XLA Ops:
  0.0 34.7 %space_time_apply.1 = (f32[1,4,256,256]{3,2,1,0:T(8,128)S(1)}, f32[32,256]{1,0:T(8,128)S(1)}) custom-call(f32[4]{0:T(128)} %shift_hbm.1, f32[1,4,256,256]{3,2,1,0:T(8,128)} %source.1, f32[4,256,256]{2,1,0:T(8,128)} %potential.1), custom_call_target="tpu_custom_call" | custom-call | tf_op jit(solution)/shard_map/space_time_apply/pallas_call | solution.py:444
  34.7 1.1 %broadcast_add_fusion = f32[1,4,256,256]{3,2,1,0:T(8,128)} fusion(f32[1,4,256,256]{3,2,1,0:T(8,128)S(1)} %get-tuple-element.7, f32[256,256]{1,0:T(8,128)S(1)} %broadcast_bitcast_fusion), kind=kLoop, calls=%fused_computation | loop fusion | flops 262144 | bytes 2359296 | tf_op jit(solution)/shard_map/add | solution.py:459
  (1 shorter events, 0.0 us)

commit v5 on v4

--- a/solution.py
+++ b/solution.py
@@ -43,7 +43,7 @@
     shift_ref, own, other, pot, pot_other, s_buf, rd, fd, sd, strip, nb, nstrip, u_buf, fv, rv, sv, ustrip, nu, nustrip, fu, ru,
     hd, hv, hu, ub, ub_own, give, bk, gives, t_d, x_d, t_uv, x_uv, pot_all, d_sums, d_x, d_total, d_other, uv_sums, uv_x, uv_total,
     tr, blocks, pick, pick_d, fix_all, mine, yours,
-    all_sent, h_sem, l_sem, p_sem, q_sem, f_sem, sent, r0, r1, r2, rt, ru_sem, rx, rp, rdx, rdp, rc, rg, rb2, rb1, ro, lo,
+    all_sent, h_sem, l_sem, p_sem, q_sem, f_sem, sent, r0, r1, r2, rt, ru_sem, rxd, rxv, rxu, rp, rdx, rdp, rc, rg, rb2, rb1, ro, lo,
 ):
     t, x = lax.axis_index("tm"), lax.axis_index("plane")
     e = t % 8
@@ -112,29 +112,44 @@
         s_buf[slot] = (own[slot] + other[slot]) * ROOT
         if slot < 2:
             to_near(slot, slot, 1 - p)
-        if slot == 1:
-            to_near(4, 0, p)
-            to_near(5, 1, p)
     for h in range(2):
         for i in range(4):
             for at, row in ((0, 7), (4, 40), (8, 39), (12, 72)):
                 strip[h, at + i : at + i + 1, :] = s_buf[i, row + 64 * h : row + 64 * h + 1, :]
+    strip_1 = remote(strip.at[1 - b], nstrip, rt, (near, x))
+    to_near(2, 2, 1 - p)
+    to_near(3, 3, 1 - p)
 
     sign = (1 - 2 * k).astype(F32)
     near_sign = (1 - 2 * b).astype(F32)
     far_sign = (1 - 2 * p).astype(F32)
     scale = ROOT * sign
-    keep_low, keep_high = ones_where(x > 0), ones_where(x < 3)
-    edge_low, edge_high = 1.0 - keep_low, 1.0 - keep_high
+    edge_low, edge_high = ones_where(x == 0), ones_where(x == 3)
     shift_load.wait()
     shift_0 = shift_ref[0]
     absorb(pot.at[:, 0:136, :], p_sem)
     for slot in range(4):
         rd[slot] = OMEGA / (6.0 + pot[slot] + shift_0)
         fd[slot] = (own[slot] - other[slot]) * scale * rd[slot]
-    below, above = (t, (x + 3) % 4), (t, (x + 1) % 4)
-    remote(fd.at[0, 8:136, :], hd.at[1], rx.at[0], below)
-    remote(fd.at[1, 8:136, :], hd.at[0], rx.at[0], above)
+
+    def to_side(src, halo, end, sem):
+        @pl.when(x < 3 if end == 0 else x > 0)
+        def _():
+            remote(src, halo.at[end], sem.at[end], (t, x + 1 - 2 * end))
+
+    def from_sides(halo, sem):
+        for end in range(2):
+            pl.when(x > 0 if end == 0 else x < 3)(lambda end=end: absorb(halo.at[end], sem.at[end]))
+
+    for end in range(2):
+        @pl.when(x == 3 * end)
+        def _():
+            hd[end] = jnp.zeros((128, 256), F32)
+            hv[end] = jnp.zeros((64, 256), F32)
+            hu[end] = jnp.zeros((2, 32, 256), F32)
+
+    to_side(fd.at[0, 8:136, :], hd, 1, rxd)
+    to_side(fd.at[1, 8:136, :], hd, 0, rxd)
 
     for slot in range(4):
         rv[slot] = OMEGA / (6.0 + pot[slot, rows(64 * b, 80), :] + shift_ref[1])
@@ -198,31 +213,24 @@
         for at, field in ((64, low), (96, high)):
             x_uv[at : at + 32, :] = field if slot == 0 else x_uv[at : at + 32, :] + field
 
-    passed_on(0)
-    passed_on(1)
-    to_near(2, 2, 1 - p)
-    to_near(3, 3, 1 - p)
-    strip_1 = remote(strip.at[1 - b], nstrip, rt, (near, x))
-    to_near(6, 2, p)
-    for slot in (0, 1):
+    for slot in range(4):
+        passed_on(slot)
+        for other_slot in ((0,), (1,), (), (2, 3))[slot]:
+            to_near(4 + other_slot, other_slot, p)
+        if slot == 0:
+            strip_1.wait_recv()
+            ustrip[...] = (strip[b] + nstrip[...]) * ROOT
+            strip_2 = remote(ustrip.at[rows(8 - 8 * p, 8), :], nustrip, ru_sem, (far, x))
+    details = (strip[b] - nstrip[...]) * (ROOT * near_sign)
+    for slot in range(4):
+        fv[slot, 7:8, :] = details[slot : slot + 1] * rv[slot, 7:8, :]
+        fv[slot, 72:73, :] = details[12 + slot : 13 + slot] * rv[slot, 72:73, :]
+    for slot, end in ((0, 1), (1, 0)):
         firsts[4 + slot].wait_recv()
         level_1(slot, p)
-    remote(fv.at[0, 8:72, :], hv.at[1], rx.at[1], below)
-    remote(fv.at[1, 8:72, :], hv.at[0], rx.at[1], above)
-    passed_on(2)
-    passed_on(3)
-    to_near(7, 3, p)
-    strip_1.wait_recv()
-    ustrip[...] = (strip[b] + nstrip[...]) * ROOT
-    strip_2 = remote(ustrip.at[rows(8 - 8 * p, 8), :], nustrip, ru_sem, (far, x))
-    details = (strip[b] - nstrip[...]) * (ROOT * near_sign)
-    for slot in range(4):
-        fv[slot, 7:8, :] = details[slot : slot + 1] * rv[slot, 7:8, :]
-        fv[slot, 72:73, :] = details[12 + slot : 13 + slot] * rv[slot, 72:73, :]
-    level_2(0)
-    level_2(1)
-    remote(fu.at[:, 0, 8:40, :], hu.at[1], rx.at[2], below)
-    remote(fu.at[:, 1, 8:40, :], hu.at[0], rx.at[2], above)
+        level_2(slot)
+        to_side(fu.at[:, slot, 8:40, :], hu, end, rxu)
+        to_side(fv.at[slot, 8:72, :], hv, end, rxv)
 
     def second_pass(f, weight, low_rim, high_rim, at, count, order, done):
         center = rows(at + 8, count)
@@ -230,8 +238,8 @@
         for plane in order:
             slot = SLOT[plane]
             mid, beside = beside_yz(f[slot, rows(at, count + 16), :])
-            low = f[SLOT[plane - 1], center, :] if plane > 0 else low_rim() * keep_low
-            high = f[SLOT[plane + 1], center, :] if plane < 3 else high_rim() * keep_high
+            low = f[SLOT[plane - 1], center, :] if plane > 0 else low_rim()
+            high = f[SLOT[plane + 1], center, :] if plane < 3 else high_rim()
             second = 1.2 * mid + weight[slot, center, :] * (beside + (low + high))
             done(slot, second)
             q = second - OMEGA * mid
@@ -241,7 +249,7 @@
                 outer = rim if outer is None else outer + rim
         return total, outer
 
-    absorb(hd, rx.at[0])
+    from_sides(hd, rxd)
 
     def odd_rows(step, _):
         at = 32 * step
@@ -261,36 +269,42 @@
         return 0
 
     lax.fori_loop(0, 4, odd_rows, 0)
+    y_at, y_row = iota((24, 128), 1), iota((24, 128), 0)
+    inner = ones_where(y_at // 8 + 1 == y_row)
+    beside = ones_where((y_at + 7) // 8 == y_row) + ones_where((y_at + 1) // 8 + 1 == y_row)
+    sums = dot(inner, dot(x_d[...], blocks[0]) + dot(t_d[...], blocks[1])) + dot(beside, dot(t_d[...], blocks[0]))
+    d_sums[...] = pltpu.roll(sums, 96, 1)
+    for m, peer in enumerate(x_peers):
+        remote(d_sums, d_x.at[m], rdx, (t, peer))
+
+    strip_2.wait_recv()
+    here = ustrip[rows(8 * p, 8), :]
+    low, high = (here + nustrip[...]) * ROOT, (here - nustrip[...]) * (ROOT * far_sign)
+    for slot in range(4):
+        for j, rim in enumerate((low, high)):
+            fu[j, slot, 7:8, :] = rim[slot : slot + 1] * ru[j, slot, 7:8, :]
+            fu[j, slot, 40:41, :] = rim[4 + slot : 5 + slot] * ru[j, slot, 40:41, :]
     for slot in (2, 3):
         firsts[4 + slot].wait_recv()
         level_1(slot, p)
-
-    def near_rows(step, _):
-        at = 32 * step
-        here = rows(at, 32)
-
-        def done(slot, second):
-            sv[slot, here, :] = second
-
-        summed, outer = second_pass(
-            fv, rv, lambda: hv[0, here, :], lambda: hv[1, here, :], at, 32, range(4), done
-        )
-        t_uv[here, :] = summed
-        x_uv[here, :] = 0.04 * x_uv[here, :] - outer
-        return 0
-
-    absorb(hv, rx.at[1])
-    lax.fori_loop(0, 2, near_rows, 0)
-
-    strip_2.wait_recv()
-    here = ustrip[rows(8 * p, 8), :]
-    low, high = (here + nustrip[...]) * ROOT, (here - nustrip[...]) * (ROOT * far_sign)
-    for slot in range(4):
-        for j, rim in enumerate((low, high)):
-            fu[j, slot, 7:8, :] = rim[slot : slot + 1] * ru[j, slot, 7:8, :]
-            fu[j, slot, 40:41, :] = rim[4 + slot : 5 + slot] * ru[j, slot, 40:41, :]
-    level_2(2)
-    level_2(3)
+        level_2(slot)
+
+    def near_rows(planes):
+        def body(step, _):
+            at = 32 * step
+            here = rows(at, 32)
+
+            def done(slot, second):
+                sv[slot, here, :] = second
+
+            summed, outer = second_pass(
+                fv, rv, lambda: hv[0, here, :], lambda: hv[1, here, :], at, 32, planes, done
+            )
+            t_uv[here, :] = summed if outer is None else t_uv[here, :] + summed
+            x_uv[here, :] = 0.04 * x_uv[here, :] if outer is None else x_uv[here, :] - outer
+            return 0
+
+        lax.fori_loop(0, 2, body, 0)
 
     backs_2 = {}
 
@@ -327,9 +341,14 @@
 
     far_rows(1)
     far_rows(2)
-    absorb(hu, rx.at[2])
+    near_rows((1, 2))
+    join(2, p, ub_own)
+    join(3, p, ub_own)
+    from_sides(hu, rxu)
     far_rows(0)
     far_rows(3)
+    from_sides(hv, rxv)
+    near_rows((0, 3))
 
     y_at, y_row = iota((32, 128), 1), iota((32, 128), 0)
     start = jnp.where(y_at < 64, 0, 16 + 8 * ((y_at - 64) // 32))
@@ -342,16 +361,8 @@
     )
     for m, peer in enumerate(x_peers):
         remote(uv_sums, uv_x.at[m], rc, (t, peer))
-    for slot in (2, 3, 0, 1):
-        join(slot, p, ub_own)
-    y_at, y_row = iota((24, 128), 1), iota((24, 128), 0)
-    inner = ones_where(y_at // 8 + 1 == y_row)
-    beside = ones_where((y_at + 7) // 8 == y_row) + ones_where((y_at + 1) // 8 + 1 == y_row)
-    sums = dot(inner, dot(x_d[...], blocks[0]) + dot(t_d[...], blocks[1])) + dot(beside, dot(t_d[...], blocks[0]))
-    d_sums[...] = pltpu.roll(sums, 96, 1)
-    for m, peer in enumerate(x_peers):
-        remote(d_sums, d_x.at[m], rdx, (t, peer))
-
+    join(0, p, ub_own)
+    join(1, p, ub_own)
     absorb(uv_x, rc)
     uv_total[...] = (uv_sums[...] + uv_x[0]) + (uv_x[1] + uv_x[2])
     for peer in group:
@@ -413,7 +424,9 @@
     fix_all[...] = dot(fix * weight, widen)
     fix_store = local(fix_all, fix_out, f_sem)
 
-    absorb(all_sent, sent)
+    outer = (x == 0) | (x == 3)
+    pl.when(outer)(lambda: absorb(all_sent.at[0:2240, :], sent))
+    pl.when(jnp.logical_not(outer))(lambda: absorb(all_sent, sent))
     absorb(yours, ro)
     absorb(mine, lo)
     fix_store.wait()
@@ -438,7 +451,7 @@
         fix_all=vmem(32, 256), mine=vmem(4, 128, 256), yours=vmem(4, 128, 256),
         all_sent=vmem(2496, 256),
         h_sem=dma(()), l_sem=dma(()), p_sem=dma(()), q_sem=dma(()), f_sem=dma(()), sent=dma(()), r0=dma((4,)), r1=dma((8,)),
-        r2=dma((4,)), rt=dma(()), ru_sem=dma(()), rx=dma((3,)), rp=dma(()), rdx=dma(()), rdp=dma(()), rc=dma(()),
+        r2=dma((4,)), rt=dma(()), ru_sem=dma(()), rxd=dma((2,)), rxv=dma((2,)), rxu=dma((2,)), rp=dma(()), rdx=dma(()), rdp=dma(()), rc=dma(()),
         rg=dma(()), rb2=dma((4,)), rb1=dma((4,)), ro=dma(()), lo=dma(()),
     )
     raw, fix = pl.pallas_call(

time: 35.9 us -> 34.3 us (0.955)
  Pallas kernels: 34.7 us -> 33.1 us
    pallas_call x1, Pallas kernels: 34.7 us -> 33.1 us  [shards(): pl.pallas_call(kernel, out_shape=(jax.ShapeDtypeStruct(source.shape, F32)...]
where the time goes in v5:
time: 34.3 us; the launch traced here: 34.2 us
  Pallas kernels  33.1 us (97%)
  other arithmetic  1.06 us (3%)
    pallas_call x1, Pallas kernels, shards(): pl.pallas_call(kernel, out_shape=(jax.ShapeDtypeStruct(source.shape, F32)...  33.1 us
    add x1, other arithmetic, shards(): raw.reshape(4, 32, 8, 256) + fix[None, :, None, :]  1.06 us

profile of v5, /device:TPU:1, one launch (start us, length us, event | category | flops | bytes accessed | tf_op | source)
XLA Modules:
  0.0 34.2 jit_solution(1338697739782181061)
XLA Ops:
  0.0 33.1 %space_time_apply.1 = (f32[1,4,256,256]{3,2,1,0:T(8,128)S(1)}, f32[32,256]{1,0:T(8,128)S(1)}) custom-call(f32[4]{0:T(128)} %shift_hbm.1, f32[1,4,256,256]{3,2,1,0:T(8,128)} %source.1, f32[4,256,256]{2,1,0:T(8,128)} %potential.1), custom_call_target="tpu_custom_call" | custom-call | tf_op jit(solution)/shard_map/space_time_apply/pallas_call | solution.py:457
  33.2 1.1 %broadcast_add_fusion = f32[1,4,256,256]{3,2,1,0:T(8,128)} fusion(f32[1,4,256,256]{3,2,1,0:T(8,128)S(1)} %get-tuple-element.7, f32[256,256]{1,0:T(8,128)S(1)} %broadcast_bitcast_fusion), kind=kLoop, calls=%fused_computation | loop fusion | flops 262144 | bytes 2359296 | tf_op jit(solution)/shard_map/add | solution.py:472
  (1 shorter events, 0.0 us)

commit v6 on v5

--- a/solution.py
+++ b/solution.py
@@ -41,9 +41,9 @@
 def kernel(
     shift_hbm, source, potential, out, fix_out,
     shift_ref, own, other, pot, pot_other, s_buf, rd, fd, sd, strip, nb, nstrip, u_buf, fv, rv, sv, ustrip, nu, nustrip, fu, ru,
-    hd, hv, hu, ub, ub_own, give, bk, gives, t_d, x_d, t_uv, x_uv, pot_all, d_sums, d_x, d_total, d_other, uv_sums, uv_x, uv_total,
+    pot_side, wv, wu, base_v, base_u, hd, hv, hu, ub, ub_own, give, bk, gives, t_d, x_d, t_uv, x_uv, pot_all, d_sums, d_x, d_total, d_other, uv_sums, uv_x, uv_total,
     tr, blocks, pick, pick_d, fix_all, mine, yours,
-    all_sent, h_sem, l_sem, p_sem, q_sem, f_sem, sent, r0, r1, r2, rt, ru_sem, rxd, rxv, rxu, rp, rdx, rdp, rc, rg, rb2, rb1, ro, lo,
+    all_sent, h_sem, l_sem, p_sem, q_sem, f_sem, sent, r0, r1, r2, rt, ru_sem, rxp, rxd, rxv, rxu, rp, rdx, rdp, rc, rg, rb2, rb1, ro, lo,
 ):
     t, x = lax.axis_index("tm"), lax.axis_index("plane")
     e = t % 8
@@ -99,9 +99,30 @@
         for slot, plane in enumerate(PLANES)
     ]
 
-    def to_near(index, slot, q):
+    def to_side(src, halo, end, sem):
+        @pl.when(x < 3 if end == 0 else x > 0)
+        def _():
+            remote(src, halo.at[end], sem.at[end], (t, x + 1 - 2 * end))
+
+    def from_sides(halo, sem):
+        for end in range(2):
+            pl.when(x > 0 if end == 0 else x < 3)(lambda end=end: absorb(halo.at[end], sem.at[end]))
+
+    for end in range(2):
+        @pl.when(x == 3 * end)
+        def _():
+            hd[end] = jnp.zeros((128, 256), F32)
+            hv[end] = jnp.zeros((64, 256), F32)
+            hu[end] = jnp.zeros((2, 32, 256), F32)
+            pot_side[end] = jnp.zeros((128, 256), F32)
+
+    to_side(potential.at[0, rows(128 * k, 128), :], pot_side, 1, rxp)
+    to_side(potential.at[3, rows(128 * k, 128), :], pot_side, 0, rxp)
+
+    def to_near(index, slots, q, start=0, count=32):
+        at = 32 * q + start
         firsts[index] = remote(
-            s_buf.at[slot, rows(72 - 64 * b + 32 * q, 32), :], nb.at[slot, rows(32 * q, 32), :],
+            s_buf.at[slots, rows(72 - 64 * b + at, count), :], nb.at[slots, rows(at, count), :],
             r1.at[index], (near, x),
         )
 
@@ -132,21 +153,6 @@
         rd[slot] = OMEGA / (6.0 + pot[slot] + shift_0)
         fd[slot] = (own[slot] - other[slot]) * scale * rd[slot]
 
-    def to_side(src, halo, end, sem):
-        @pl.when(x < 3 if end == 0 else x > 0)
-        def _():
-            remote(src, halo.at[end], sem.at[end], (t, x + 1 - 2 * end))
-
-    def from_sides(halo, sem):
-        for end in range(2):
-            pl.when(x > 0 if end == 0 else x < 3)(lambda end=end: absorb(halo.at[end], sem.at[end]))
-
-    for end in range(2):
-        @pl.when(x == 3 * end)
-        def _():
-            hd[end] = jnp.zeros((128, 256), F32)
-            hv[end] = jnp.zeros((64, 256), F32)
-            hu[end] = jnp.zeros((2, 32, 256), F32)
 
     to_side(fd.at[0, 8:136, :], hd, 1, rxd)
     to_side(fd.at[1, 8:136, :], hd, 0, rxd)
@@ -185,49 +191,82 @@
     pick_d[0] = ones_where((col < 18) & (16 * k - 1 + col == row))
     pick_d[1] = ones_where((col < 18) & (16 * (1 - k) - 1 + col == row))
 
-    def level_1(slot, q):
-        here = s_buf[slot, rows(8 + 64 * b + 32 * q, 32), :]
-        there = nb[slot, rows(32 * q, 32), :]
-        at = rows(8 + 32 * q, 32)
+    def level_1(slot, q, start=0, count=32):
+        inside = 32 * q + start
+        here = s_buf[slot, rows(8 + 64 * b + inside, count), :]
+        there = nb[slot, rows(inside, count), :]
+        at = rows(8 + inside, count)
         u_buf[slot, at, :] = (here + there) * ROOT
         detail = (here - there) * (ROOT * near_sign)
         fv[slot, at, :] = detail * rv[slot, at, :]
-        at = rows(32 * q, 32)
+        at = rows(inside, count)
         x_uv[at, :] = detail if slot == 0 else x_uv[at, :] + detail
 
     seconds = {}
+
+    def to_far(index, slots, start=0, count=32):
+        seconds[index] = remote(
+            u_buf.at[slots, rows(40 - 32 * p + start, count), :], nu.at[slots, start : start + count, :],
+            r2.at[index], (far, x),
+        )
 
     def passed_on(slot):
         firsts[slot].wait_recv()
         level_1(slot, 1 - p)
-        seconds[slot] = remote(
-            u_buf.at[slot, rows(40 - 32 * p, 32), :], nu.at[slot], r2.at[slot], (far, x)
-        )
-
-    def level_2(slot):
-        seconds[slot].wait_recv()
-        here = u_buf[slot, rows(8 + 32 * p, 32), :]
-        low, high = (here + nu[slot]) * ROOT, (here - nu[slot]) * (ROOT * far_sign)
-        fu[0, slot, 8:40, :] = low * ru[0, slot, 8:40, :]
-        fu[1, slot, 8:40, :] = high * ru[1, slot, 8:40, :]
-        for at, field in ((64, low), (96, high)):
-            x_uv[at : at + 32, :] = field if slot == 0 else x_uv[at : at + 32, :] + field
-
+        to_far(slot, slot, 0, 32 if slot < 2 else 24)
+
+    def level_2(slot, start=0, count=32):
+        here = u_buf[slot, rows(8 + 32 * p + start, count), :]
+        there = nu[slot, start : start + count, :]
+        low, high = (here + there) * ROOT, (here - there) * (ROOT * far_sign)
+        at = slice(8 + start, 8 + start + count)
+        fu[0, slot, at, :] = low * ru[0, slot, at, :]
+        fu[1, slot, at, :] = high * ru[1, slot, at, :]
+        for first, field in ((64 + start, low), (96 + start, high)):
+            at = slice(first, first + count)
+            x_uv[at, :] = field if slot == 0 else x_uv[at, :] + field
+
+    inner_slots = slice(2, 4)
     for slot in range(4):
         passed_on(slot)
-        for other_slot in ((0,), (1,), (), (2, 3))[slot]:
-            to_near(4 + other_slot, other_slot, p)
+        if slot < 2:
+            to_near(4 + slot, slot, p)
         if slot == 0:
             strip_1.wait_recv()
             ustrip[...] = (strip[b] + nstrip[...]) * ROOT
             strip_2 = remote(ustrip.at[rows(8 - 8 * p, 8), :], nustrip, ru_sem, (far, x))
+    to_near(6, 2, p, 0, 24)
+    to_near(7, 3, p, 0, 24)
+    to_far(4, inner_slots, 24, 8)
+    to_near(8, inner_slots, p, 24, 8)
     details = (strip[b] - nstrip[...]) * (ROOT * near_sign)
     for slot in range(4):
         fv[slot, 7:8, :] = details[slot : slot + 1] * rv[slot, 7:8, :]
         fv[slot, 72:73, :] = details[12 + slot : 13 + slot] * rv[slot, 72:73, :]
+        if slot > 1:
+            fv[slot, 39:40, :] = details[8 + slot : 9 + slot] * rv[slot, 39:40, :]
+    from_sides(pot_side, rxp)
+    kept = [ones_where(x > 0), ones_where(x < 3)]
+
+    def beside_weights(weight, start, count, shift, out):
+        side = []
+        for end in range(2):
+            field = 6.0 + pot_side[end, rows(start, count), :] + shift
+            side.append((OMEGA * kept[end]) / field)
+        inner = [weight[SLOT[plane], 8 : 8 + count, :] for plane in range(4)]
+        out[SLOT[0]] = side[0] + inner[1]
+        out[SLOT[1]] = inner[0] + inner[2]
+        out[SLOT[2]] = inner[1] + inner[3]
+        out[SLOT[3]] = inner[2] + side[1]
+
+    beside_weights(rv, 64 * b, 64, shift_ref[1], wv)
+    for j, level in ((0, 3), (1, 2)):
+        beside_weights(ru.at[j], 64 * b + 32 * p, 32, shift_ref[level], wu.at[j])
+
     for slot, end in ((0, 1), (1, 0)):
         firsts[4 + slot].wait_recv()
         level_1(slot, p)
+        seconds[slot].wait_recv()
         level_2(slot)
         to_side(fu.at[:, slot, 8:40, :], hu, end, rxu)
         to_side(fv.at[slot, 8:72, :], hv, end, rxv)
@@ -285,70 +324,116 @@
             fu[j, slot, 7:8, :] = rim[slot : slot + 1] * ru[j, slot, 7:8, :]
             fu[j, slot, 40:41, :] = rim[4 + slot : 5 + slot] * ru[j, slot, 40:41, :]
     for slot in (2, 3):
+        seconds[slot].wait_recv()
         firsts[4 + slot].wait_recv()
-        level_1(slot, p)
-        level_2(slot)
-
-    def near_rows(planes):
+        level_1(slot, p, 0, 24)
+        level_2(slot, 0, 24)
+
+    def own_planes(f, weight, sides, base, at, count, planes):
+        here, center = rows(at, count), rows(at + 8, count)
+        total, outer = None, None
+        for plane in planes:
+            slot = SLOT[plane]
+            mid, beside = beside_yz(f[slot, rows(at, count + 16), :])
+            within = weight[slot, center, :] * beside
+            base[slot, here, :] = 1.2 * mid + within
+            within = 0.4 * mid + within
+            q = within + mid * sides[slot, here, :]
+            total = q if total is None else total + q
+            if plane in (0, 3):
+                next_in = f[SLOT[1 if plane == 0 else 2], center, :]
+                rim = (within + weight[slot, center, :] * next_in) * (edge_low if plane == 0 else edge_high)
+                outer = rim if outer is None else outer + rim
+        return total, outer
+
+    def with_sides(f, weight, base, halo, at, count, plane):
+        here, center = rows(at, count), rows(at + 8, count)
+        low = f[SLOT[plane - 1], center, :] if plane > 0 else halo(0)
+        high = f[SLOT[plane + 1], center, :] if plane < 3 else halo(1)
+        return base[SLOT[plane], here, :] + weight[SLOT[plane], center, :] * (low + high)
+
+    def near_planes(planes, start, count):
         def body(step, _):
-            at = 32 * step
-            here = rows(at, 32)
-
-            def done(slot, second):
-                sv[slot, here, :] = second
-
-            summed, outer = second_pass(
-                fv, rv, lambda: hv[0, here, :], lambda: hv[1, here, :], at, 32, planes, done
-            )
-            t_uv[here, :] = summed if outer is None else t_uv[here, :] + summed
-            x_uv[here, :] = 0.04 * x_uv[here, :] if outer is None else x_uv[here, :] - outer
+            here = rows(32 * step + start, count)
+            summed, outer = own_planes(fv, rv, wv, base_v, 32 * step + start, count, planes)
+            if outer is None:
+                t_uv[here, :] = summed
+            else:
+                t_uv[here, :] += summed
+                x_uv[here, :] = 0.04 * x_uv[here, :] - outer
             return 0
 
         lax.fori_loop(0, 2, body, 0)
 
+    def near_rows(planes, start, count):
+        def body(step, _):
+            here = rows(32 * step + start, count)
+            for plane in planes:
+                sv[SLOT[plane], here, :] = with_sides(
+                    fv, rv, base_v, lambda end: hv[end, here, :], 32 * step + start, count, plane
+                )
+            return 0
+
+        lax.fori_loop(0, 2, body, 0)
+
     backs_2 = {}
 
-    def far_rows(plane):
-        made = []
-        for j, at in ((0, slice(64, 96)), (1, slice(96, 128))):
-            summed, outer = second_pass(
-                fu.at[j], ru.at[j], lambda: hu[0, j], lambda: hu[1, j], 0, 32, (plane,),
-                lambda slot, second: made.append(second),
-            )
-            t_uv[at, :] = summed if plane == 1 else t_uv[at, :] + summed
-            if plane == 1:
-                x_uv[at, :] = 0.04 * x_uv[at, :]
-            if outer is not None:
-                x_uv[at, :] = x_uv[at, :] - outer
+    def far_planes(planes, start, count):
+        for j in range(2):
+            at = slice(64 + 32 * j + start, 64 + 32 * j + start + count)
+            summed, outer = own_planes(fu.at[j], ru.at[j], wu.at[j], base_u.at[j], start, count, planes)
+            if outer is None:
+                t_uv[at, :] = summed
+            else:
+                t_uv[at, :] += summed
+                x_uv[at, :] = 0.04 * x_uv[at, :] - outer
+
+    def far_rows(plane, index, start=0, count=32):
+        here = slice(start, start + count)
+        made = [
+            with_sides(fu.at[j], ru.at[j], base_u.at[j], lambda end, j=j: hu[end, j, here, :], start, count, plane)
+            for j in range(2)
+        ]
         slot = SLOT[plane]
         low, high = made[0] * ROOT, made[1] * (ROOT * far_sign)
-        give[slot] = low - high
-        ub_own[slot] = low + high
-        backs_2[slot] = remote(give.at[slot], ub.at[slot], rb2.at[slot], (far, x))
-
-    def join(slot, q, ref):
-        low, high = ref[slot] * ROOT, sv[slot, rows(32 * q, 32), :] * (ROOT * near_sign)
-        gives[slot, rows(32 * q, 32), :] = low - high
-        bk[slot, rows(64 * b + 32 * q, 32), :] = low + high
+        give[slot, here, :] = low - high
+        ub_own[slot, here, :] = low + high
+        backs_2[index] = remote(give.at[slot, here, :], ub.at[slot, here, :], rb2.at[index], (far, x))
+
+    def join(slot, q, ref, start=0, count=32):
+        at = 32 * q + start
+        low = ref[slot, start : start + count, :] * ROOT
+        high = sv[slot, rows(at, count), :] * (ROOT * near_sign)
+        gives[slot, rows(at, count), :] = low - high
+        bk[slot, rows(64 * b + at, count), :] = low + high
         remote(
-            gives.at[slot, rows(32 * q, 32), :], bk.at[slot, rows(64 * b + 32 * q, 32), :],
-            rb1.at[slot], (near, x),
+            gives.at[slot, rows(at, count), :], bk.at[slot, rows(64 * b + at, count), :], rb1.at[slot], (near, x)
         )
 
     def rest(slot):
         backs_2[slot].wait_recv()
+        if slot > 1:
+            backs_2[2 + slot].wait_recv()
         join(slot, 1 - p, ub)
 
-    far_rows(1)
-    far_rows(2)
-    near_rows((1, 2))
-    join(2, p, ub_own)
-    join(3, p, ub_own)
-    from_sides(hu, rxu)
-    far_rows(0)
-    far_rows(3)
-    from_sides(hv, rxv)
-    near_rows((0, 3))
+    def inner_rows(start):
+        far_planes((1, 2), start, 16)
+        far_rows(1, 2 + start // 8, start, 16)
+        far_rows(2, 3 + start // 8, start, 16)
+        near_planes((1, 2), start, 16)
+        near_rows((1, 2), start, 16)
+        join(2, p, ub_own, start, 16)
+        join(3, p, ub_own, start, 16)
+
+    inner_rows(0)
+    seconds[4].wait_recv()
+    firsts[8].wait_recv()
+    for slot in (2, 3):
+        level_1(slot, p, 24, 8)
+        level_2(slot, 24, 8)
+    inner_rows(16)
+    far_planes((0, 3), 0, 32)
+    near_planes((0, 3), 0, 32)
 
     y_at, y_row = iota((32, 128), 1), iota((32, 128), 0)
     start = jnp.where(y_at < 64, 0, 16 + 8 * ((y_at - 64) // 32))
@@ -361,14 +446,19 @@
     )
     for m, peer in enumerate(x_peers):
         remote(uv_sums, uv_x.at[m], rc, (t, peer))
+    from_sides(hu, rxu)
+    far_rows(0, 0)
+    far_rows(3, 1)
+    from_sides(hv, rxv)
+    near_rows((0, 3), 0, 32)
     join(0, p, ub_own)
     join(1, p, ub_own)
+    rest(2)
     absorb(uv_x, rc)
     uv_total[...] = (uv_sums[...] + uv_x[0]) + (uv_x[1] + uv_x[2])
     for peer in group:
         remote(uv_total, tr.at[e], rg, (peer, x))
     tr[e] = uv_total[...]
-    rest(2)
     rest(3)
     absorb(d_x, rdx)
     absorb(pot_all.at[1:4], rp)
@@ -425,7 +515,7 @@
     fix_store = local(fix_all, fix_out, f_sem)
 
     outer = (x == 0) | (x == 3)
-    pl.when(outer)(lambda: absorb(all_sent.at[0:2240, :], sent))
+    pl.when(outer)(lambda: absorb(all_sent.at[0:2368, :], sent))
     pl.when(jnp.logical_not(outer))(lambda: absorb(all_sent, sent))
     absorb(yours, ro)
     absorb(mine, lo)
@@ -442,6 +532,7 @@
         nb=vmem(4, 64, 256), nstrip=vmem(16, 256), u_buf=vmem(4, 80, 256), fv=vmem(4, 80, 256), rv=vmem(4, 80, 256),
         sv=vmem(4, 64, 256), ustrip=vmem(16, 256), nu=vmem(4, 32, 256), nustrip=vmem(8, 256),
         fu=vmem(2, 4, 48, 256), ru=vmem(2, 4, 48, 256),
+        pot_side=vmem(2, 128, 256), wv=vmem(4, 64, 256), wu=vmem(2, 4, 32, 256), base_v=vmem(4, 64, 256), base_u=vmem(2, 4, 32, 256),
         hd=vmem(2, 128, 256), hv=vmem(2, 64, 256), hu=vmem(2, 2, 32, 256),
         ub=vmem(4, 32, 256), ub_own=vmem(4, 32, 256), give=vmem(4, 32, 256), bk=vmem(4, 128, 256), gives=vmem(4, 64, 256),
         t_d=vmem(128, 256), x_d=vmem(128, 256), t_uv=vmem(128, 256), x_uv=vmem(128, 256),
@@ -449,10 +540,10 @@
         d_other=vmem(24, 128), uv_sums=vmem(8, 128), uv_x=vmem(3, 8, 128), uv_total=vmem(8, 128),
         tr=vmem(8, 8, 128), blocks=vmem(2, 256, 128), pick=vmem(3, 32, 64), pick_d=vmem(2, 32, 24),
         fix_all=vmem(32, 256), mine=vmem(4, 128, 256), yours=vmem(4, 128, 256),
-        all_sent=vmem(2496, 256),
-        h_sem=dma(()), l_sem=dma(()), p_sem=dma(()), q_sem=dma(()), f_sem=dma(()), sent=dma(()), r0=dma((4,)), r1=dma((8,)),
-        r2=dma((4,)), rt=dma(()), ru_sem=dma(()), rxd=dma((2,)), rxv=dma((2,)), rxu=dma((2,)), rp=dma(()), rdx=dma(()), rdp=dma(()), rc=dma(()),
-        rg=dma(()), rb2=dma((4,)), rb1=dma((4,)), ro=dma(()), lo=dma(()),
+        all_sent=vmem(2752, 256),
+        h_sem=dma(()), l_sem=dma(()), p_sem=dma(()), q_sem=dma(()), f_sem=dma(()), sent=dma(()), r0=dma((4,)), r1=dma((9,)),
+        r2=dma((5,)), rt=dma(()), ru_sem=dma(()), rxp=dma((2,)), rxd=dma((2,)), rxv=dma((2,)), rxu=dma((2,)), rp=dma(()), rdx=dma(()), rdp=dma(()), rc=dma(()),
+        rg=dma(()), rb2=dma((6,)), rb1=dma((4,)), ro=dma(()), lo=dma(()),
     )
     raw, fix = pl.pallas_call(
         kernel,

time: 34.3 us -> 34.6 us (level)
  no operation moved by 1% of the time
where the time goes in v6:
time: 34.6 us; the launch traced here: 34.4 us
  Pallas kernels  33.3 us (96%)
  other arithmetic  1.06 us (3%)
    pallas_call x1, Pallas kernels, shards(): pl.pallas_call(kernel, out_shape=(jax.ShapeDtypeStruct(source.shape, F32)...  33.3 us
    add x1, other arithmetic, shards(): raw.reshape(4, 32, 8, 256) + fix[None, :, None, :]  1.06 us

profile of v6, /device:TPU:1, one launch (start us, length us, event | category | flops | bytes accessed | tf_op | source)
XLA Modules:
  0.0 34.4 jit_solution(9899784969278593463)
XLA Ops:
  0.0 33.3 %space_time_apply.1 = (f32[1,4,256,256]{3,2,1,0:T(8,128)S(1)}, f32[32,256]{1,0:T(8,128)S(1)}) custom-call(f32[4]{0:T(128)} %shift_hbm.1, f32[1,4,256,256]{3,2,1,0:T(8,128)} %source.1, f32[4,256,256]{2,1,0:T(8,128)} %potential.1), custom_call_target="tpu_custom_call" | custom-call | tf_op jit(solution)/shard_map/space_time_apply/pallas_call | solution.py:548
  33.4 1.1 %broadcast_add_fusion = f32[1,4,256,256]{3,2,1,0:T(8,128)} fusion(f32[1,4,256,256]{3,2,1,0:T(8,128)S(1)} %get-tuple-element.7, f32[256,256]{1,0:T(8,128)S(1)} %broadcast_bitcast_fusion), kind=kLoop, calls=%fused_computation | loop fusion | flops 262144 | bytes 2359296 | tf_op jit(solution)/shard_map/add | solution.py:563
  (1 shorter events, 0.0 us)

commit v7 on v6

--- a/solution.py
+++ b/solution.py
@@ -40,10 +40,10 @@
 
 def kernel(
     shift_hbm, source, potential, out, fix_out,
-    shift_ref, own, other, pot, pot_other, s_buf, rd, fd, sd, strip, nb, nstrip, u_buf, fv, rv, sv, ustrip, nu, nustrip, fu, ru,
+    shift_ref, own, other, pot, pot_other, s_buf, rd, fd, sd, strip, nb, raw, nstrip, u_buf, fv, rv, sv, ustrip, nu, nustrip, fu, ru,
     pot_side, wv, wu, base_v, base_u, hd, hv, hu, ub, ub_own, give, bk, gives, t_d, x_d, t_uv, x_uv, pot_all, d_sums, d_x, d_total, d_other, uv_sums, uv_x, uv_total,
     tr, blocks, pick, pick_d, fix_all, mine, yours,
-    all_sent, h_sem, l_sem, p_sem, q_sem, f_sem, sent, r0, r1, r2, rt, ru_sem, rxp, rxd, rxv, rxu, rp, rdx, rdp, rc, rg, rb2, rb1, ro, lo,
+    all_sent, h_sem, l_sem, p_sem, q_sem, f_sem, sent, r_raw, r0, r1, r2, rt, ru_sem, rxp, rxd, rxv, rxu, rp, rdx, rdp, rc, rg, rb2, rb1, ro, lo,
 ):
     t, x = lax.axis_index("tm"), lax.axis_index("plane")
     e = t % 8
@@ -91,13 +91,14 @@
 
     pl.semaphore_wait(barrier, 10)
 
-    swaps = [
+    first_rows = 64 - 64 * b + 32 - 32 * p
+    remote(source.at[0, PLANES[0], rows(128 * k + first_rows, 32), :], raw.at[0], r_raw, (near, x))
+    remote(source.at[0, PLANES[0], rows(128 - 128 * k + first_rows, 32), :], raw.at[1], r_raw, (near + 1 - 2 * k, x))
+    for slot in (1, 0, 2, 3):
         remote(
-            source.at[0, plane, rows(120 - 120 * k, 136), :], other.at[slot, rows(8 * k, 136), :],
-            r0.at[slot], (partner, x),
+            source.at[0, PLANES[slot], rows(120 - 120 * k, 136), :], other.at[slot, rows(8 * k, 136), :],
+            r0.at[0 if slot == 1 else 1], (partner, x),
         )
-        for slot, plane in enumerate(PLANES)
-    ]
 
     def to_side(src, halo, end, sem):
         @pl.when(x < 3 if end == 0 else x > 0)
@@ -123,16 +124,17 @@
         at = 32 * q + start
         firsts[index] = remote(
             s_buf.at[slots, rows(72 - 64 * b + at, count), :], nb.at[slots, rows(at, count), :],
-            r1.at[index], (near, x),
+            r1.at[min(index, 6) if index < 8 else 0], (near, x),
         )
 
     firsts = {}
     absorb(own.at[:, 0:136, :], l_sem)
-    for slot in range(4):
-        swaps[slot].wait_recv()
+    absorb(other.at[1, 0:136, :], r0.at[0])
+    s_buf[1] = (own[1] + other[1]) * ROOT
+    to_near(1, 1, 1 - p)
+    absorb(other.at[0:3, 0:136, :], r0.at[1])
+    for slot in (0, 2, 3):
         s_buf[slot] = (own[slot] + other[slot]) * ROOT
-        if slot < 2:
-            to_near(slot, slot, 1 - p)
     for h in range(2):
         for i in range(4):
             for at, row in ((0, 7), (4, 40), (8, 39), (12, 72)):
@@ -207,11 +209,15 @@
     def to_far(index, slots, start=0, count=32):
         seconds[index] = remote(
             u_buf.at[slots, rows(40 - 32 * p + start, count), :], nu.at[slots, start : start + count, :],
-            r2.at[index], (far, x),
+            r2.at[index - index // 3], (far, x),
         )
 
     def passed_on(slot):
-        firsts[slot].wait_recv()
+        if slot == 0:
+            absorb(raw, r_raw)
+            nb[0, rows(32 - 32 * p, 32), :] = (raw[0] + raw[1]) * ROOT
+        else:
+            firsts[slot].wait_recv()
         level_1(slot, 1 - p)
         to_far(slot, slot, 0, 32 if slot < 2 else 24)
 
@@ -323,9 +329,9 @@
         for j, rim in enumerate((low, high)):
             fu[j, slot, 7:8, :] = rim[slot : slot + 1] * ru[j, slot, 7:8, :]
             fu[j, slot, 40:41, :] = rim[4 + slot : 5 + slot] * ru[j, slot, 40:41, :]
+    absorb(nu.at[2:4, 0:24, :], r2.at[2])
+    absorb(nb.at[2:4, 0:24, :], r1.at[6])
     for slot in (2, 3):
-        seconds[slot].wait_recv()
-        firsts[4 + slot].wait_recv()
         level_1(slot, p, 0, 24)
         level_2(slot, 0, 24)
 
@@ -376,8 +382,6 @@
 
         lax.fori_loop(0, 2, body, 0)
 
-    backs_2 = {}
-
     def far_planes(planes, start, count):
         for j in range(2):
             at = slice(64 + 32 * j + start, 64 + 32 * j + start + count)
@@ -388,7 +392,7 @@
                 t_uv[at, :] += summed
                 x_uv[at, :] = 0.04 * x_uv[at, :] - outer
 
-    def far_rows(plane, index, start=0, count=32):
+    def far_rows(plane, start=0, count=32):
         here = slice(start, start + count)
         made = [
             with_sides(fu.at[j], ru.at[j], base_u.at[j], lambda end, j=j: hu[end, j, here, :], start, count, plane)
@@ -398,7 +402,7 @@
         low, high = made[0] * ROOT, made[1] * (ROOT * far_sign)
         give[slot, here, :] = low - high
         ub_own[slot, here, :] = low + high
-        backs_2[index] = remote(give.at[slot, here, :], ub.at[slot, here, :], rb2.at[index], (far, x))
+        remote(give.at[slot, here, :], ub.at[slot, here, :], rb2.at[slot], (far, x))
 
     def join(slot, q, ref, start=0, count=32):
         at = 32 * q + start
@@ -407,19 +411,17 @@
         gives[slot, rows(at, count), :] = low - high
         bk[slot, rows(64 * b + at, count), :] = low + high
         remote(
-            gives.at[slot, rows(at, count), :], bk.at[slot, rows(64 * b + at, count), :], rb1.at[slot], (near, x)
+            gives.at[slot, rows(at, count), :], bk.at[slot, rows(64 * b + at, count), :], rb1.at[4 if slot == 1 and ref is ub else slot], (near, x)
         )
 
     def rest(slot):
-        backs_2[slot].wait_recv()
-        if slot > 1:
-            backs_2[2 + slot].wait_recv()
+        absorb(ub.at[slot], rb2.at[slot])
         join(slot, 1 - p, ub)
 
     def inner_rows(start):
         far_planes((1, 2), start, 16)
-        far_rows(1, 2 + start // 8, start, 16)
-        far_rows(2, 3 + start // 8, start, 16)
+        far_rows(1, start, 16)
+        far_rows(2, start, 16)
         near_planes((1, 2), start, 16)
         near_rows((1, 2), start, 16)
         join(2, p, ub_own, start, 16)
@@ -447,8 +449,8 @@
     for m, peer in enumerate(x_peers):
         remote(uv_sums, uv_x.at[m], rc, (t, peer))
     from_sides(hu, rxu)
-    far_rows(0, 0)
-    far_rows(3, 1)
+    far_rows(0)
+    far_rows(3)
     from_sides(hv, rxv)
     near_rows((0, 3), 0, 32)
     join(0, p, ub_own)
@@ -465,11 +467,11 @@
     d_total[...] = (d_sums[...] + d_x[0]) + (d_x[1] + d_x[2])
     d_swap = remote(d_total, d_other, rdp, (partner, x))
 
-    def finish(slot, start):
-        here = rows(start, 64)
+    def finish(slot, start, count=64):
+        here = rows(start, count)
         even, odd = bk[slot, here, :], sd[slot, here, :] * sign
         yours[slot, here, :] = (even - odd) * ROOT
-        there = out.at[0, PLANES[slot], rows(128 * k + start, 64), :]
+        there = out.at[0, PLANES[slot], rows(128 * k + start, count), :]
         remote(yours.at[slot, here, :], there, ro, (partner, x))
         mine[slot, here, :] = (even + odd) * ROOT
         local(mine.at[slot, here, :], there, lo)
@@ -483,8 +485,11 @@
         absorb(gives.at[slot], rb1.at[slot])
         finish(slot, 64 - 64 * b)
 
-    for slot in (2, 3, 0, 1):
+    for slot in (2, 3, 0):
         finish_far(slot)
+    for q, index in ((p, 1), (1 - p, 4)):
+        absorb(gives.at[1, 0:32, :], rb1.at[index])
+        finish(1, 64 - 64 * b + 32 * q, 32)
     absorb(tr.at[0:7], rg)
     d_swap.wait_recv()
 
@@ -515,7 +520,7 @@
     fix_store = local(fix_all, fix_out, f_sem)
 
     outer = (x == 0) | (x == 3)
-    pl.when(outer)(lambda: absorb(all_sent.at[0:2368, :], sent))
+    pl.when(outer)(lambda: absorb(all_sent.at[0:2400, :], sent))
     pl.when(jnp.logical_not(outer))(lambda: absorb(all_sent, sent))
     absorb(yours, ro)
     absorb(mine, lo)
@@ -529,7 +534,7 @@
         shift_ref=pltpu.SMEM((4,), F32),
         own=vmem(4, 144, 256), other=vmem(4, 144, 256), pot=vmem(4, 144, 256), pot_other=vmem(4, 128, 256), s_buf=vmem(4, 144, 256),
         rd=vmem(4, 144, 256), fd=vmem(4, 144, 256), sd=vmem(4, 128, 256), strip=vmem(2, 16, 256),
-        nb=vmem(4, 64, 256), nstrip=vmem(16, 256), u_buf=vmem(4, 80, 256), fv=vmem(4, 80, 256), rv=vmem(4, 80, 256),
+        nb=vmem(4, 64, 256), raw=vmem(2, 32, 256), nstrip=vmem(16, 256), u_buf=vmem(4, 80, 256), fv=vmem(4, 80, 256), rv=vmem(4, 80, 256),
         sv=vmem(4, 64, 256), ustrip=vmem(16, 256), nu=vmem(4, 32, 256), nustrip=vmem(8, 256),
         fu=vmem(2, 4, 48, 256), ru=vmem(2, 4, 48, 256),
         pot_side=vmem(2, 128, 256), wv=vmem(4, 64, 256), wu=vmem(2, 4, 32, 256), base_v=vmem(4, 64, 256), base_u=vmem(2, 4, 32, 256),
@@ -540,10 +545,10 @@
         d_other=vmem(24, 128), uv_sums=vmem(8, 128), uv_x=vmem(3, 8, 128), uv_total=vmem(8, 128),
         tr=vmem(8, 8, 128), blocks=vmem(2, 256, 128), pick=vmem(3, 32, 64), pick_d=vmem(2, 32, 24),
         fix_all=vmem(32, 256), mine=vmem(4, 128, 256), yours=vmem(4, 128, 256),
-        all_sent=vmem(2752, 256),
-        h_sem=dma(()), l_sem=dma(()), p_sem=dma(()), q_sem=dma(()), f_sem=dma(()), sent=dma(()), r0=dma((4,)), r1=dma((9,)),
-        r2=dma((5,)), rt=dma(()), ru_sem=dma(()), rxp=dma((2,)), rxd=dma((2,)), rxv=dma((2,)), rxu=dma((2,)), rp=dma(()), rdx=dma(()), rdp=dma(()), rc=dma(()),
-        rg=dma(()), rb2=dma((6,)), rb1=dma((4,)), ro=dma(()), lo=dma(()),
+        all_sent=vmem(2784, 256),
+        h_sem=dma(()), l_sem=dma(()), p_sem=dma(()), q_sem=dma(()), f_sem=dma(()), sent=dma(()), r_raw=dma(()), r0=dma((2,)), r1=dma((7,)),
+        r2=dma((4,)), rt=dma(()), ru_sem=dma(()), rxp=dma((2,)), rxd=dma((2,)), rxv=dma((2,)), rxu=dma((2,)), rp=dma(()), rdx=dma(()), rdp=dma(()), rc=dma(()),
+        rg=dma(()), rb2=dma((4,)), rb1=dma((5,)), ro=dma(()), lo=dma(()),
     )
     raw, fix = pl.pallas_call(
         kernel,

time: 34.6 us -> 34 us (0.983)
  Pallas kernels: 33.3 us -> 32.8 us
    pallas_call x1, Pallas kernels: 33.3 us -> 32.8 us  [shards(): pl.pallas_call(kernel, out_shape=(jax.ShapeDtypeStruct(source.shape, F32)...]
where the time goes in v7:
time: 34 us; the launch traced here: 33.9 us
  Pallas kernels  32.8 us (96%)
  other arithmetic  1.06 us (3%)
    pallas_call x1, Pallas kernels, shards(): pl.pallas_call(kernel, out_shape=(jax.ShapeDtypeStruct(source.shape, F32)...  32.8 us
    add x1, other arithmetic, shards(): raw.reshape(4, 32, 8, 256) + fix[None, :, None, :]  1.06 us

profile of v7, /device:TPU:1, one launch (start us, length us, event | category | flops | bytes accessed | tf_op | source)
XLA Modules:
  0.0 33.9 jit_solution(3626838159464846566)
XLA Ops:
  0.0 32.8 %space_time_apply.1 = (f32[1,4,256,256]{3,2,1,0:T(8,128)S(1)}, f32[32,256]{1,0:T(8,128)S(1)}) custom-call(f32[4]{0:T(128)} %shift_hbm.1, f32[1,4,256,256]{3,2,1,0:T(8,128)} %source.1, f32[4,256,256]{2,1,0:T(8,128)} %potential.1), custom_call_target="tpu_custom_call" | custom-call | tf_op jit(solution)/shard_map/space_time_apply/pallas_call | solution.py:553
  32.8 1.1 %broadcast_add_fusion = f32[1,4,256,256]{3,2,1,0:T(8,128)} fusion(f32[1,4,256,256]{3,2,1,0:T(8,128)S(1)} %get-tuple-element.7, f32[256,256]{1,0:T(8,128)S(1)} %broadcast_bitcast_fusion), kind=kLoop, calls=%fused_computation | loop fusion | flops 262144 | bytes 2359296 | tf_op jit(solution)/shard_map/add | solution.py:568
  (1 shorter events, 0.0 us)

commit v8 on v7

--- a/solution.py
+++ b/solution.py
@@ -56,7 +56,7 @@
     group = [t - e + (e + m) % 8 for m in range(1, 8)]
 
     barrier = pltpu.get_barrier_semaphore()
-    for peer in group:
+    for peer in (far, near, near + 1 - 2 * k, partner):
         pl.semaphore_signal(barrier, inc=1, device_id=(peer, x), device_id_type=MESH)
     for peer in x_peers:
         pl.semaphore_signal(barrier, inc=1, device_id=(t, peer), device_id_type=MESH)
@@ -89,7 +89,7 @@
         for ref in (own, other, pot):
             ref[slot, rows(136 * k, 8), :] = jnp.zeros((8, 256), F32)
 
-    pl.semaphore_wait(barrier, 10)
+    pl.semaphore_wait(barrier, 7)
 
     first_rows = 64 - 64 * b + 32 - 32 * p
     remote(source.at[0, PLANES[0], rows(128 * k + first_rows, 32), :], raw.at[0], r_raw, (near, x))

time: 34 us -> 33.1 us (0.974)
  Pallas kernels: 32.8 us -> 31.9 us
    pallas_call x1, Pallas kernels: 32.8 us -> 31.9 us  [shards(): pl.pallas_call(kernel, out_shape=(jax.ShapeDtypeStruct(source.shape, F32)...]
where the time goes in v8:
time: 33.1 us; the launch traced here: 33 us
  Pallas kernels  31.9 us (96%)
  other arithmetic  1.06 us (3%)
    pallas_call x1, Pallas kernels, shards(): pl.pallas_call(kernel, out_shape=(jax.ShapeDtypeStruct(source.shape, F32)...  31.9 us
    add x1, other arithmetic, shards(): raw.reshape(4, 32, 8, 256) + fix[None, :, None, :]  1.06 us

profile of v8, /device:TPU:1, one launch (start us, length us, event | category | flops | bytes accessed | tf_op | source)
XLA Modules:
  0.0 33.0 jit_solution(10229911331044661213)
XLA Ops:
  0.0 31.9 %space_time_apply.1 = (f32[1,4,256,256]{3,2,1,0:T(8,128)S(1)}, f32[32,256]{1,0:T(8,128)S(1)}) custom-call(f32[4]{0:T(128)} %shift_hbm.1, f32[1,4,256,256]{3,2,1,0:T(8,128)} %source.1, f32[4,256,256]{2,1,0:T(8,128)} %potential.1), custom_call_target="tpu_custom_call" | custom-call | tf_op jit(solution)/shard_map/space_time_apply/pallas_call | solution.py:553
  31.9 1.1 %broadcast_add_fusion = f32[1,4,256,256]{3,2,1,0:T(8,128)} fusion(f32[1,4,256,256]{3,2,1,0:T(8,128)S(1)} %get-tuple-element.7, f32[256,256]{1,0:T(8,128)S(1)} %broadcast_bitcast_fusion), kind=kLoop, calls=%fused_computation | loop fusion | flops 262144 | bytes 2359296 | tf_op jit(solution)/shard_map/add | solution.py:568
  (1 shorter events, 0.0 us)

commit v9 on v8

--- a/solution.py
+++ b/solution.py
@@ -43,7 +43,7 @@
     shift_ref, own, other, pot, pot_other, s_buf, rd, fd, sd, strip, nb, raw, nstrip, u_buf, fv, rv, sv, ustrip, nu, nustrip, fu, ru,
     pot_side, wv, wu, base_v, base_u, hd, hv, hu, ub, ub_own, give, bk, gives, t_d, x_d, t_uv, x_uv, pot_all, d_sums, d_x, d_total, d_other, uv_sums, uv_x, uv_total,
     tr, blocks, pick, pick_d, fix_all, mine, yours,
-    all_sent, h_sem, l_sem, p_sem, q_sem, f_sem, sent, r_raw, r0, r1, r2, rt, ru_sem, rxp, rxd, rxv, rxu, rp, rdx, rdp, rc, rg, rb2, rb1, ro, lo,
+    all_sent, h_sem, l_sem, p_sem, sent, ends, r_raw, r0, r1, r2, rt, ru_sem, rxp, rxd, rxv, rxu, rp, rdx, rdp, rc, rg, rb2, rb1,
 ):
     t, x = lax.axis_index("tm"), lax.axis_index("plane")
     e = t % 8
@@ -84,7 +84,7 @@
     shift_load = local(shift_hbm, shift_ref, h_sem)
     for slot, plane in enumerate(PLANES):
         local(potential.at[plane, rows(120 * k, 136), :], pot.at[slot, rows(8 - 8 * k, 136), :], p_sem)
-    rest_load = local(potential.at[:, rows(128 - 128 * k, 128), :], pot_other, q_sem)
+    local(potential.at[:, rows(128 - 128 * k, 128), :], pot_other, p_sem)
     for slot in range(4):
         for ref in (own, other, pot):
             ref[slot, rows(136 * k, 8), :] = jnp.zeros((8, 256), F32)
@@ -150,7 +150,7 @@
     edge_low, edge_high = ones_where(x == 0), ones_where(x == 3)
     shift_load.wait()
     shift_0 = shift_ref[0]
-    absorb(pot.at[:, 0:136, :], p_sem)
+    absorb(all_sent.at[0:1056, :], p_sem)
     for slot in range(4):
         rd[slot] = OMEGA / (6.0 + pot[slot] + shift_0)
         fd[slot] = (own[slot] - other[slot]) * scale * rd[slot]
@@ -168,7 +168,6 @@
     z_at, z_block = iota((256, 128), 0), iota((256, 128), 1)
     lane_block = ones_where(z_at // 8 == z_block % 32)
     row, col = iota((32, 128), 0), iota((32, 128), 1)
-    rest_load.wait()
     pot_sum = (pot[0, 8:136, :] + pot[1, 8:136, :]) + (pot[2, 8:136, :] + pot[3, 8:136, :])
     pot_rest = (pot_other[0] + pot_other[1]) + (pot_other[2] + pot_other[3])
     pot_all[0] = dot(ones_where(col // 8 + 16 * k == row), dot(pot_sum, lane_block)) + dot(
@@ -472,9 +471,9 @@
         even, odd = bk[slot, here, :], sd[slot, here, :] * sign
         yours[slot, here, :] = (even - odd) * ROOT
         there = out.at[0, PLANES[slot], rows(128 * k + start, count), :]
-        remote(yours.at[slot, here, :], there, ro, (partner, x))
+        remote(yours.at[slot, here, :], there, ends, (partner, x))
         mine[slot, here, :] = (even + odd) * ROOT
-        local(mine.at[slot, here, :], there, lo)
+        local(mine.at[slot, here, :], there, sent)
 
     rest(0)
     rest(1)
@@ -517,14 +516,25 @@
     )
     widen = ones_where(iota((128, 256), 0) % 32 == iota((128, 256), 1) // 8)
     fix_all[...] = dot(fix * weight, widen)
-    fix_store = local(fix_all, fix_out, f_sem)
+    local(fix_all, fix_out, sent)
 
     outer = (x == 0) | (x == 3)
-    pl.when(outer)(lambda: absorb(all_sent.at[0:2400, :], sent))
+    pl.when(outer)(lambda: absorb(all_sent.at[0:2944, :], sent))
     pl.when(jnp.logical_not(outer))(lambda: absorb(all_sent, sent))
-    absorb(yours, ro)
-    absorb(mine, lo)
-    fix_store.wait()
+    absorb(yours, ends)
+
+
+def add_fix(raw, fix, out, buffer, sems):
+    copies = []
+    for plane in range(4):
+        for i in range(32):
+            at = slice(8 * i, 8 * i + 8)
+            buffer[plane, at, :] = raw[0, plane, at, :] + fix[i : i + 1, :]
+        copy = pltpu.make_async_copy(buffer.at[plane], out.at[0, plane], sems.at[plane])
+        copy.start()
+        copies.append(copy)
+    for copy in copies:
+        copy.wait()
 
 
 def shards(source, potential, level_shift):
@@ -545,10 +555,10 @@
         d_other=vmem(24, 128), uv_sums=vmem(8, 128), uv_x=vmem(3, 8, 128), uv_total=vmem(8, 128),
         tr=vmem(8, 8, 128), blocks=vmem(2, 256, 128), pick=vmem(3, 32, 64), pick_d=vmem(2, 32, 24),
         fix_all=vmem(32, 256), mine=vmem(4, 128, 256), yours=vmem(4, 128, 256),
-        all_sent=vmem(2784, 256),
-        h_sem=dma(()), l_sem=dma(()), p_sem=dma(()), q_sem=dma(()), f_sem=dma(()), sent=dma(()), r_raw=dma(()), r0=dma((2,)), r1=dma((7,)),
+        all_sent=vmem(3328, 256),
+        h_sem=dma(()), l_sem=dma(()), p_sem=dma(()), sent=dma(()), ends=dma(()), r_raw=dma(()), r0=dma((2,)), r1=dma((7,)),
         r2=dma((4,)), rt=dma(()), ru_sem=dma(()), rxp=dma((2,)), rxd=dma((2,)), rxv=dma((2,)), rxu=dma((2,)), rp=dma(()), rdx=dma(()), rdp=dma(()), rc=dma(()),
-        rg=dma(()), rb2=dma((4,)), rb1=dma((5,)), ro=dma(()), lo=dma(()),
+        rg=dma(()), rb2=dma((4,)), rb1=dma((5,)),
     )
     raw, fix = pl.pallas_call(
         kernel,
@@ -565,7 +575,14 @@
         ),
         name="space_time_apply",
     )(*(pltpu.with_memory_space_constraint(a, pltpu.HBM) for a in (level_shift, source, potential)))
-    return (raw.reshape(4, 32, 8, 256) + fix[None, :, None, :]).reshape(source.shape)
+    return pl.pallas_call(
+        add_fix,
+        out_shape=jax.ShapeDtypeStruct(source.shape, F32),
+        in_specs=[pl.BlockSpec(memory_space=pltpu.VMEM)] * 2,
+        out_specs=pl.BlockSpec(memory_space=pltpu.HBM),
+        scratch_shapes=[pltpu.VMEM((4, 256, 256), F32), dma((4,))],
+        name="add_fix",
+    )(*(pltpu.with_memory_space_constraint(a, pltpu.VMEM) for a in (raw, fix)))
 
 
 def solution(mesh):

time: 33.1 us -> 33 us (level)
  other arithmetic: 1.06 us -> 0 us
  Pallas kernels: 31.9 us -> 32.9 us
    add x1 -> x0, other arithmetic: 1.06 us -> none  [shards(): raw.reshape(4, 32, 8, 256) + fix[None, :, None, :]]
    pallas_call x0 -> x1, Pallas kernels: none -> 1.03 us  [shards(): pl.pallas_call(add_fix, out_shape=jax.ShapeDtypeStruct(source.shape, F32)...]
where the time goes in v9:
time: 33 us; the launch traced here: 32.9 us
  Pallas kernels  32.9 us (100%)
    pallas_call x1, Pallas kernels, shards(): pl.pallas_call(kernel, out_shape=(jax.ShapeDtypeStruct(source.shape, F32)...  31.9 us
    pallas_call x1, Pallas kernels, shards(): pl.pallas_call(add_fix, out_shape=jax.ShapeDtypeStruct(source.shape, F32)...  1.03 us

profile of v9, /device:TPU:1, one launch (start us, length us, event | category | flops | bytes accessed | tf_op | source)
XLA Modules:
  0.0 32.9 jit_solution(10057827688263905784)
XLA Ops:
  0.0 31.9 %space_time_apply.1 = (f32[1,4,256,256]{3,2,1,0:T(8,128)S(1)}, f32[32,256]{1,0:T(8,128)S(1)}) custom-call(f32[4]{0:T(128)} %shift_hbm.1, f32[1,4,256,256]{3,2,1,0:T(8,128)} %source.1, f32[4,256,256]{2,1,0:T(8,128)} %potential.1), custom_call_target="tpu_custom_call" | custom-call | tf_op jit(solution)/shard_map/space_time_apply/pallas_call | solution.py:563
  31.9 1.0 %add_fix.1 = f32[1,4,256,256]{3,2,1,0:T(8,128)} custom-call(f32[1,4,256,256]{3,2,1,0:T(8,128)S(1)} %get-tuple-element.7.raw, f32[32,256]{1,0:T(8,128)S(1)} %get-tuple-element.8.fix), custom_call_target="tpu_custom_call" | custom-call | tf_op jit(solution)/shard_map/add_fix/pallas_call | solution.py:578

commit v10 on v9

--- a/solution.py
+++ b/solution.py
@@ -435,6 +435,9 @@
     inner_rows(16)
     far_planes((0, 3), 0, 32)
     near_planes((0, 3), 0, 32)
+    from_sides(hu, rxu)
+    far_rows(0)
+    far_rows(3)
 
     y_at, y_row = iota((32, 128), 1), iota((32, 128), 0)
     start = jnp.where(y_at < 64, 0, 16 + 8 * ((y_at - 64) // 32))
@@ -447,9 +450,6 @@
     )
     for m, peer in enumerate(x_peers):
         remote(uv_sums, uv_x.at[m], rc, (t, peer))
-    from_sides(hu, rxu)
-    far_rows(0)
-    far_rows(3)
     from_sides(hv, rxv)
     near_rows((0, 3), 0, 32)
     join(0, p, ub_own)

time: 33 us -> 33 us (level)
  no operation moved by 1% of the time
where the time goes in v10:
time: 33 us; the launch traced here: 32.9 us
  Pallas kernels  32.9 us (100%)
    pallas_call x1, Pallas kernels, shards(): pl.pallas_call(kernel, out_shape=(jax.ShapeDtypeStruct(source.shape, F32)...  31.9 us
    pallas_call x1, Pallas kernels, shards(): pl.pallas_call(add_fix, out_shape=jax.ShapeDtypeStruct(source.shape, F32)...  1.03 us

profile of v10, /device:TPU:1, one launch (start us, length us, event | category | flops | bytes accessed | tf_op | source)
XLA Modules:
  0.0 32.9 jit_solution(10444878767604515392)
XLA Ops:
  0.0 31.9 %space_time_apply.1 = (f32[1,4,256,256]{3,2,1,0:T(8,128)S(1)}, f32[32,256]{1,0:T(8,128)S(1)}) custom-call(f32[4]{0:T(128)} %shift_hbm.1, f32[1,4,256,256]{3,2,1,0:T(8,128)} %source.1, f32[4,256,256]{2,1,0:T(8,128)} %potential.1), custom_call_target="tpu_custom_call" | custom-call | tf_op jit(solution)/shard_map/space_time_apply/pallas_call | solution.py:563
  31.9 1.0 %add_fix.1 = f32[1,4,256,256]{3,2,1,0:T(8,128)} custom-call(f32[1,4,256,256]{3,2,1,0:T(8,128)S(1)} %get-tuple-element.7.raw, f32[32,256]{1,0:T(8,128)S(1)} %get-tuple-element.8.fix), custom_call_target="tpu_custom_call" | custom-call | tf_op jit(solution)/shard_map/add_fix/pallas_call | solution.py:578

commit v11 on v10

--- a/solution.py
+++ b/solution.py
@@ -313,13 +313,6 @@
         return 0
 
     lax.fori_loop(0, 4, odd_rows, 0)
-    y_at, y_row = iota((24, 128), 1), iota((24, 128), 0)
-    inner = ones_where(y_at // 8 + 1 == y_row)
-    beside = ones_where((y_at + 7) // 8 == y_row) + ones_where((y_at + 1) // 8 + 1 == y_row)
-    sums = dot(inner, dot(x_d[...], blocks[0]) + dot(t_d[...], blocks[1])) + dot(beside, dot(t_d[...], blocks[0]))
-    d_sums[...] = pltpu.roll(sums, 96, 1)
-    for m, peer in enumerate(x_peers):
-        remote(d_sums, d_x.at[m], rdx, (t, peer))
 
     strip_2.wait_recv()
     here = ustrip[rows(8 * p, 8), :]
@@ -454,6 +447,13 @@
     near_rows((0, 3), 0, 32)
     join(0, p, ub_own)
     join(1, p, ub_own)
+    y_at, y_row = iota((24, 128), 1), iota((24, 128), 0)
+    inner = ones_where(y_at // 8 + 1 == y_row)
+    beside = ones_where((y_at + 7) // 8 == y_row) + ones_where((y_at + 1) // 8 + 1 == y_row)
+    sums = dot(inner, dot(x_d[...], blocks[0]) + dot(t_d[...], blocks[1])) + dot(beside, dot(t_d[...], blocks[0]))
+    d_sums[...] = pltpu.roll(sums, 96, 1)
+    for m, peer in enumerate(x_peers):
+        remote(d_sums, d_x.at[m], rdx, (t, peer))
     rest(2)
     absorb(uv_x, rc)
     uv_total[...] = (uv_sums[...] + uv_x[0]) + (uv_x[1] + uv_x[2])

time: 33 us -> 33.1 us (level)
  no operation moved by 1% of the time
where the time goes in v11:
time: 33.1 us; the launch traced here: 32.9 us
  Pallas kernels  32.9 us (99%)
    pallas_call x1, Pallas kernels, shards(): pl.pallas_call(kernel, out_shape=(jax.ShapeDtypeStruct(source.shape, F32)...  31.9 us
    pallas_call x1, Pallas kernels, shards(): pl.pallas_call(add_fix, out_shape=jax.ShapeDtypeStruct(source.shape, F32)...  1.03 us

profile of v11, /device:TPU:1, one launch (start us, length us, event | category | flops | bytes accessed | tf_op | source)
XLA Modules:
  0.0 32.9 jit_solution(8038850465314001845)
XLA Ops:
  0.0 31.9 %space_time_apply.1 = (f32[1,4,256,256]{3,2,1,0:T(8,128)S(1)}, f32[32,256]{1,0:T(8,128)S(1)}) custom-call(f32[4]{0:T(128)} %shift_hbm.1, f32[1,4,256,256]{3,2,1,0:T(8,128)} %source.1, f32[4,256,256]{2,1,0:T(8,128)} %potential.1), custom_call_target="tpu_custom_call" | custom-call | tf_op jit(solution)/shard_map/space_time_apply/pallas_call | solution.py:563
  31.9 1.0 %add_fix.1 = f32[1,4,256,256]{3,2,1,0:T(8,128)} custom-call(f32[1,4,256,256]{3,2,1,0:T(8,128)S(1)} %get-tuple-element.7.raw, f32[32,256]{1,0:T(8,128)S(1)} %get-tuple-element.8.fix), custom_call_target="tpu_custom_call" | custom-call | tf_op jit(solution)/shard_map/add_fix/pallas_call | solution.py:578
